TPU v7x, 256 devices: a whole 4x4x8 slice. The times are simulated.
256 devices in a mesh: pipe: 16 (over y, x), dp: 16 (over z, core).
Axes of the slice: x: 4, y: 4, z: 8, core: 2. Of those that a mesh axis runs over, the one named last changes fastest.
Arguments:
- embedded: bfloat16 [2048, 1024], P('dp'), may hold values from -6 to 6
- targets: bfloat16 [2048, 1024], P('dp'), may hold values from -6 to 6
- w_up: bfloat16 [16, 1024, 2048], P('pipe'), may hold values from -0.1875 to 0.1875
- w_down: bfloat16 [16, 2048, 1024], P('pipe'), may hold values from -0.125 to 0.125
- probe_up: bfloat16 [16, 1024, 2048], P('pipe', 'dp'), may hold values from -5 to 5
- probe_down: bfloat16 [16, 1024, 2048], P('pipe', 'dp'), may hold values from -5 to 5
Outputs:
- curv_up: float32 [16, 1024, 2048], P('pipe', 'dp')
- curv_down: float32 [16, 1024, 2048], P('pipe', 'dp')
All inputs are finite; a program needn't handle non-finite values.
Results may differ from a plain program's by a relative error of at most 0.022.
Values may be sent and summed in bfloat16 or wider, within the bound.
No kernel may reach another device: no remote copies, remote signals or barrier semaphores. Data moves between devices by JAX's collectives and lax.ppermute only.
A program may use at most 128 MiB of HBM per device.

v0:
```python
import jax
import jax.numpy as jnp
from jax import lax
from jax.sharding import PartitionSpec as P

MICRO = 4


epsilon = 1e-05
half_root = 0.7071067811865476
density_scale = 0.3989422804014327


def from_behind(block, axis, distance):
    devices = range(lax.axis_size(axis))
    route = [(i - distance, i) for i in devices if i - distance in devices]
    return lax.ppermute(block, axis, route)


def gelu_terms(values):
    normal_cdf = 0.5 * (1.0 + jax.scipy.special.erf(values * half_root))
    density = density_scale * jnp.exp(-0.5 * values * values)
    return (values * normal_cdf, normal_cdf + values * density, density * (2.0 - values * values))


def normalize(stream):
    centre = stream - jnp.mean(stream, axis=-1, keepdims=True)
    spread = jnp.mean(centre * centre, axis=-1, keepdims=True)
    return centre * lax.rsqrt(spread + epsilon)


def normalize_back(stream, cotangent):
    unused, pullback = jax.vjp(normalize, stream)
    return pullback(cotangent)[0]


def contract_last(left, right):
    return lax.dot_general(
        left, right, (((1,), (1,)), ((), ())), preferred_element_type=jnp.float32
    )


def contract_first(left, right):
    return lax.dot_general(
        left, right, (((0,), (0,)), ((), ())), preferred_element_type=jnp.float32
    )


def layer_forward(stream, tangent, w_one, w_two, probe_one, probe_two):
    stream_f = stream.astype(jnp.float32)
    tangent_f = tangent.astype(jnp.float32)
    normed, normed_tan = jax.jvp(normalize, (stream_f,), (tangent_f,))
    normed_b = normed.astype(jnp.bfloat16)
    normed_tb = normed_tan.astype(jnp.bfloat16)
    pre_act = jnp.dot(normed_b, w_one, preferred_element_type=jnp.float32)
    pre_tan = jnp.dot(normed_tb, w_one, preferred_element_type=jnp.float32) + jnp.dot(
        normed_b, probe_one, preferred_element_type=jnp.float32
    )
    active, slope, unused = gelu_terms(pre_act)
    active_b = active.astype(jnp.bfloat16)
    active_tb = (slope * pre_tan).astype(jnp.bfloat16)
    branch = jnp.dot(active_b, w_two, preferred_element_type=jnp.float32)
    branch_tan = jnp.dot(active_tb, w_two, preferred_element_type=jnp.float32) + contract_last(
        active_b, probe_two
    )
    next_stream = (stream_f + branch).astype(jnp.bfloat16)
    next_tan = (tangent_f + branch_tan).astype(jnp.bfloat16)
    return (next_stream, next_tan, (normed_b, normed_tb, pre_act, pre_tan, active_b, active_tb))


def layer_backward(
    cotan, cotan_tan, stream, tangent, pre_act, pre_tan, w_one, w_two, probe_one, probe_two
):
    grad_act = contract_last(cotan, w_two)
    grad_act_tan = contract_last(cotan_tan, w_two) + jnp.dot(
        cotan, probe_two, preferred_element_type=jnp.float32
    )
    unused, slope, curve = gelu_terms(pre_act)
    grad_pre = (grad_act * slope).astype(jnp.bfloat16)
    grad_pre_tan = (grad_act_tan * slope + grad_act * curve * pre_tan).astype(jnp.bfloat16)
    grad_norm = contract_last(grad_pre, w_one)
    grad_norm_tan = contract_last(grad_pre_tan, w_one) + contract_last(grad_pre, probe_one)
    stream_f = stream.astype(jnp.float32)
    tangent_f = tangent.astype(jnp.float32)
    back, back_tan = jax.jvp(normalize_back, (stream_f, grad_norm), (tangent_f, grad_norm_tan))
    previous = (cotan.astype(jnp.float32) + back).astype(jnp.bfloat16)
    previous_tan = (cotan_tan.astype(jnp.float32) + back_tan).astype(jnp.bfloat16)
    return (previous, previous_tan, grad_pre, grad_pre_tan)


def on_device(embedded, targets, w_up, w_down, probe_up, probe_down):
    sections = lax.axis_size("pipe")
    my_section = lax.axis_index("pipe")
    groups = lax.axis_size("dp")
    w_one = w_up[0]
    w_two = w_down[0]
    probe_one, probe_two = (
        lax.all_gather(probe_up[0], "dp", axis=0, tiled=True),
        lax.all_gather(probe_down[0], "dp", axis=0, tiled=True),
    )
    tokens_here = embedded.shape[0]
    model_width = embedded.shape[1]
    hidden = w_one.shape[1]
    pieces = MICRO
    piece_rows = tokens_here // pieces
    loss_scale = 1.0 / (tokens_here * groups)
    sources = embedded.reshape(pieces, piece_rows, model_width)
    goal_rows = targets.reshape(pieces, piece_rows, model_width)
    at_first = my_section == 0
    at_last = my_section == sections - 1
    ticks = jnp.arange(pieces + sections - 1, dtype=jnp.int32)
    quiet = jnp.zeros((2, piece_rows, model_width), jnp.bfloat16)

    def blank(columns, kind):
        return jnp.zeros((pieces, piece_rows, columns), kind)

    def forward_tick(carry, tick_now):
        received, stash_bufs = carry
        piece_now = tick_now - my_section
        is_valid = (piece_now >= 0) & (piece_now < pieces)
        slot_index = jnp.clip(piece_now, 0, pieces - 1)
        source_now = lax.dynamic_index_in_dim(sources, slot_index, 0, keepdims=False)
        stream = jnp.where(at_first, source_now, received[0])
        tangent = jnp.where(at_first, jnp.zeros_like(source_now), received[1])

        def forward_compute(bufs):
            next_stream, next_tan, kept = layer_forward(
                stream, tangent, w_one, w_two, probe_one, probe_two
            )
            goal_now = lax.dynamic_index_in_dim(goal_rows, slot_index, 0, keepdims=False)
            cotan_top = (
                (next_stream.astype(jnp.float32) - goal_now.astype(jnp.float32)) * loss_scale
            ).astype(jnp.bfloat16)
            tan_top = (next_tan.astype(jnp.float32) * loss_scale).astype(jnp.bfloat16)
            values = (stream, tangent) + kept + (cotan_top, tan_top)
            updated = tuple(
                (
                    lax.dynamic_update_index_in_dim(buffer, value, slot_index, 0)
                    for buffer, value in zip(bufs, values)
                )
            )
            return (jnp.stack((next_stream, next_tan)), updated)

        def forward_spare_step(bufs):
            return (quiet, bufs)

        outgoing, stash_bufs = lax.cond(is_valid, forward_compute, forward_spare_step, stash_bufs)
        received = from_behind(outgoing, "pipe", 1)
        return ((received, stash_bufs), None)

    forward_init = (
        blank(model_width, jnp.bfloat16),
        blank(model_width, jnp.bfloat16),
        blank(model_width, jnp.bfloat16),
        blank(model_width, jnp.bfloat16),
        blank(hidden, jnp.float32),
        blank(hidden, jnp.float32),
        blank(hidden, jnp.bfloat16),
        blank(hidden, jnp.bfloat16),
        blank(model_width, jnp.bfloat16),
        blank(model_width, jnp.bfloat16),
    )
    (unused_recv, stash_bufs), unused_out = lax.scan(forward_tick, (quiet, forward_init), ticks)
    (
        stream_ins,
        tangent_ins,
        normed_bs,
        normed_tbs,
        pre_acts,
        pre_tans,
        active_bs,
        active_tbs,
        cotan_tops,
        tan_tops,
    ) = stash_bufs

    def backward_tick(carry, tick_now):
        received, grad_bufs = carry
        piece_now = tick_now - (sections - 1 - my_section)
        is_valid = (piece_now >= 0) & (piece_now < pieces)
        slot_index = jnp.clip(piece_now, 0, pieces - 1)

        def select(buffer):
            return lax.dynamic_index_in_dim(buffer, slot_index, 0, keepdims=False)

        cotan = jnp.where(at_last, select(cotan_tops), received[0])
        cotan_tan = jnp.where(at_last, select(tan_tops), received[1])

        def backward_compute(bufs):
            previous, previous_tan, grad_pre, grad_pre_tan = layer_backward(
                cotan,
                cotan_tan,
                select(stream_ins),
                select(tangent_ins),
                select(pre_acts),
                select(pre_tans),
                w_one,
                w_two,
                probe_one,
                probe_two,
            )
            values = (cotan, cotan_tan, grad_pre, grad_pre_tan)
            updated = tuple(
                (
                    lax.dynamic_update_index_in_dim(buffer, value, slot_index, 0)
                    for buffer, value in zip(bufs, values)
                )
            )
            return (jnp.stack((previous, previous_tan)), updated)

        def backward_spare_step(bufs):
            return (quiet, bufs)

        outgoing, grad_bufs = lax.cond(is_valid, backward_compute, backward_spare_step, grad_bufs)
        received = from_behind(outgoing, "pipe", -1)
        return ((received, grad_bufs), None)

    backward_init = (
        blank(model_width, jnp.bfloat16),
        blank(model_width, jnp.bfloat16),
        blank(hidden, jnp.bfloat16),
        blank(hidden, jnp.bfloat16),
    )
    (unused_back, grad_bufs), unused_more = lax.scan(backward_tick, (quiet, backward_init), ticks)
    cotans, cotan_tans, grad_pres, grad_pre_tans = grad_bufs

    def flatten(buffer):
        return buffer.reshape(tokens_here, buffer.shape[2])

    left_one = jnp.concatenate((flatten(normed_bs), flatten(normed_tbs)), axis=0)
    right_one = jnp.concatenate((flatten(grad_pre_tans), flatten(grad_pres)), axis=0)
    left_two = jnp.concatenate((flatten(cotan_tans), flatten(cotans)), axis=0)
    right_two = jnp.concatenate((flatten(active_bs), flatten(active_tbs)), axis=0)
    summed = lax.psum_scatter(
        jnp.concatenate(
            (contract_first(left_one, right_one), contract_first(left_two, right_two)), axis=1
        ).astype(jnp.bfloat16),
        "dp",
        scatter_dimension=0,
        tiled=True,
    ).astype(jnp.float32)
    summed_up = summed[:, :hidden]
    summed_down = summed[:, hidden:]
    curv_up = probe_up[0].astype(jnp.float32) * summed_up
    curv_down = probe_down[0].astype(jnp.float32) * summed_down
    return (curv_up[None], curv_down[None])


def solution(mesh):
    in_specs = (
        P("dp", None),
        P("dp", None),
        P("pipe", None, None),
        P("pipe", None, None),
        P("pipe", "dp", None),
        P("pipe", "dp", None),
    )
    out_specs = (P("pipe", "dp", None), P("pipe", "dp", None))
    return jax.shard_map(
        on_device, mesh=mesh, in_specs=in_specs, out_specs=out_specs, check_vma=False
    )
```

profile of v0, /device:TPU:6, one launch (start us, length us, event | category | flops | bytes accessed | tf_op | source)
XLA Modules:
  0.0 1015.5 jit_solution(12198297871945982760)
XLA Ops:
  8.7 46.2 %all-gather.5.cloned.1.call-done = bf16[1,1024,2048]{2,1,0:T(8,128)(2,1)} async-done(((bf16[1,64,2048]{2,1,0:T(8,128)(2,1)}), bf16[1,1024,2048]{2,1,0:T(8,128)(2,1)}) %all-gather.5.cloned.1.call-update) | async-done | bytes 4194320 | tf_op jit(solution)/shard_map/all_gather | solution.py:98
  54.9 42.5 %all-gather.7.cloned.1.call-done = bf16[1,1024,2048]{2,1,0:T(8,128)(2,1)} async-done(((bf16[1,64,2048]{2,1,0:T(8,128)(2,1)}), bf16[1,1024,2048]{2,1,0:T(8,128)(2,1)}) %all-gather.7.cloned.1.call-update) | async-done | bytes 4194320 | tf_op jit(solution)/shard_map/all_gather | solution.py:99
  101.6 323.7 %while.50 = (s32[]{:T(128)}, bf16[2,32,1024]{2,1,0:T(8,128)(2,1)S(1)}, bf16[4,32,1024]{2,1,0:T(8,128)(2,1)S(1)}, bf16[4,32,1024]{2,1,0:T(8,128)(2,1)S(1)}, bf16[...) while((s32[]{:T(128)}, ...), condition=%wide.region_7.8_spmd, body=%wide.region_0.7_spmd.sunk | while | flops 808845440 | bytes 98051600 | solution.py:163
  120.9 6.5 collective-permute-start
  127.3 35.5 %collective-permute-done = bf16[2,32,1024]{2,1,0:T(8,128)(2,1)S(1)} collective-permute-done((bf16[2,32,1024]{2,1,0:T(8,128)(2,1)S(1)}, bf16[2,32,1024]{2,1,0:T(8,128)(2,1)S(1)}, u32[]{:S(2)}, u32[]{:S(2)}) %collective-permute-start) | collective-permute-done | bytes 131104 | tf_op jit(solution)/shard_map/while/body/eval_jaxpr/ppermute | solution.py:17
  164.0 13.5 %conditional.4 = (bf16[2,32,1024]{2,1,0:T(8,128)(2,1)S(1)}, bf16[4,32,1024]{2,1,0:T(8,128)(2,1)S(1)}, bf16[4,32,1024]{2,1,0:T(8,128)(2,1)S(1)}, bf16[4,32,1024]{...) conditional(s32[]{:T(128)} %convert_element_type.372, ...), branch_computations={%region_1.1_spmd, %region_2.6_spmd} | conditional | flops 808845440 | bytes 97526776 | solution.py:147
  185.5 13.4 %conditional.4 = (bf16[2,32,1024]{2,1,0:T(8,128)(2,1)S(1)}, bf16[4,32,1024]{2,1,0:T(8,128)(2,1)S(1)}, bf16[4,32,1024]{2,1,0:T(8,128)(2,1)S(1)}, bf16[4,32,1024]{...) conditional(s32[]{:T(128)} %convert_element_type.372, ...), branch_computations={%region_1.1_spmd, %region_2.6_spmd} | conditional | flops 808845440 | bytes 97526776 | solution.py:147
  207.0 13.4 %conditional.4 = (bf16[2,32,1024]{2,1,0:T(8,128)(2,1)S(1)}, bf16[4,32,1024]{2,1,0:T(8,128)(2,1)S(1)}, bf16[4,32,1024]{2,1,0:T(8,128)(2,1)S(1)}, bf16[4,32,1024]{...) conditional(s32[]{:T(128)} %convert_element_type.372, ...), branch_computations={%region_1.1_spmd, %region_2.6_spmd} | conditional | flops 808845440 | bytes 97526776 | solution.py:147
  220.4 6.2 collective-permute-start
  230.3 13.5 %conditional.4 = (bf16[2,32,1024]{2,1,0:T(8,128)(2,1)S(1)}, bf16[4,32,1024]{2,1,0:T(8,128)(2,1)S(1)}, bf16[4,32,1024]{2,1,0:T(8,128)(2,1)S(1)}, bf16[4,32,1024]{...) conditional(s32[]{:T(128)} %convert_element_type.372, ...), branch_computations={%region_1.1_spmd, %region_2.6_spmd} | conditional | flops 808845440 | bytes 97526776 | solution.py:147
  243.7 6.4 collective-permute-start
  253.9 19.9 %collective-permute-start = (bf16[2,32,1024]{2,1,0:T(8,128)(2,1)S(1)}, bf16[2,32,1024]{2,1,0:T(8,128)(2,1)S(1)}, u32[]{:S(2)}, u32[]{:S(2)}) collective-permute-start(bf16[2,32,1024]{2,1,0:T(8,128)(2,1)S(1)} %get-tuple-element.1170), channel_id=1, source_target_pairs={{0,16},{16,32},{32,48},{48,64},{64,80},{80,96},{96,112},{112,128},... | collective-permute-start | bytes 393224 | tf_op jit(solution)/shard_map/while/body/eval_jaxpr/ppermute | solution.py:17
  277.5 6.5 collective-permute-start
  287.7 13.7 %collective-permute-start = (bf16[2,32,1024]{2,1,0:T(8,128)(2,1)S(1)}, bf16[2,32,1024]{2,1,0:T(8,128)(2,1)S(1)}, u32[]{:S(2)}, u32[]{:S(2)}) collective-permute-start(bf16[2,32,1024]{2,1,0:T(8,128)(2,1)S(1)} %get-tuple-element.1170), channel_id=1, source_target_pairs={{0,16},{16,32},{32,48},{48,64},{64,80},{80,96},{96,112},{112,128},... | collective-permute-start | bytes 393224 | tf_op jit(solution)/shard_map/while/body/eval_jaxpr/ppermute | solution.py:17
  306.4 6.5 collective-permute-start
  316.6 11.4 %collective-permute-start = (bf16[2,32,1024]{2,1,0:T(8,128)(2,1)S(1)}, bf16[2,32,1024]{2,1,0:T(8,128)(2,1)S(1)}, u32[]{:S(2)}, u32[]{:S(2)}) collective-permute-start(bf16[2,32,1024]{2,1,0:T(8,128)(2,1)S(1)} %get-tuple-element.1170), channel_id=1, source_target_pairs={{0,16},{16,32},{32,48},{48,64},{64,80},{80,96},{96,112},{112,128},... | collective-permute-start | bytes 393224 | tf_op jit(solution)/shard_map/while/body/eval_jaxpr/ppermute | solution.py:17
  331.8 6.5 collective-permute-start
  342.0 13.2 %collective-permute-start = (bf16[2,32,1024]{2,1,0:T(8,128)(2,1)S(1)}, bf16[2,32,1024]{2,1,0:T(8,128)(2,1)S(1)}, u32[]{:S(2)}, u32[]{:S(2)}) collective-permute-start(bf16[2,32,1024]{2,1,0:T(8,128)(2,1)S(1)} %get-tuple-element.1170), channel_id=1, source_target_pairs={{0,16},{16,32},{32,48},{48,64},{64,80},{80,96},{96,112},{112,128},... | collective-permute-start | bytes 393224 | tf_op jit(solution)/shard_map/while/body/eval_jaxpr/ppermute | solution.py:17
  358.9 6.5 collective-permute-start
  369.1 15.3 %collective-permute-start = (bf16[2,32,1024]{2,1,0:T(8,128)(2,1)S(1)}, bf16[2,32,1024]{2,1,0:T(8,128)(2,1)S(1)}, u32[]{:S(2)}, u32[]{:S(2)}) collective-permute-start(bf16[2,32,1024]{2,1,0:T(8,128)(2,1)S(1)} %get-tuple-element.1170), channel_id=1, source_target_pairs={{0,16},{16,32},{32,48},{48,64},{64,80},{80,96},{96,112},{112,128},... | collective-permute-start | bytes 393224 | tf_op jit(solution)/shard_map/while/body/eval_jaxpr/ppermute | solution.py:17
  388.2 6.5 collective-permute-start
  398.4 13.2 %collective-permute-start = (bf16[2,32,1024]{2,1,0:T(8,128)(2,1)S(1)}, bf16[2,32,1024]{2,1,0:T(8,128)(2,1)S(1)}, u32[]{:S(2)}, u32[]{:S(2)}) collective-permute-start(bf16[2,32,1024]{2,1,0:T(8,128)(2,1)S(1)} %get-tuple-element.1170), channel_id=1, source_target_pairs={{0,16},{16,32},{32,48},{48,64},{64,80},{80,96},{96,112},{112,128},... | collective-permute-start | bytes 393224 | tf_op jit(solution)/shard_map/while/body/eval_jaxpr/ppermute | solution.py:17
  415.4 7.4 collective-permute-start
  428.4 481.4 %while.51 = (s32[]{:T(128)}, bf16[2,32,1024]{2,1,0:T(8,128)(2,1)S(1)}, bf16[4,32,1024]{2,1,0:T(8,128)(2,1)}, bf16[4,32,1024]{2,1,0:T(8,128)(2,1)}, bf16[4,32,204...) while((s32[]{:T(128)}, ...), condition=%wide.region_19.20_spmd, body=%wide.region_8.19_spmd.sunk | while | flops 808911424 | bytes 98441488 | solution.py:224
  431.7 13.3 %collective-permute-done.1 = bf16[2,32,1024]{2,1,0:T(8,128)(2,1)S(1)} collective-permute-done((bf16[2,32,1024]{2,1,0:T(8,128)(2,1)S(1)}, bf16[2,32,1024]{2,1,0:T(8,128)(2,1)S(1)}, u32[]{:S(2)}, u32[]{:S(2)}) %collective-permute-start.1) | collective-permute-done | bytes 131104 | tf_op jit(solution)/shard_map/while/body/eval_jaxpr/ppermute | solution.py:17
  448.2 9.7 collective-permute-done.1
  461.1 12.0 %collective-permute-done.1 = bf16[2,32,1024]{2,1,0:T(8,128)(2,1)S(1)} collective-permute-done((bf16[2,32,1024]{2,1,0:T(8,128)(2,1)S(1)}, bf16[2,32,1024]{2,1,0:T(8,128)(2,1)S(1)}, u32[]{:S(2)}, u32[]{:S(2)}) %collective-permute-start.1) | collective-permute-done | bytes 131104 | tf_op jit(solution)/shard_map/while/body/eval_jaxpr/ppermute | solution.py:17
  476.3 10.1 collective-permute-done.1
  489.6 13.7 %collective-permute-done.1 = bf16[2,32,1024]{2,1,0:T(8,128)(2,1)S(1)} collective-permute-done((bf16[2,32,1024]{2,1,0:T(8,128)(2,1)S(1)}, bf16[2,32,1024]{2,1,0:T(8,128)(2,1)S(1)}, u32[]{:S(2)}, u32[]{:S(2)}) %collective-permute-start.1) | collective-permute-done | bytes 131104 | tf_op jit(solution)/shard_map/while/body/eval_jaxpr/ppermute | solution.py:17
  506.5 9.7 collective-permute-done.1
  519.4 12.0 %collective-permute-done.1 = bf16[2,32,1024]{2,1,0:T(8,128)(2,1)S(1)} collective-permute-done((bf16[2,32,1024]{2,1,0:T(8,128)(2,1)S(1)}, bf16[2,32,1024]{2,1,0:T(8,128)(2,1)S(1)}, u32[]{:S(2)}, u32[]{:S(2)}) %collective-permute-start.1) | collective-permute-done | bytes 131104 | tf_op jit(solution)/shard_map/while/body/eval_jaxpr/ppermute | solution.py:17
  534.7 8.7 collective-permute-done.1
  546.6 12.9 %collective-permute-done.1 = bf16[2,32,1024]{2,1,0:T(8,128)(2,1)S(1)} collective-permute-done((bf16[2,32,1024]{2,1,0:T(8,128)(2,1)S(1)}, bf16[2,32,1024]{2,1,0:T(8,128)(2,1)S(1)}, u32[]{:S(2)}, u32[]{:S(2)}) %collective-permute-start.1) | collective-permute-done | bytes 131104 | tf_op jit(solution)/shard_map/while/body/eval_jaxpr/ppermute | solution.py:17
  562.8 7.5 collective-permute-done.1
  573.4 14.2 %collective-permute-done.1 = bf16[2,32,1024]{2,1,0:T(8,128)(2,1)S(1)} collective-permute-done((bf16[2,32,1024]{2,1,0:T(8,128)(2,1)S(1)}, bf16[2,32,1024]{2,1,0:T(8,128)(2,1)S(1)}, u32[]{:S(2)}, u32[]{:S(2)}) %collective-permute-start.1) | collective-permute-done | bytes 131104 | tf_op jit(solution)/shard_map/while/body/eval_jaxpr/ppermute | solution.py:17
  590.9 174.8 %collective-permute-done.1 = bf16[2,32,1024]{2,1,0:T(8,128)(2,1)S(1)} collective-permute-done((bf16[2,32,1024]{2,1,0:T(8,128)(2,1)S(1)}, bf16[2,32,1024]{2,1,0:T(8,128)(2,1)S(1)}, u32[]{:S(2)}, u32[]{:S(2)}) %collective-permute-start.1) | collective-permute-done | bytes 131104 | tf_op jit(solution)/shard_map/while/body/eval_jaxpr/ppermute | solution.py:17
  766.9 14.0 %conditional.5 = (bf16[2,32,1024]{2,1,0:T(8,128)(2,1)S(1)}, bf16[4,32,1024]{2,1,0:T(8,128)(2,1)}, bf16[4,32,1024]{2,1,0:T(8,128)(2,1)}, bf16[4,32,2048]{2,1,0:T(8,128)(2,1)}, bf16[4,32,2048]{2,1,0:T(8,128)(2,1)}) conditional(s32[]{:T(128)} %convert_element_type.373, (bf16[4,32,1024]{2,1,0:T(8,128)(2,1)}, bf16[4,32,1024]{2,1,0:T(8,128)(2,1)}, ...), branch_computations={%region_9.9_spmd, %region_10.18_spmd} | conditional | flops 808911424 | bytes 97916744 | solution.py:214
  782.9 7.3 collective-permute-done.1
  791.4 14.0 %conditional.5 = (bf16[2,32,1024]{2,1,0:T(8,128)(2,1)S(1)}, bf16[4,32,1024]{2,1,0:T(8,128)(2,1)}, bf16[4,32,1024]{2,1,0:T(8,128)(2,1)}, bf16[4,32,2048]{2,1,0:T(8,128)(2,1)}, bf16[4,32,2048]{2,1,0:T(8,128)(2,1)}) conditional(s32[]{:T(128)} %convert_element_type.373, (bf16[4,32,1024]{2,1,0:T(8,128)(2,1)}, bf16[4,32,1024]{2,1,0:T(8,128)(2,1)}, ...), branch_computations={%region_9.9_spmd, %region_10.18_spmd} | conditional | flops 808911424 | bytes 97916744 | solution.py:214
  807.3 7.0 collective-permute-done.1
  815.6 14.0 %conditional.5 = (bf16[2,32,1024]{2,1,0:T(8,128)(2,1)S(1)}, bf16[4,32,1024]{2,1,0:T(8,128)(2,1)}, bf16[4,32,1024]{2,1,0:T(8,128)(2,1)}, bf16[4,32,2048]{2,1,0:T(8,128)(2,1)}, bf16[4,32,2048]{2,1,0:T(8,128)(2,1)}) conditional(s32[]{:T(128)} %convert_element_type.373, (bf16[4,32,1024]{2,1,0:T(8,128)(2,1)}, bf16[4,32,1024]{2,1,0:T(8,128)(2,1)}, ...), branch_computations={%region_9.9_spmd, %region_10.18_spmd} | conditional | flops 808911424 | bytes 97916744 | solution.py:214
  831.5 8.7 collective-permute-done.1
  841.5 14.0 %conditional.5 = (bf16[2,32,1024]{2,1,0:T(8,128)(2,1)S(1)}, bf16[4,32,1024]{2,1,0:T(8,128)(2,1)}, bf16[4,32,1024]{2,1,0:T(8,128)(2,1)}, bf16[4,32,2048]{2,1,0:T(8,128)(2,1)}, bf16[4,32,2048]{2,1,0:T(8,128)(2,1)}) conditional(s32[]{:T(128)} %convert_element_type.373, (bf16[4,32,1024]{2,1,0:T(8,128)(2,1)}, bf16[4,32,1024]{2,1,0:T(8,128)(2,1)}, ...), branch_computations={%region_9.9_spmd, %region_10.18_spmd} | conditional | flops 808911424 | bytes 97916744 | solution.py:214
  857.4 7.0 collective-permute-done.1
  865.7 13.8 %collective-permute-start.1 = (bf16[2,32,1024]{2,1,0:T(8,128)(2,1)S(1)}, bf16[2,32,1024]{2,1,0:T(8,128)(2,1)S(1)}, u32[]{:S(2)}, u32[]{:S(2)}) collective-permute-start(bf16[2,32,1024]{2,1,0:T(8,128)(2,1)S(1)} %get-tuple-element.1200), channel_id=1, source_target_pairs={{16,0},{32,16},{48,32},{64,48},{80,64},{96,80},{112,96},{128,112},... | collective-permute-start | bytes 393224 | tf_op jit(solution)/shard_map/while/body/eval_jaxpr/ppermute | solution.py:17
  893.5 13.8 %collective-permute-start.1 = (bf16[2,32,1024]{2,1,0:T(8,128)(2,1)S(1)}, bf16[2,32,1024]{2,1,0:T(8,128)(2,1)S(1)}, u32[]{:S(2)}, u32[]{:S(2)}) collective-permute-start(bf16[2,32,1024]{2,1,0:T(8,128)(2,1)S(1)} %get-tuple-element.1200), channel_id=1, source_target_pairs={{16,0},{32,16},{48,32},{64,48},{80,64},{96,80},{112,96},{128,112},... | collective-permute-start | bytes 393224 | tf_op jit(solution)/shard_map/while/body/eval_jaxpr/ppermute | solution.py:17
  917.7 7.8 pad_maximum_fusion.2
  925.5 81.2 %reduce-scatter.2.cloned.1.call-done = bf16[64,4096]{1,0:T(8,128)(2,1)} async-done(((bf16[1024,4096]{1,0:T(8,128)(2,1)}), bf16[64,4096]{1,0:T(8,128)(2,1)}) %reduce-scatter.2.cloned.1.call-update) | async-done | bytes 524304 | tf_op jit(solution)/shard_map/reduce_scatter | solution.py:234
  (370 shorter events, 262.4 us)
Async XLA Ops:
  7.2 47.7 %all-gather.5.cloned.1.call-start = ((), (), s32[]{:S(2)}) async-start(), calls=%async_computation.2 | async-start | bytes 4456448 | tf_op jit(solution)/shard_map/all_gather | solution.py:98
  7.9 89.5 %all-gather.7.cloned.1.call-start = ((), (), s32[]{:S(2)}) async-start(), calls=%async_computation.3 | async-start | bytes 4456448 | tf_op jit(solution)/shard_map/all_gather | solution.py:99
  8.6 998.1 %reduce-scatter.2.cloned.1.call-start = ((), (), s32[]{:S(2)}) async-start(), calls=%async_computation.1 | async-start | bytes 8912896 | tf_op jit(solution)/shard_map/reduce_scatter | solution.py:234
  102.8 7.5 collective-permute-start
  111.6 8.0 collective-permute-start
  120.9 42.0 %collective-permute-start = (bf16[2,32,1024]{2,1,0:T(8,128)(2,1)S(1)}, bf16[2,32,1024]{2,1,0:T(8,128)(2,1)S(1)}, u32[]{:S(2)}, u32[]{:S(2)}) collective-permute-start(bf16[2,32,1024]{2,1,0:T(8,128)(2,1)S(1)} %get-tuple-element.1170), channel_id=1, source_target_pairs={{0,16},{16,32},{32,48},{48,64},{64,80},{80,96},{96,112},{112,128},... | collective-permute-start | bytes 393224 | tf_op jit(solution)/shard_map/while/body/eval_jaxpr/ppermute | solution.py:17
  177.5 6.8 collective-permute-start
  199.0 6.8 collective-permute-start
  220.4 8.7 collective-permute-start
  243.7 8.9 collective-permute-start
  253.9 22.4 %collective-permute-start = (bf16[2,32,1024]{2,1,0:T(8,128)(2,1)S(1)}, bf16[2,32,1024]{2,1,0:T(8,128)(2,1)S(1)}, u32[]{:S(2)}, u32[]{:S(2)}) collective-permute-start(bf16[2,32,1024]{2,1,0:T(8,128)(2,1)S(1)} %get-tuple-element.1170), channel_id=1, source_target_pairs={{0,16},{16,32},{32,48},{48,64},{64,80},{80,96},{96,112},{112,128},... | collective-permute-start | bytes 393224 | tf_op jit(solution)/shard_map/while/body/eval_jaxpr/ppermute | solution.py:17
  277.5 9.0 collective-permute-start
  287.7 17.5 %collective-permute-start = (bf16[2,32,1024]{2,1,0:T(8,128)(2,1)S(1)}, bf16[2,32,1024]{2,1,0:T(8,128)(2,1)S(1)}, u32[]{:S(2)}, u32[]{:S(2)}) collective-permute-start(bf16[2,32,1024]{2,1,0:T(8,128)(2,1)S(1)} %get-tuple-element.1170), channel_id=1, source_target_pairs={{0,16},{16,32},{32,48},{48,64},{64,80},{80,96},{96,112},{112,128},... | collective-permute-start | bytes 393224 | tf_op jit(solution)/shard_map/while/body/eval_jaxpr/ppermute | solution.py:17
  306.4 9.0 collective-permute-start
  316.6 14.0 %collective-permute-start = (bf16[2,32,1024]{2,1,0:T(8,128)(2,1)S(1)}, bf16[2,32,1024]{2,1,0:T(8,128)(2,1)S(1)}, u32[]{:S(2)}, u32[]{:S(2)}) collective-permute-start(bf16[2,32,1024]{2,1,0:T(8,128)(2,1)S(1)} %get-tuple-element.1170), channel_id=1, source_target_pairs={{0,16},{16,32},{32,48},{48,64},{64,80},{80,96},{96,112},{112,128},... | collective-permute-start | bytes 393224 | tf_op jit(solution)/shard_map/while/body/eval_jaxpr/ppermute | solution.py:17
  331.8 9.0 collective-permute-start
  342.0 15.7 %collective-permute-start = (bf16[2,32,1024]{2,1,0:T(8,128)(2,1)S(1)}, bf16[2,32,1024]{2,1,0:T(8,128)(2,1)S(1)}, u32[]{:S(2)}, u32[]{:S(2)}) collective-permute-start(bf16[2,32,1024]{2,1,0:T(8,128)(2,1)S(1)} %get-tuple-element.1170), channel_id=1, source_target_pairs={{0,16},{16,32},{32,48},{48,64},{64,80},{80,96},{96,112},{112,128},... | collective-permute-start | bytes 393224 | tf_op jit(solution)/shard_map/while/body/eval_jaxpr/ppermute | solution.py:17
  358.9 9.0 collective-permute-start
  369.1 17.9 %collective-permute-start = (bf16[2,32,1024]{2,1,0:T(8,128)(2,1)S(1)}, bf16[2,32,1024]{2,1,0:T(8,128)(2,1)S(1)}, u32[]{:S(2)}, u32[]{:S(2)}) collective-permute-start(bf16[2,32,1024]{2,1,0:T(8,128)(2,1)S(1)} %get-tuple-element.1170), channel_id=1, source_target_pairs={{0,16},{16,32},{32,48},{48,64},{64,80},{80,96},{96,112},{112,128},... | collective-permute-start | bytes 393224 | tf_op jit(solution)/shard_map/while/body/eval_jaxpr/ppermute | solution.py:17
  388.2 9.0 collective-permute-start
  398.4 15.7 %collective-permute-start = (bf16[2,32,1024]{2,1,0:T(8,128)(2,1)S(1)}, bf16[2,32,1024]{2,1,0:T(8,128)(2,1)S(1)}, u32[]{:S(2)}, u32[]{:S(2)}) collective-permute-start(bf16[2,32,1024]{2,1,0:T(8,128)(2,1)S(1)} %get-tuple-element.1170), channel_id=1, source_target_pairs={{0,16},{16,32},{32,48},{48,64},{64,80},{80,96},{96,112},{112,128},... | collective-permute-start | bytes 393224 | tf_op jit(solution)/shard_map/while/body/eval_jaxpr/ppermute | solution.py:17
  415.4 9.9 collective-permute-start
  429.7 15.2 %collective-permute-start.1 = (bf16[2,32,1024]{2,1,0:T(8,128)(2,1)S(1)}, bf16[2,32,1024]{2,1,0:T(8,128)(2,1)S(1)}, u32[]{:S(2)}, u32[]{:S(2)}) collective-permute-start(bf16[2,32,1024]{2,1,0:T(8,128)(2,1)S(1)} %get-tuple-element.1200), channel_id=1, source_target_pairs={{16,0},{32,16},{48,32},{64,48},{80,64},{96,80},{112,96},{128,112},... | collective-permute-start | bytes 393224 | tf_op jit(solution)/shard_map/while/body/eval_jaxpr/ppermute | solution.py:17
  446.2 11.6 %collective-permute-start.1 = (bf16[2,32,1024]{2,1,0:T(8,128)(2,1)S(1)}, bf16[2,32,1024]{2,1,0:T(8,128)(2,1)S(1)}, u32[]{:S(2)}, u32[]{:S(2)}) collective-permute-start(bf16[2,32,1024]{2,1,0:T(8,128)(2,1)S(1)} %get-tuple-element.1200), channel_id=1, source_target_pairs={{16,0},{32,16},{48,32},{64,48},{80,64},{96,80},{112,96},{128,112},... | collective-permute-start | bytes 393224 | tf_op jit(solution)/shard_map/while/body/eval_jaxpr/ppermute | solution.py:17
  459.1 14.0 %collective-permute-start.1 = (bf16[2,32,1024]{2,1,0:T(8,128)(2,1)S(1)}, bf16[2,32,1024]{2,1,0:T(8,128)(2,1)S(1)}, u32[]{:S(2)}, u32[]{:S(2)}) collective-permute-start(bf16[2,32,1024]{2,1,0:T(8,128)(2,1)S(1)} %get-tuple-element.1200), channel_id=1, source_target_pairs={{16,0},{32,16},{48,32},{64,48},{80,64},{96,80},{112,96},{128,112},... | collective-permute-start | bytes 393224 | tf_op jit(solution)/shard_map/while/body/eval_jaxpr/ppermute | solution.py:17
  474.4 12.1 %collective-permute-start.1 = (bf16[2,32,1024]{2,1,0:T(8,128)(2,1)S(1)}, bf16[2,32,1024]{2,1,0:T(8,128)(2,1)S(1)}, u32[]{:S(2)}, u32[]{:S(2)}) collective-permute-start(bf16[2,32,1024]{2,1,0:T(8,128)(2,1)S(1)} %get-tuple-element.1200), channel_id=1, source_target_pairs={{16,0},{32,16},{48,32},{64,48},{80,64},{96,80},{112,96},{128,112},... | collective-permute-start | bytes 393224 | tf_op jit(solution)/shard_map/while/body/eval_jaxpr/ppermute | solution.py:17
  487.7 15.6 %collective-permute-start.1 = (bf16[2,32,1024]{2,1,0:T(8,128)(2,1)S(1)}, bf16[2,32,1024]{2,1,0:T(8,128)(2,1)S(1)}, u32[]{:S(2)}, u32[]{:S(2)}) collective-permute-start(bf16[2,32,1024]{2,1,0:T(8,128)(2,1)S(1)} %get-tuple-element.1200), channel_id=1, source_target_pairs={{16,0},{32,16},{48,32},{64,48},{80,64},{96,80},{112,96},{128,112},... | collective-permute-start | bytes 393224 | tf_op jit(solution)/shard_map/while/body/eval_jaxpr/ppermute | solution.py:17
  504.6 11.6 %collective-permute-start.1 = (bf16[2,32,1024]{2,1,0:T(8,128)(2,1)S(1)}, bf16[2,32,1024]{2,1,0:T(8,128)(2,1)S(1)}, u32[]{:S(2)}, u32[]{:S(2)}) collective-permute-start(bf16[2,32,1024]{2,1,0:T(8,128)(2,1)S(1)} %get-tuple-element.1200), channel_id=1, source_target_pairs={{16,0},{32,16},{48,32},{64,48},{80,64},{96,80},{112,96},{128,112},... | collective-permute-start | bytes 393224 | tf_op jit(solution)/shard_map/while/body/eval_jaxpr/ppermute | solution.py:17
  517.5 14.0 %collective-permute-start.1 = (bf16[2,32,1024]{2,1,0:T(8,128)(2,1)S(1)}, bf16[2,32,1024]{2,1,0:T(8,128)(2,1)S(1)}, u32[]{:S(2)}, u32[]{:S(2)}) collective-permute-start(bf16[2,32,1024]{2,1,0:T(8,128)(2,1)S(1)} %get-tuple-element.1200), channel_id=1, source_target_pairs={{16,0},{32,16},{48,32},{64,48},{80,64},{96,80},{112,96},{128,112},... | collective-permute-start | bytes 393224 | tf_op jit(solution)/shard_map/while/body/eval_jaxpr/ppermute | solution.py:17
  532.7 10.7 %collective-permute-start.1 = (bf16[2,32,1024]{2,1,0:T(8,128)(2,1)S(1)}, bf16[2,32,1024]{2,1,0:T(8,128)(2,1)S(1)}, u32[]{:S(2)}, u32[]{:S(2)}) collective-permute-start(bf16[2,32,1024]{2,1,0:T(8,128)(2,1)S(1)} %get-tuple-element.1200), channel_id=1, source_target_pairs={{16,0},{32,16},{48,32},{64,48},{80,64},{96,80},{112,96},{128,112},... | collective-permute-start | bytes 393224 | tf_op jit(solution)/shard_map/while/body/eval_jaxpr/ppermute | solution.py:17
  544.7 14.9 %collective-permute-start.1 = (bf16[2,32,1024]{2,1,0:T(8,128)(2,1)S(1)}, bf16[2,32,1024]{2,1,0:T(8,128)(2,1)S(1)}, u32[]{:S(2)}, u32[]{:S(2)}) collective-permute-start(bf16[2,32,1024]{2,1,0:T(8,128)(2,1)S(1)} %get-tuple-element.1200), channel_id=1, source_target_pairs={{16,0},{32,16},{48,32},{64,48},{80,64},{96,80},{112,96},{128,112},... | collective-permute-start | bytes 393224 | tf_op jit(solution)/shard_map/while/body/eval_jaxpr/ppermute | solution.py:17
  560.8 9.4 collective-permute-start.1
  571.5 16.1 %collective-permute-start.1 = (bf16[2,32,1024]{2,1,0:T(8,128)(2,1)S(1)}, bf16[2,32,1024]{2,1,0:T(8,128)(2,1)S(1)}, u32[]{:S(2)}, u32[]{:S(2)}) collective-permute-start(bf16[2,32,1024]{2,1,0:T(8,128)(2,1)S(1)} %get-tuple-element.1200), channel_id=1, source_target_pairs={{16,0},{32,16},{48,32},{64,48},{80,64},{96,80},{112,96},{128,112},... | collective-permute-start | bytes 393224 | tf_op jit(solution)/shard_map/while/body/eval_jaxpr/ppermute | solution.py:17
  588.9 176.7 %collective-permute-start.1 = (bf16[2,32,1024]{2,1,0:T(8,128)(2,1)S(1)}, bf16[2,32,1024]{2,1,0:T(8,128)(2,1)S(1)}, u32[]{:S(2)}, u32[]{:S(2)}) collective-permute-start(bf16[2,32,1024]{2,1,0:T(8,128)(2,1)S(1)} %get-tuple-element.1200), channel_id=1, source_target_pairs={{16,0},{32,16},{48,32},{64,48},{80,64},{96,80},{112,96},{128,112},... | collective-permute-start | bytes 393224 | tf_op jit(solution)/shard_map/while/body/eval_jaxpr/ppermute | solution.py:17
  766.9 6.2 copy-start.1
  768.7 6.0 copy-start.3
  780.9 9.2 collective-permute-start.1
  791.4 6.2 copy-start.1
  805.4 9.0 collective-permute-start.1
  815.6 6.2 copy-start.1
  829.6 10.7 %collective-permute-start.1 = (bf16[2,32,1024]{2,1,0:T(8,128)(2,1)S(1)}, bf16[2,32,1024]{2,1,0:T(8,128)(2,1)S(1)}, u32[]{:S(2)}, u32[]{:S(2)}) collective-permute-start(bf16[2,32,1024]{2,1,0:T(8,128)(2,1)S(1)} %get-tuple-element.1200), channel_id=1, source_target_pairs={{16,0},{32,16},{48,32},{64,48},{80,64},{96,80},{112,96},{128,112},... | collective-permute-start | bytes 393224 | tf_op jit(solution)/shard_map/while/body/eval_jaxpr/ppermute | solution.py:17
  841.5 6.2 copy-start.1
  855.5 9.0 collective-permute-start.1
  865.7 16.3 %collective-permute-start.1 = (bf16[2,32,1024]{2,1,0:T(8,128)(2,1)S(1)}, bf16[2,32,1024]{2,1,0:T(8,128)(2,1)S(1)}, u32[]{:S(2)}, u32[]{:S(2)}) collective-permute-start(bf16[2,32,1024]{2,1,0:T(8,128)(2,1)S(1)} %get-tuple-element.1200), channel_id=1, source_target_pairs={{16,0},{32,16},{48,32},{64,48},{80,64},{96,80},{112,96},{128,112},... | collective-permute-start | bytes 393224 | tf_op jit(solution)/shard_map/while/body/eval_jaxpr/ppermute | solution.py:17
  883.3 9.0 collective-permute-start.1
  893.5 16.3 %collective-permute-start.1 = (bf16[2,32,1024]{2,1,0:T(8,128)(2,1)S(1)}, bf16[2,32,1024]{2,1,0:T(8,128)(2,1)S(1)}, u32[]{:S(2)}, u32[]{:S(2)}) collective-permute-start(bf16[2,32,1024]{2,1,0:T(8,128)(2,1)S(1)} %get-tuple-element.1200), channel_id=1, source_target_pairs={{16,0},{32,16},{48,32},{64,48},{80,64},{96,80},{112,96},{128,112},... | collective-permute-start | bytes 393224 | tf_op jit(solution)/shard_map/while/body/eval_jaxpr/ppermute | solution.py:17
  925.5 82.4 %copy-start.9 = (bf16[1,64,2048]{2,1,0:T(8,128)(2,1)S(1)}, bf16[1,64,2048]{2,1,0:T(8,128)(2,1)}, u32[]{:S(2)}) copy-start(bf16[1,64,2048]{2,1,0:T(8,128)(2,1)} %param.18) | copy-start | bytes 786436
  925.5 82.4 %copy-start.10 = (bf16[1,64,2048]{2,1,0:T(8,128)(2,1)S(1)}, bf16[1,64,2048]{2,1,0:T(8,128)(2,1)}, u32[]{:S(2)}) copy-start(bf16[1,64,2048]{2,1,0:T(8,128)(2,1)} %param.19) | copy-start | bytes 786436
  (30 other events, 111.6 us)
Sparse Core Ops, SparseCore 0:
  9.8 45.0 all-gather.4
  56.7 40.6 all-gather.6
  925.7 81.0 reduce-scatter.1
where the time goes:
time: 1020 us
  waiting for transfers between devices  596 us (58%)
  starting transfers between devices  223 us (22%)
  matrix products  97.1 us (10%)
  local copies, waits for them, and re-layouts  32 us (3%)
  other arithmetic  28.1 us (3%)
  loops' own time  25.7 us (3%)
  between operations  13.8 us (1%)
    ppermute x38, waiting for transfers between devices, from_behind(): return lax.ppermute(block, axis, route)  424 us
    ppermute x38, starting transfers between devices, from_behind(): return lax.ppermute(block, axis, route)  223 us
    reduce_scatter x1, waiting for transfers between devices, on_device(): lax.psum_scatter(jnp.concatenate((contract_first(left_one, right_one), co...  81.2 us
    dot_general x24, matrix products, contract_last(): lax.dot_general(left, right, (((1,), (1,)), ((), ())), preferred_element_...  47.7 us
    all_gather x1, waiting for transfers between devices, on_device(): lax.all_gather(probe_up[0], 'dp', axis=0, tiled=True)  46.2 us
    all_gather x1, waiting for transfers between devices, on_device(): lax.all_gather(probe_down[0], 'dp', axis=0, tiled=True)  42.5 us
    dynamic_slice x38, local copies, waits for them, and re-layouts, on_device(): lax.scan(forward_tick, (quiet, forward_init), ticks)  22.8 us
  transfers between devices with their start and end apart: 41, of which 41 were waited for; matrix products, arithmetic and copies ran while one was open for 0% of the time, Pallas kernels for 0%

commit v1 on v0

v1 whole, which is shorter than its diff:
```python
import functools

import jax
import jax.numpy as jnp
from jax import lax
from jax.experimental import pallas as pl
from jax.experimental.pallas import tpu as pltpu
from jax.sharding import PartitionSpec as P

PIECES = 4
LAG = 12
CHUNK = 512

epsilon = 1e-05
half_root = 0.7071067811865476
density_scale = 0.3989422804014327

f32 = jnp.float32
bf16 = jnp.bfloat16

X, TX, G, TG = range(4)
A, TA, PR, TP = range(4)
XH, TXF, QN, BN, PU, AV = range(6)
SLOPE, CURVE, TY, XU, CC, GV = range(6)
INV, RR, M1 = range(3)

IN_VMEM = pl.BlockSpec(memory_space=pltpu.VMEM)
ANYWHERE = pl.BlockSpec(memory_space=pl.ANY)


def vmem(array):
    return pltpu.with_memory_space_constraint(array, pltpu.VMEM)


def hbm(array):
    return pltpu.with_memory_space_constraint(array, pltpu.HBM)


def dot(left, right):
    return jnp.dot(left, right, preferred_element_type=f32)


def dot_last(left, right):
    return lax.dot_general(left, right, (((1,), (1,)), ((), ())), preferred_element_type=f32)


def dot_first(left, right):
    return lax.dot_general(left, right, (((0,), (0,)), ((), ())), preferred_element_type=f32)


def mean(values):
    return jnp.mean(values, axis=-1, keepdims=True)


def gelu_terms(values):
    normal_cdf = 0.5 * (1.0 + lax.erf(values * half_root))
    density = density_scale * jnp.exp(-0.5 * values * values)
    return (values * normal_cdf, normal_cdf + values * density, density * (2.0 - values * values))


def load(arrays):
    count = len(arrays)

    def kernel(*refs):
        sources, targets, sems = refs[:count], refs[count : 2 * count], refs[2 * count]
        copies = [
            pltpu.make_async_copy(source, target, sems.at[i])
            for i, (source, target) in enumerate(zip(sources, targets))
        ]
        for copy in copies:
            copy.start()
        for copy in copies:
            copy.wait()

    return pl.pallas_call(
        kernel,
        out_shape=tuple(pltpu.VMEM(a.shape, a.dtype) for a in arrays),
        in_specs=[ANYWHERE] * count,
        out_specs=(IN_VMEM,) * count,
        scratch_shapes=[pltpu.SemaphoreType.DMA((count,))],
        compiler_params=pltpu.CompilerParams(vmem_limit_bytes=1 << 20),
        name="load",
    )(*[hbm(a) for a in arrays])


def blank(shapes):
    def kernel(*refs):
        refs[-1][...] = jnp.zeros(refs[-1].shape, refs[-1].dtype)

    return pl.pallas_call(
        kernel,
        out_shape=tuple(pltpu.VMEM(shape, kind) for shape, kind in shapes),
        out_specs=(IN_VMEM,) * len(shapes),
        compiler_params=pltpu.CompilerParams(vmem_limit_bytes=1 << 20),
        name="blank",
    )()


class Plan:
    def __init__(self, layers, pieces, lag):
        self.layers, self.pieces, self.lag = layers, pieces, lag
        self.ticks = 2 * layers + lag + pieces - 1

    def stages(self, first, step):
        found = [first - step * m for m in range(self.pieces)]
        return [s for s in found if 0 <= s < self.layers]

    def forward(self, t):
        return self.stages(t, 1)

    def forward_tan(self, t):
        return self.stages(t - self.lag, 1)

    def backward(self, t):
        return self.stages(2 * self.layers - 1 - t, -1)

    def backward_tan(self, t):
        return self.stages(2 * self.layers - 1 - t + self.lag, -1)

    def ready_forward(self, t):
        return 0 <= t - (self.lag - 1) < self.layers

    def ready_backward(self, t):
        return 0 <= 2 * self.layers - 2 + self.lag - t < self.layers

    def edges(self, t):
        up = [(s, s + 1) for s in self.forward(t) + self.forward_tan(t) if s + 1 < self.layers]
        down = [(s, s - 1) for s in self.backward(t) + self.backward_tan(t) if s > 0]
        return up, down


def disjoint(edges):
    sources, targets = [e[0] for e in edges], [e[1] for e in edges]
    return len(set(sources)) == len(sources) and len(set(targets)) == len(targets)


def tick_kernel(plan, t, split_in, split_out, with_probes, loss_scale, rows, width, hidden, *refs):
    refs = list(refs)
    state_in = refs[:5]
    del state_in
    refs = refs[5:]
    w_up, w_down, source, goal = refs[:4]
    refs = refs[4:]
    if with_probes:
        u_up, u_down = refs[:2]
        refs = refs[2:]
    got_up = refs.pop(0)
    got_down = refs.pop(0) if split_in else got_up
    sb_d, sb_f, sf_d, sf_f, sf_n = refs[:5]
    refs = refs[5:]
    put_up = refs.pop(0)
    put_down = refs.pop(0) if split_out else put_up

    layers, pieces, lag = plan.layers, plan.pieces, plan.lag
    stage = lax.axis_index("pipe")
    at_first, at_last = stage == 0, stage == layers - 1
    chunks = [slice(c, c + CHUNK) for c in range(0, hidden, CHUNK)]
    lanes = (rows, 128)

    def when_due(piece, work):
        @pl.when((piece >= 0) & (piece < pieces))
        def _():
            work(pl.ds(pl.multiple_of(jnp.clip(piece, 0, pieces - 1) * rows, rows), rows))

    def spread(value):
        return jnp.broadcast_to(value, lanes)

    def narrow(slot, at):
        return sf_n[slot, at, :][:, :1]

    def forward(at):
        stream = jnp.where(at_first, source[at, :], got_up[...]).astype(f32)
        centre = stream - mean(stream)
        inverse = lax.rsqrt(mean(centre * centre) + epsilon)
        normed = centre * inverse
        sf_d[XH, at, :] = normed
        sf_n[INV, at, :] = spread(inverse)
        normed_b = normed.astype(bf16)
        sb_d[X, at, :] = normed_b
        total = stream
        for c in chunks:
            active, slope, curve = gelu_terms(dot(normed_b, w_up[:, c]))
            active_b = active.astype(bf16)
            sb_f[A, at, c] = active_b
            sf_f[SLOPE, at, c] = slope
            sf_f[CURVE, at, c] = curve
            total = total + dot(active_b, w_down[c, :])
        result = total.astype(bf16)

        @pl.when(jnp.logical_not(at_last))
        def _():
            put_up[...] = result

        @pl.when(at_last)
        def _():
            gap = result.astype(f32) - goal[at, :].astype(f32)
            sb_d[G, at, :] = (gap * loss_scale).astype(bf16)

    def ready_forward():
        for c in chunks:
            sf_f[XU, :, c] = dot(sb_d[X], u_up[:, c])
        for c in [slice(c, c + CHUNK) for c in range(0, width, CHUNK)]:
            sf_d[AV, :, c] = dot_last(sb_f[A], u_down[c, :])

    def forward_tan(at):
        tangent = got_up[...].astype(f32)
        tangent = jnp.where(at_first, jnp.zeros_like(tangent), tangent)
        normed = sf_d[XH, at, :]
        inverse = narrow(INV, at)
        centre = tangent - mean(tangent)
        ratio = mean(normed * centre)
        normed_t = inverse * (centre - normed * ratio)
        sf_d[TXF, at, :] = normed_t
        sf_n[RR, at, :] = spread(-inverse * ratio)
        normed_tb = normed_t.astype(bf16)
        sb_d[TX, at, :] = normed_tb
        total = tangent + sf_d[AV, at, :]
        for c in chunks:
            pre_tan = dot(normed_tb, w_up[:, c]) + sf_f[XU, at, c]
            sf_f[TY, at, c] = pre_tan
            active_tb = (sf_f[SLOPE, at, c] * pre_tan).astype(bf16)
            sb_f[TA, at, c] = active_tb
            total = total + dot(active_tb, w_down[c, :])
        result = total.astype(bf16)

        @pl.when(jnp.logical_not(at_last))
        def _():
            put_up[...] = result

        @pl.when(at_last)
        def _():
            sb_d[TG, at, :] = (result.astype(f32) * loss_scale).astype(bf16)

    def backward(at):
        cotan = jnp.where(at_last, sb_d[G, at, :], got_down[...])
        sb_d[G, at, :] = cotan
        grad = jnp.zeros((rows, width), f32)
        for c in chunks:
            grad_act = dot_last(cotan, w_down[c, :])
            sf_f[CC, at, c] = grad_act * sf_f[CURVE, at, c]
            grad_pre = (grad_act * sf_f[SLOPE, at, c]).astype(bf16)
            sb_f[PR, at, c] = grad_pre
            grad = grad + dot_last(grad_pre, w_up[:, c])
        sf_d[QN, at, :] = grad
        normed = sf_d[XH, at, :]
        along = mean(grad * normed)
        sf_n[M1, at, :] = spread(along)
        back = narrow(INV, at) * (grad - mean(grad) - normed * along)
        sf_d[BN, at, :] = back
        result = (cotan.astype(f32) + back).astype(bf16)

        @pl.when(jnp.logical_not(at_first))
        def _():
            put_down[...] = result

    def ready_backward():
        for c in chunks:
            sf_f[GV, :, c] = dot(sb_d[G], u_down[:, c])
        for c in [slice(c, c + CHUNK) for c in range(0, width, CHUNK)]:
            sf_d[PU, :, c] = dot_last(sb_f[PR], u_up[c, :])

    def backward_tan(at):
        cotan_t = jnp.where(at_last, sb_d[TG, at, :], got_down[...])
        sb_d[TG, at, :] = cotan_t
        grad_t = sf_d[PU, at, :]
        for c in chunks:
            grad_act_t = dot_last(cotan_t, w_down[c, :]) + sf_f[GV, at, c]
            grad_pre_t = grad_act_t * sf_f[SLOPE, at, c] + sf_f[CC, at, c] * sf_f[TY, at, c]
            grad_pre_tb = grad_pre_t.astype(bf16)
            sb_f[TP, at, c] = grad_pre_tb
            grad_t = grad_t + dot_last(grad_pre_tb, w_up[:, c])
        normed, normed_t, inverse = sf_d[XH, at, :], sf_d[TXF, at, :], narrow(INV, at)
        along_t = mean(grad_t * normed + sf_d[QN, at, :] * normed_t)
        inner = grad_t - mean(grad_t) - normed_t * narrow(M1, at) - normed * along_t
        back_t = narrow(RR, at) * sf_d[BN, at, :] + inverse * inner
        result = (cotan_t.astype(f32) + back_t).astype(bf16)

        @pl.when(jnp.logical_not(at_first))
        def _():
            put_down[...] = result

    if plan.backward_tan(t):
        when_due(t - lag - (2 * layers - 1 - stage), backward_tan)
    if plan.forward_tan(t):
        when_due(t - lag - stage, forward_tan)
    if plan.backward(t):
        when_due(t - (2 * layers - 1 - stage), backward)
    if plan.forward(t):
        when_due(t - stage, forward)
    if plan.ready_forward(t):
        pl.when(stage == t - (lag - 1))(ready_forward)
    if plan.ready_backward(t):
        pl.when(stage == 2 * layers - 2 + lag - t)(ready_backward)


def curvature_kernel(sb_d, sb_f, out, hold, sems):
    width, hidden = sb_d.shape[2], sb_f.shape[2]
    step = hold.shape[1]
    copies = []
    for i in range(width // step):
        at = slice(i * step, (i + 1) * step)
        if i >= 2:
            copies[i - 2].wait()
        left = jnp.concatenate((sb_d[X, :, at], sb_d[TX, :, at]), axis=0)
        right = jnp.concatenate((sb_f[TP], sb_f[PR]), axis=0)
        hold[i % 2, :, :hidden] = dot_first(left, right).astype(bf16)
        left = jnp.concatenate((sb_d[TG, :, at], sb_d[G, :, at]), axis=0)
        right = jnp.concatenate((sb_f[A], sb_f[TA]), axis=0)
        hold[i % 2, :, hidden:] = dot_first(left, right).astype(bf16)
        copy = pltpu.make_async_copy(hold.at[i % 2], out.at[at, :], sems.at[i % 2])
        copy.start()
        copies.append(copy)
    for copy in copies[-2:]:
        copy.wait()


def curvature(sb_d, sb_f):
    width, hidden = sb_d.shape[2], sb_f.shape[2]
    step = 128
    return pl.pallas_call(
        curvature_kernel,
        out_shape=jax.ShapeDtypeStruct((width, 2 * hidden), bf16),
        in_specs=[IN_VMEM, IN_VMEM],
        out_specs=ANYWHERE,
        scratch_shapes=[
            pltpu.VMEM((2, step, 2 * hidden), bf16),
            pltpu.SemaphoreType.DMA((2,)),
        ],
        compiler_params=pltpu.CompilerParams(vmem_limit_bytes=16 << 20),
        name="curvature",
    )(vmem(sb_d), vmem(sb_f))


def on_device(embedded, targets, w_up, w_down, probe_up, probe_down):
    layers = lax.axis_size("pipe")
    groups = lax.axis_size("dp")
    tokens, width = embedded.shape
    hidden = w_up.shape[2]
    rows = tokens // PIECES
    loss_scale = 1.0 / (tokens * groups)
    plan = Plan(layers, PIECES, LAG)

    gathered = [
        lax.all_gather(probe[0], "dp", axis=0, tiled=True) for probe in (probe_up, probe_down)
    ]
    held = load((w_up[0], w_down[0], embedded, targets))
    *state, nothing = blank(
        (
            ((4, tokens, width), bf16),
            ((4, tokens, hidden), bf16),
            ((6, tokens, width), f32),
            ((6, tokens, hidden), f32),
            ((3, tokens, 128), f32),
            ((rows, width), bf16),
        )
    )
    probes = None
    got = (nothing,)
    packet = pltpu.VMEM((rows, width), bf16)
    for t in range(plan.ticks):
        if t == LAG - 1:
            probes = load(gathered)
        up, down = plan.edges(t)
        split_out = not disjoint(up + down)
        with_probes = plan.ready_forward(t) or plan.ready_backward(t)
        operands = list(state) + list(held) + (list(probes) if with_probes else []) + list(got)
        results = 2 if split_out else 1
        outs = pl.pallas_call(
            functools.partial(
                tick_kernel, plan, t, len(got) == 2, split_out, with_probes, loss_scale, rows, width, hidden
            ),
            out_shape=tuple(pltpu.VMEM(s.shape, s.dtype) for s in state) + (packet,) * results,
            in_specs=[IN_VMEM] * len(operands),
            out_specs=(IN_VMEM,) * (5 + results),
            input_output_aliases={i: i for i in range(5)},
            compiler_params=pltpu.CompilerParams(vmem_limit_bytes=8 << 20),
            cost_estimate=pl.CostEstimate(flops=1 << 28, bytes_accessed=1 << 23, transcendentals=0),
            name="tick",
        )(*[vmem(o) for o in operands])
        state, sent = outs[:5], outs[5:]
        if split_out:
            got = (lax.ppermute(sent[0], "pipe", up), lax.ppermute(sent[1], "pipe", down))
        elif up + down:
            got = (lax.ppermute(sent[0], "pipe", up + down),)

    sums = curvature(state[0], state[1])
    summed = lax.psum_scatter(sums, "dp", scatter_dimension=0, tiled=True).astype(f32)
    curv_up = probe_up[0].astype(f32) * summed[:, :hidden]
    curv_down = probe_down[0].astype(f32) * summed[:, hidden:]
    return (curv_up[None], curv_down[None])


def solution(mesh):
    in_specs = (
        P("dp", None),
        P("dp", None),
        P("pipe", None, None),
        P("pipe", None, None),
        P("pipe", "dp", None),
        P("pipe", "dp", None),
    )
    out_specs = (P("pipe", "dp", None), P("pipe", "dp", None))
    return jax.shard_map(
        on_device, mesh=mesh, in_specs=in_specs, out_specs=out_specs, check_vma=False
    )
```

time: 1020 us -> 690 us (0.68)
  waiting for transfers between devices: 596 us -> 245 us
  matrix products: 97.1 us -> 0 us
  starting transfers between devices: 223 us -> 318 us
  Pallas kernels: 0 us -> 78.7 us
  other arithmetic: 28.1 us -> 2.19 us
  loops' own time: 25.7 us -> 0 us
  local copies, waits for them, and re-layouts: 32 us -> 20.9 us
    ppermute x38 -> x54, waiting for transfers between devices: 424 us -> 140 us  [the longest x38 126 us: on_device(): got = (lax.ppermute(sent[0], 'pipe', up + down),)]
    dot_general x50 -> x0, matrix products: 97.1 us -> none  [the longest x24 47.7 us: contract_last(): lax.dot_general(left, right, (((1,), (1,)), ((), ())), preferred_element_...]
    ppermute x38 -> x54, starting transfers between devices: 223 us -> 318 us  [the longest x38 269 us: on_device(): got = (lax.ppermute(sent[0], 'pipe', up + down),)]
    pallas_call x0 -> x51, Pallas kernels: none -> 78.7 us  [the longest x47 67.2 us: on_device(): pl.pallas_call(functools.partial(tick_kernel, plan, t, len(got) == 2, spl...]
    all_gather x2, waiting for transfers between devices: 88.7 us -> 17.7 us  [on_device(): lax.all_gather(probe[0], 'dp', axis=0, tiled=True)]
    another operation x40 -> x0, loops' own time: 25.7 us -> none  [the longest x1 12.2 us: on_device(): lax.scan(backward_tick, (quiet, backward_init), ticks)]
    dynamic_slice x38 -> x0, local copies, waits for them, and re-layouts: 22.8 us -> none  [on_device(): lax.scan(forward_tick, (quiet, forward_init), ticks)]
    unnamed x10 -> x38, local copies, waits for them, and re-layouts: 0.02 us -> 20.9 us
  transfers between devices with their start and end apart: 41 -> 57, of which waited for: 41 -> 22; matrix products, arithmetic and copies ran while one was open for 0% -> 0% of each run, Pallas kernels for 0% -> 2%
where the time goes in v1:
time: 690 us; the launch traced here: 680 us
  starting transfers between devices  318 us (46%)
  waiting for transfers between devices  245 us (36%)
  Pallas kernels  78.7 us (11%)
  local copies, waits for them, and re-layouts  20.9 us (3%)
  between operations  15.3 us (2%)
    ppermute x38, starting transfers between devices, on_device(): got = (lax.ppermute(sent[0], 'pipe', up + down),)  269 us
    ppermute x38, waiting for transfers between devices, on_device(): got = (lax.ppermute(sent[0], 'pipe', up + down),)  126 us
    reduce_scatter x1, waiting for transfers between devices, on_device(): lax.psum_scatter(sums, 'dp', scatter_dimension=0, tiled=True).astype(f32)  86.6 us
    pallas_call x47, Pallas kernels, on_device(): pl.pallas_call(functools.partial(tick_kernel, plan, t, len(got) == 2, spl...  67.2 us
    ppermute x8, starting transfers between devices, on_device(): lax.ppermute(sent[0], 'pipe', up)  24.7 us
    ppermute x8, starting transfers between devices, on_device(): lax.ppermute(sent[1], 'pipe', down)  23.6 us
    unnamed x38, local copies, waits for them, and re-layouts  20.9 us
    all_gather x2, waiting for transfers between devices, on_device(): lax.all_gather(probe[0], 'dp', axis=0, tiled=True)  17.7 us
  transfers between devices with their start and end apart: 57, of which 22 were waited for; matrix products, arithmetic and copies ran while one was open for 0% of the time, Pallas kernels for 2%

profile of v1, /device:TPU:6, one launch (start us, length us, event | category | flops | bytes accessed | tf_op | source)
XLA Modules:
  0.0 680.2 jit_solution(1226170463160972959)
XLA Ops:
  8.7 3.5 load.2
  15.0 19.0 %collective-permute-done.2.refs_9_ = bf16[32,1024]{1,0:T(8,128)(2,1)S(1)} collective-permute-done((bf16[32,1024]{1,0:T(8,128)(2,1)S(1)}, bf16[32,1024]{1,0:T(8,128)(2,1)S(1)}, u32[]{:S(2)}, u32[]{:S(2)}) %collective-permute-start.2) | collective-permute-done | bytes 65568 | tf_op jit(solution)/shard_map/ppermute | solution.py:384
  38.1 4.2 collective-permute-done.3.refs_9_
  44.4 4.0 collective-permute-start.4
  52.7 6.1 collective-permute-start.5
  62.8 6.4 collective-permute-start.6
  73.5 2.6 copy-done
  79.8 17.6 %all-gather.7.cloned.1.call-done = bf16[1,1024,2048]{2,1,0:T(8,128)(2,1)} async-done(((bf16[1,64,2048]{2,1,0:T(8,128)(2,1)}), bf16[1,1024,2048]{2,1,0:T(8,128)(2,1)}) %all-gather.7.cloned.1.call-update) | async-done | bytes 4194320 | tf_op jit(solution)/shard_map/all_gather | solution.py:344
  97.5 3.6 load.3
  112.2 9.2 %tick.60 = (bf16[4,128,1024]{2,1,0:T(8,128)(2,1)S(1)}, bf16[4,128,2048]{2,1,0:T(8,128)(2,1)S(1)}, f32[6,128,1024]{2,1,0:T(8,128)S(1)}, f32[6,128,2048]{2,1,0:T(8...) custom-call(bf16[4,128,1024]{2,1,0:T(8,128)(2,1)S(1)} %get-tuple-ele, ...), custom_call_target="tpu_custom_call", output_to_operand_aliasing={{0}: (0, {}), {1}: (1, {}), {2}: (2, {}), {3}: (3, {}), {4}... | custom-call | flops 268435456 | bytes 8388608 | tf_op jit(solution)/shard_map/tick/pallas_call | solution.py:368
  124.2 34.8 %collective-permute-start.14 = (bf16[32,1024]{1,0:T(8,128)(2,1)S(1)}, bf16[32,1024]{1,0:T(8,128)(2,1)S(1)}, u32[]{:S(2)}, u32[]{:S(2)}) collective-permute-start(bf16[32,1024]{1,0:T(8,128)(2,1)S(1)} %get-tuple-element.401), channel_id=1, source_target_pairs={{224,240},{208,224},{192,208},{176,192},{32,48},{16,32},{0,16},{22... | collective-permute-start | bytes 196616 | tf_op jit(solution)/shard_map/ppermute | solution.py:384
  159.0 3.9 collective-permute-done.14.refs_11_
  165.0 12.7 %collective-permute-start.15 = (bf16[32,1024]{1,0:T(8,128)(2,1)S(1)}, bf16[32,1024]{1,0:T(8,128)(2,1)S(1)}, u32[]{:S(2)}, u32[]{:S(2)}) collective-permute-start(bf16[32,1024]{1,0:T(8,128)(2,1)S(1)} %get-tuple-element.407), channel_id=1, source_target_pairs={{224,240},{208,224},{192,208},{48,64},{32,48},{16,32},{0,16},{225,... | collective-permute-start | bytes 196616 | tf_op jit(solution)/shard_map/ppermute | solution.py:384
  177.7 3.2 collective-permute-done.15.refs_11_
  180.9 2.4 tick.63
  183.3 15.5 %collective-permute-start.16 = (bf16[32,1024]{1,0:T(8,128)(2,1)S(1)}, bf16[32,1024]{1,0:T(8,128)(2,1)S(1)}, u32[]{:S(2)}, u32[]{:S(2)}) collective-permute-start(bf16[32,1024]{1,0:T(8,128)(2,1)S(1)} %get-tuple-element.413), channel_id=1, source_target_pairs={{224,240},{208,224},{64,80},{48,64},{32,48},{16,32},{225,241},{209... | collective-permute-start | bytes 196616 | tf_op jit(solution)/shard_map/ppermute | solution.py:382
  199.5 2.6 collective-permute-done.16.refs_11_
  204.1 5.2 collective-permute-start.18
  213.2 20.5 %collective-permute-start.20 = (bf16[32,1024]{1,0:T(8,128)(2,1)S(1)}, bf16[32,1024]{1,0:T(8,128)(2,1)S(1)}, u32[]{:S(2)}, u32[]{:S(2)}) collective-permute-start(bf16[32,1024]{1,0:T(8,128)(2,1)S(1)} %get-tuple-element.427), channel_id=1, source_target_pairs={{96,112},{80,96},{64,80},{48,64},{208,192},{224,208},{240,224},{97... | collective-permute-start | bytes 196616 | tf_op jit(solution)/shard_map/ppermute | solution.py:384
  235.8 16.7 %collective-permute-start.21 = (bf16[32,1024]{1,0:T(8,128)(2,1)S(1)}, bf16[32,1024]{1,0:T(8,128)(2,1)S(1)}, u32[]{:S(2)}, u32[]{:S(2)}) collective-permute-start(bf16[32,1024]{1,0:T(8,128)(2,1)S(1)} %get-tuple-element.433), channel_id=1, source_target_pairs={{112,128},{96,112},{80,96},{64,80},{192,176},{208,192},{224,208},{... | collective-permute-start | bytes 196616 | tf_op jit(solution)/shard_map/ppermute | solution.py:384
  252.6 19.2 %collective-permute-start.22 = (bf16[32,1024]{1,0:T(8,128)(2,1)S(1)}, bf16[32,1024]{1,0:T(8,128)(2,1)S(1)}, u32[]{:S(2)}, u32[]{:S(2)}) collective-permute-start(bf16[32,1024]{1,0:T(8,128)(2,1)S(1)} %get-tuple-element.439), channel_id=1, source_target_pairs={{128,144},{112,128},{96,112},{80,96},{176,160},{192,176},{208,192}... | collective-permute-start | bytes 196616 | tf_op jit(solution)/shard_map/ppermute | solution.py:384
  277.8 5.2 tick.72
  283.0 62.1 %collective-permute-start.31 = (bf16[32,1024]{1,0:T(8,128)(2,1)S(1)}, bf16[32,1024]{1,0:T(8,128)(2,1)S(1)}, u32[]{:S(2)}, u32[]{:S(2)}) collective-permute-start(bf16[32,1024]{1,0:T(8,128)(2,1)S(1)} %get-tuple-element.473), channel_id=1, source_target_pairs={{208,224},{192,208},{176,192},{160,176},{96,80},{112,96},{128,112}... | collective-permute-start | bytes 196616 | tf_op jit(solution)/shard_map/ppermute | solution.py:384
  345.1 18.1 %collective-permute-start.32 = (bf16[32,1024]{1,0:T(8,128)(2,1)S(1)}, bf16[32,1024]{1,0:T(8,128)(2,1)S(1)}, u32[]{:S(2)}, u32[]{:S(2)}) collective-permute-start(bf16[32,1024]{1,0:T(8,128)(2,1)S(1)} %get-tuple-element.479), channel_id=1, source_target_pairs={{224,240},{208,224},{192,208},{176,192},{80,64},{96,80},{112,96},{... | collective-permute-start | bytes 196616 | tf_op jit(solution)/shard_map/ppermute | solution.py:384
  363.2 19.9 %collective-permute-start.33 = (bf16[32,1024]{1,0:T(8,128)(2,1)S(1)}, bf16[32,1024]{1,0:T(8,128)(2,1)S(1)}, u32[]{:S(2)}, u32[]{:S(2)}) collective-permute-start(bf16[32,1024]{1,0:T(8,128)(2,1)S(1)} %get-tuple-element.485), channel_id=1, source_target_pairs={{224,240},{208,224},{192,208},{64,48},{80,64},{96,80},{112,96},{22... | collective-permute-start | bytes 196616 | tf_op jit(solution)/shard_map/ppermute | solution.py:384
  383.1 4.5 collective-permute-done.33.refs_11_
  387.6 3.2 tick.75
  393.4 6.3 collective-permute-done.35.refs_12_
  399.8 2.8 tick.76
  403.3 17.7 %collective-permute-start.37 = (bf16[32,1024]{1,0:T(8,128)(2,1)S(1)}, bf16[32,1024]{1,0:T(8,128)(2,1)S(1)}, u32[]{:S(2)}, u32[]{:S(2)}) collective-permute-start(bf16[32,1024]{1,0:T(8,128)(2,1)S(1)} %get-tuple-element.499), channel_id=1, source_target_pairs={{32,16},{48,32},{64,48},{80,64},{224,208},{240,224},{33,17},{49,33... | collective-permute-start | bytes 196616 | tf_op jit(solution)/shard_map/ppermute | solution.py:382
  420.9 3.8 collective-permute-done.37.refs_12_
  424.8 3.0 tick.77
  427.8 12.8 %collective-permute-start.38 = (bf16[32,1024]{1,0:T(8,128)(2,1)S(1)}, bf16[32,1024]{1,0:T(8,128)(2,1)S(1)}, u32[]{:S(2)}, u32[]{:S(2)}) collective-permute-start(bf16[32,1024]{1,0:T(8,128)(2,1)S(1)} %get-tuple-element.505), channel_id=1, source_target_pairs={{16,0},{32,16},{48,32},{64,48},{208,192},{224,208},{240,224},{17,1... | collective-permute-start | bytes 196616 | tf_op jit(solution)/shard_map/ppermute | solution.py:384
  440.6 3.8 collective-permute-done.38.refs_11_
  444.4 2.8 tick.78
  447.2 12.7 %collective-permute-start.39 = (bf16[32,1024]{1,0:T(8,128)(2,1)S(1)}, bf16[32,1024]{1,0:T(8,128)(2,1)S(1)}, u32[]{:S(2)}, u32[]{:S(2)}) collective-permute-start(bf16[32,1024]{1,0:T(8,128)(2,1)S(1)} %get-tuple-element.511), channel_id=1, source_target_pairs={{16,0},{32,16},{48,32},{192,176},{208,192},{224,208},{240,224},{17... | collective-permute-start | bytes 196616 | tf_op jit(solution)/shard_map/ppermute | solution.py:384
  465.8 5.5 tick.84
  476.1 55.3 %collective-permute-done.47.refs_11_ = bf16[32,1024]{1,0:T(8,128)(2,1)S(1)} collective-permute-done((bf16[32,1024]{1,0:T(8,128)(2,1)S(1)}, bf16[32,1024]{1,0:T(8,128)(2,1)S(1)}, u32[]{:S(2)}, u32[]{:S(2)}) %collective-permute-start.47) | collective-permute-done | bytes 65568 | tf_op jit(solution)/shard_map/ppermute | solution.py:384
  531.4 2.9 tick.87
  536.2 6.3 collective-permute-done.48.refs_11_
  542.5 3.1 tick.88
  547.5 7.4 %collective-permute-done.49.refs_11_ = bf16[32,1024]{1,0:T(8,128)(2,1)S(1)} collective-permute-done((bf16[32,1024]{1,0:T(8,128)(2,1)S(1)}, bf16[32,1024]{1,0:T(8,128)(2,1)S(1)}, u32[]{:S(2)}, u32[]{:S(2)}) %collective-permute-start.49) | collective-permute-done | bytes 65568 | tf_op jit(solution)/shard_map/ppermute | solution.py:384
  554.9 2.9 tick.89
  559.7 6.3 collective-permute-done.50.refs_9_
  566.1 2.9 tick.90
  576.6 4.4 curvature.1
  581.1 3.3 copy-done.16
  584.5 86.6 %reduce-scatter.2.cloned.1.call-done = bf16[64,4096]{1,0:T(8,128)(2,1)} async-done(((bf16[1024,4096]{1,0:T(8,128)(2,1)}), bf16[64,4096]{1,0:T(8,128)(2,1)}) %reduce-scatter.2.cloned.1.call-update) | async-done | bytes 524304 | tf_op jit(solution)/shard_map/reduce_scatter | solution.py:387
  (160 shorter events, 86.3 us)
Async XLA Ops:
  7.2 72.7 %all-gather.5.cloned.1.call-start = ((), (), s32[]{:S(2)}) async-start(), calls=%async_computation.2 | async-start | bytes 4456448 | tf_op jit(solution)/shard_map/all_gather | solution.py:344
  7.9 89.6 %all-gather.7.cloned.1.call-start = ((), (), s32[]{:S(2)}) async-start(), calls=%async_computation.3 | async-start | bytes 4456448 | tf_op jit(solution)/shard_map/all_gather | solution.py:344
  8.6 662.4 %reduce-scatter.2.cloned.1.call-start = ((), (), s32[]{:S(2)}) async-start(), calls=%async_computation.1 | async-start | bytes 8912896 | tf_op jit(solution)/shard_map/reduce_scatter | solution.py:387
  12.3 0.7 collective-permute-start
  13.0 0.7 collective-permute-start.1
  13.7 20.3 %collective-permute-start.2 = (bf16[32,1024]{1,0:T(8,128)(2,1)S(1)}, bf16[32,1024]{1,0:T(8,128)(2,1)S(1)}, u32[]{:S(2)}, u32[]{:S(2)}) collective-permute-start(bf16[32,1024]{1,0:T(8,128)(2,1)S(1)} %get-tuple-element.327), channel_id=1, source_target_pairs={{32,48},{16,32},{0,16},{33,49},{17,33},{1,17},{34,50},{18,34},{2,1... | collective-permute-start | bytes 196616 | tf_op jit(solution)/shard_map/ppermute | solution.py:384
  36.2 6.2 collective-permute-start.3
  44.4 6.2 collective-permute-start.4
  52.7 8.0 %collective-permute-start.5 = (bf16[32,1024]{1,0:T(8,128)(2,1)S(1)}, bf16[32,1024]{1,0:T(8,128)(2,1)S(1)}, u32[]{:S(2)}, u32[]{:S(2)}) collective-permute-start(bf16[32,1024]{1,0:T(8,128)(2,1)S(1)} %get-tuple-element.345), channel_id=1, source_target_pairs={{80,96},{64,80},{48,64},{32,48},{81,97},{65,81},{49,65},{33,49},{8... | collective-permute-start | bytes 196616 | tf_op jit(solution)/shard_map/ppermute | solution.py:384
  62.8 8.3 %collective-permute-start.6 = (bf16[32,1024]{1,0:T(8,128)(2,1)S(1)}, bf16[32,1024]{1,0:T(8,128)(2,1)S(1)}, u32[]{:S(2)}, u32[]{:S(2)}) collective-permute-start(bf16[32,1024]{1,0:T(8,128)(2,1)S(1)} %get-tuple-element.351), channel_id=1, source_target_pairs={{96,112},{80,96},{64,80},{48,64},{97,113},{81,97},{65,81},{49,65},... | collective-permute-start | bytes 196616 | tf_op jit(solution)/shard_map/ppermute | solution.py:384
  72.1 0.7 collective-permute-start.8
  72.8 0.7 collective-permute-start.9
  79.1 22.0 %collective-permute-start.10 = (bf16[32,1024]{1,0:T(8,128)(2,1)S(1)}, bf16[32,1024]{1,0:T(8,128)(2,1)S(1)}, u32[]{:S(2)}, u32[]{:S(2)}) collective-permute-start(bf16[32,1024]{1,0:T(8,128)(2,1)S(1)} %get-tuple-element.377), channel_id=1, source_target_pairs={{160,176},{144,160},{128,144},{112,128},{161,177},{145,161},{129,1... | collective-permute-start | bytes 196616 | tf_op jit(solution)/shard_map/ppermute | solution.py:384
  111.5 0.7 collective-permute-start.12
  121.5 0.7 collective-permute-start.13
  124.2 38.7 %collective-permute-start.14 = (bf16[32,1024]{1,0:T(8,128)(2,1)S(1)}, bf16[32,1024]{1,0:T(8,128)(2,1)S(1)}, u32[]{:S(2)}, u32[]{:S(2)}) collective-permute-start(bf16[32,1024]{1,0:T(8,128)(2,1)S(1)} %get-tuple-element.401), channel_id=1, source_target_pairs={{224,240},{208,224},{192,208},{176,192},{32,48},{16,32},{0,16},{22... | collective-permute-start | bytes 196616 | tf_op jit(solution)/shard_map/ppermute | solution.py:384
  165.0 15.9 %collective-permute-start.15 = (bf16[32,1024]{1,0:T(8,128)(2,1)S(1)}, bf16[32,1024]{1,0:T(8,128)(2,1)S(1)}, u32[]{:S(2)}, u32[]{:S(2)}) collective-permute-start(bf16[32,1024]{1,0:T(8,128)(2,1)S(1)} %get-tuple-element.407), channel_id=1, source_target_pairs={{224,240},{208,224},{192,208},{48,64},{32,48},{16,32},{0,16},{225,... | collective-permute-start | bytes 196616 | tf_op jit(solution)/shard_map/ppermute | solution.py:384
  183.3 18.7 %collective-permute-start.16 = (bf16[32,1024]{1,0:T(8,128)(2,1)S(1)}, bf16[32,1024]{1,0:T(8,128)(2,1)S(1)}, u32[]{:S(2)}, u32[]{:S(2)}) collective-permute-start(bf16[32,1024]{1,0:T(8,128)(2,1)S(1)} %get-tuple-element.413), channel_id=1, source_target_pairs={{224,240},{208,224},{64,80},{48,64},{32,48},{16,32},{225,241},{209... | collective-permute-start | bytes 196616 | tf_op jit(solution)/shard_map/ppermute | solution.py:382
  198.8 3.2 collective-permute-start.17
  204.1 7.1 %collective-permute-start.18 = (bf16[32,1024]{1,0:T(8,128)(2,1)S(1)}, bf16[32,1024]{1,0:T(8,128)(2,1)S(1)}, u32[]{:S(2)}, u32[]{:S(2)}) collective-permute-start(bf16[32,1024]{1,0:T(8,128)(2,1)S(1)} %get-tuple-element.420), channel_id=1, source_target_pairs={{224,240},{80,96},{64,80},{48,64},{32,48},{225,241},{81,97},{65,81... | collective-permute-start | bytes 196616 | tf_op jit(solution)/shard_map/ppermute | solution.py:382
  209.3 1.9 collective-permute-start.19
  213.2 22.4 %collective-permute-start.20 = (bf16[32,1024]{1,0:T(8,128)(2,1)S(1)}, bf16[32,1024]{1,0:T(8,128)(2,1)S(1)}, u32[]{:S(2)}, u32[]{:S(2)}) collective-permute-start(bf16[32,1024]{1,0:T(8,128)(2,1)S(1)} %get-tuple-element.427), channel_id=1, source_target_pairs={{96,112},{80,96},{64,80},{48,64},{208,192},{224,208},{240,224},{97... | collective-permute-start | bytes 196616 | tf_op jit(solution)/shard_map/ppermute | solution.py:384
  235.8 16.7 %collective-permute-start.21 = (bf16[32,1024]{1,0:T(8,128)(2,1)S(1)}, bf16[32,1024]{1,0:T(8,128)(2,1)S(1)}, u32[]{:S(2)}, u32[]{:S(2)}) collective-permute-start(bf16[32,1024]{1,0:T(8,128)(2,1)S(1)} %get-tuple-element.433), channel_id=1, source_target_pairs={{112,128},{96,112},{80,96},{64,80},{192,176},{208,192},{224,208},{... | collective-permute-start | bytes 196616 | tf_op jit(solution)/shard_map/ppermute | solution.py:384
  252.6 19.2 %collective-permute-start.22 = (bf16[32,1024]{1,0:T(8,128)(2,1)S(1)}, bf16[32,1024]{1,0:T(8,128)(2,1)S(1)}, u32[]{:S(2)}, u32[]{:S(2)}) collective-permute-start(bf16[32,1024]{1,0:T(8,128)(2,1)S(1)} %get-tuple-element.439), channel_id=1, source_target_pairs={{128,144},{112,128},{96,112},{80,96},{176,160},{192,176},{208,192}... | collective-permute-start | bytes 196616 | tf_op jit(solution)/shard_map/ppermute | solution.py:384
  271.9 1.3 collective-permute-start.23
  272.5 0.7 collective-permute-start.24
  273.7 1.3 collective-permute-start.25
  274.3 0.7 collective-permute-start.26
  275.1 1.3 collective-permute-start.27
  275.7 0.7 collective-permute-start.28
  276.5 1.3 collective-permute-start.29
  277.2 0.7 collective-permute-start.30
  283.0 62.1 %collective-permute-start.31 = (bf16[32,1024]{1,0:T(8,128)(2,1)S(1)}, bf16[32,1024]{1,0:T(8,128)(2,1)S(1)}, u32[]{:S(2)}, u32[]{:S(2)}) collective-permute-start(bf16[32,1024]{1,0:T(8,128)(2,1)S(1)} %get-tuple-element.473), channel_id=1, source_target_pairs={{208,224},{192,208},{176,192},{160,176},{96,80},{112,96},{128,112}... | collective-permute-start | bytes 196616 | tf_op jit(solution)/shard_map/ppermute | solution.py:384
  345.1 18.1 %collective-permute-start.32 = (bf16[32,1024]{1,0:T(8,128)(2,1)S(1)}, bf16[32,1024]{1,0:T(8,128)(2,1)S(1)}, u32[]{:S(2)}, u32[]{:S(2)}) collective-permute-start(bf16[32,1024]{1,0:T(8,128)(2,1)S(1)} %get-tuple-element.479), channel_id=1, source_target_pairs={{224,240},{208,224},{192,208},{176,192},{80,64},{96,80},{112,96},{... | collective-permute-start | bytes 196616 | tf_op jit(solution)/shard_map/ppermute | solution.py:384
  363.2 24.4 %collective-permute-start.33 = (bf16[32,1024]{1,0:T(8,128)(2,1)S(1)}, bf16[32,1024]{1,0:T(8,128)(2,1)S(1)}, u32[]{:S(2)}, u32[]{:S(2)}) collective-permute-start(bf16[32,1024]{1,0:T(8,128)(2,1)S(1)} %get-tuple-element.485), channel_id=1, source_target_pairs={{224,240},{208,224},{192,208},{64,48},{80,64},{96,80},{112,96},{22... | collective-permute-start | bytes 196616 | tf_op jit(solution)/shard_map/ppermute | solution.py:384
  390.8 2.6 collective-permute-start.34
  391.5 8.3 %collective-permute-start.35 = (bf16[32,1024]{1,0:T(8,128)(2,1)S(1)}, bf16[32,1024]{1,0:T(8,128)(2,1)S(1)}, u32[]{:S(2)}, u32[]{:S(2)}) collective-permute-start(bf16[32,1024]{1,0:T(8,128)(2,1)S(1)} %get-tuple-element.492), channel_id=1, source_target_pairs={{48,32},{64,48},{80,64},{96,80},{240,224},{49,33},{65,49},{81,65},... | collective-permute-start | bytes 196616 | tf_op jit(solution)/shard_map/ppermute | solution.py:382
  402.6 18.3 %collective-permute-start.36 = (bf16[32,1024]{1,0:T(8,128)(2,1)S(1)}, bf16[32,1024]{1,0:T(8,128)(2,1)S(1)}, u32[]{:S(2)}, u32[]{:S(2)}) collective-permute-start(bf16[32,1024]{1,0:T(8,128)(2,1)S(1)} %get-tuple-element.498), channel_id=1, source_target_pairs={{224,240},{225,241},{226,242},{227,243},{228,244},{229,245},{230,2... | collective-permute-start | bytes 196616 | tf_op jit(solution)/shard_map/ppermute | solution.py:382
  403.3 21.5 %collective-permute-start.37 = (bf16[32,1024]{1,0:T(8,128)(2,1)S(1)}, bf16[32,1024]{1,0:T(8,128)(2,1)S(1)}, u32[]{:S(2)}, u32[]{:S(2)}) collective-permute-start(bf16[32,1024]{1,0:T(8,128)(2,1)S(1)} %get-tuple-element.499), channel_id=1, source_target_pairs={{32,16},{48,32},{64,48},{80,64},{224,208},{240,224},{33,17},{49,33... | collective-permute-start | bytes 196616 | tf_op jit(solution)/shard_map/ppermute | solution.py:382
  427.8 16.6 %collective-permute-start.38 = (bf16[32,1024]{1,0:T(8,128)(2,1)S(1)}, bf16[32,1024]{1,0:T(8,128)(2,1)S(1)}, u32[]{:S(2)}, u32[]{:S(2)}) collective-permute-start(bf16[32,1024]{1,0:T(8,128)(2,1)S(1)} %get-tuple-element.505), channel_id=1, source_target_pairs={{16,0},{32,16},{48,32},{64,48},{208,192},{224,208},{240,224},{17,1... | collective-permute-start | bytes 196616 | tf_op jit(solution)/shard_map/ppermute | solution.py:384
  447.2 14.6 %collective-permute-start.39 = (bf16[32,1024]{1,0:T(8,128)(2,1)S(1)}, bf16[32,1024]{1,0:T(8,128)(2,1)S(1)}, u32[]{:S(2)}, u32[]{:S(2)}) collective-permute-start(bf16[32,1024]{1,0:T(8,128)(2,1)S(1)} %get-tuple-element.511), channel_id=1, source_target_pairs={{16,0},{32,16},{48,32},{192,176},{208,192},{224,208},{240,224},{17... | collective-permute-start | bytes 196616 | tf_op jit(solution)/shard_map/ppermute | solution.py:384
  462.9 0.7 collective-permute-start.41
  463.7 0.7 collective-permute-start.42
  474.8 56.6 %collective-permute-start.47 = (bf16[32,1024]{1,0:T(8,128)(2,1)S(1)}, bf16[32,1024]{1,0:T(8,128)(2,1)S(1)}, u32[]{:S(2)}, u32[]{:S(2)}) collective-permute-start(bf16[32,1024]{1,0:T(8,128)(2,1)S(1)} %get-tuple-element.559), channel_id=1, source_target_pairs={{64,48},{80,64},{96,80},{112,96},{65,49},{81,65},{97,81},{113,97},... | collective-permute-start | bytes 196616 | tf_op jit(solution)/shard_map/ppermute | solution.py:384
  534.2 8.3 %collective-permute-start.48 = (bf16[32,1024]{1,0:T(8,128)(2,1)S(1)}, bf16[32,1024]{1,0:T(8,128)(2,1)S(1)}, u32[]{:S(2)}, u32[]{:S(2)}) collective-permute-start(bf16[32,1024]{1,0:T(8,128)(2,1)S(1)} %get-tuple-element.565), channel_id=1, source_target_pairs={{48,32},{64,48},{80,64},{96,80},{49,33},{65,49},{81,65},{97,81},{5... | collective-permute-start | bytes 196616 | tf_op jit(solution)/shard_map/ppermute | solution.py:384
  545.6 9.3 %collective-permute-start.49 = (bf16[32,1024]{1,0:T(8,128)(2,1)S(1)}, bf16[32,1024]{1,0:T(8,128)(2,1)S(1)}, u32[]{:S(2)}, u32[]{:S(2)}) collective-permute-start(bf16[32,1024]{1,0:T(8,128)(2,1)S(1)} %get-tuple-element.571), channel_id=1, source_target_pairs={{32,16},{48,32},{64,48},{80,64},{33,17},{49,33},{65,49},{81,65},{3... | collective-permute-start | bytes 196616 | tf_op jit(solution)/shard_map/ppermute | solution.py:384
  557.8 8.3 %collective-permute-start.50 = (bf16[32,1024]{1,0:T(8,128)(2,1)S(1)}, bf16[32,1024]{1,0:T(8,128)(2,1)S(1)}, u32[]{:S(2)}, u32[]{:S(2)}) collective-permute-start(bf16[32,1024]{1,0:T(8,128)(2,1)S(1)} %get-tuple-element.577), channel_id=1, source_target_pairs={{16,0},{32,16},{48,32},{64,48},{17,1},{33,17},{49,33},{65,49},{18,... | collective-permute-start | bytes 196616 | tf_op jit(solution)/shard_map/ppermute | solution.py:384
  568.9 3.2 collective-permute-start.51
  (28 other events, 395.0 us)
Sparse Core Ops, SparseCore 0:
  9.8 44.9 all-gather.4
  56.7 40.7 all-gather.6
  584.6 86.4 reduce-scatter.1

commit v2 on v1

--- a/solution.py
+++ b/solution.py
@@ -8,7 +8,7 @@
 from jax.sharding import PartitionSpec as P
 
 PIECES = 4
-LAG = 12
+LAG = 7
 CHUNK = 512
 
 epsilon = 1e-05
@@ -123,33 +123,30 @@
     def ready_backward(self, t):
         return 0 <= 2 * self.layers - 2 + self.lag - t < self.layers
 
-    def edges(self, t):
-        up = [(s, s + 1) for s in self.forward(t) + self.forward_tan(t) if s + 1 < self.layers]
-        down = [(s, s - 1) for s in self.backward(t) + self.backward_tan(t) if s > 0]
-        return up, down
-
-
-def disjoint(edges):
-    sources, targets = [e[0] for e in edges], [e[1] for e in edges]
-    return len(set(sources)) == len(sources) and len(set(targets)) == len(targets)
-
-
-def tick_kernel(plan, t, split_in, split_out, with_probes, loss_scale, rows, width, hidden, *refs):
-    refs = list(refs)
-    state_in = refs[:5]
-    del state_in
-    refs = refs[5:]
+    def waves(self, t):
+        found = {}
+        for name, stages, way in (
+            ("tan_up", self.forward_tan(t), 1),
+            ("tan_down", self.backward_tan(t), -1),
+            ("up", self.forward(t), 1),
+            ("down", self.backward(t), -1),
+        ):
+            if stages:
+                found[name] = [(s, s + way) for s in stages if 0 <= s + way < self.layers]
+        return found
+
+
+def tick_kernel(plan, t, with_probes, loss_scale, rows, width, hidden, *refs):
+    refs = list(refs[5:])
+    waves = plan.waves(t)
     w_up, w_down, source, goal = refs[:4]
     refs = refs[4:]
     if with_probes:
         u_up, u_down = refs[:2]
         refs = refs[2:]
-    got_up = refs.pop(0)
-    got_down = refs.pop(0) if split_in else got_up
+    got = {name: refs.pop(0) for name in waves}
     sb_d, sb_f, sf_d, sf_f, sf_n = refs[:5]
-    refs = refs[5:]
-    put_up = refs.pop(0)
-    put_down = refs.pop(0) if split_out else put_up
+    put_up, put_down = refs[5:]
 
     layers, pieces, lag = plan.layers, plan.pieces, plan.lag
     stage = lax.axis_index("pipe")
@@ -169,7 +166,7 @@
         return sf_n[slot, at, :][:, :1]
 
     def forward(at):
-        stream = jnp.where(at_first, source[at, :], got_up[...]).astype(f32)
+        stream = jnp.where(at_first, source[at, :], got["up"][...]).astype(f32)
         centre = stream - mean(stream)
         inverse = lax.rsqrt(mean(centre * centre) + epsilon)
         normed = centre * inverse
@@ -203,7 +200,7 @@
             sf_d[AV, :, c] = dot_last(sb_f[A], u_down[c, :])
 
     def forward_tan(at):
-        tangent = got_up[...].astype(f32)
+        tangent = got["tan_up"][...].astype(f32)
         tangent = jnp.where(at_first, jnp.zeros_like(tangent), tangent)
         normed = sf_d[XH, at, :]
         inverse = narrow(INV, at)
@@ -232,7 +229,7 @@
             sb_d[TG, at, :] = (result.astype(f32) * loss_scale).astype(bf16)
 
     def backward(at):
-        cotan = jnp.where(at_last, sb_d[G, at, :], got_down[...])
+        cotan = jnp.where(at_last, sb_d[G, at, :], got["down"][...])
         sb_d[G, at, :] = cotan
         grad = jnp.zeros((rows, width), f32)
         for c in chunks:
@@ -260,7 +257,7 @@
             sf_d[PU, :, c] = dot_last(sb_f[PR], u_up[c, :])
 
     def backward_tan(at):
-        cotan_t = jnp.where(at_last, sb_d[TG, at, :], got_down[...])
+        cotan_t = jnp.where(at_last, sb_d[TG, at, :], got["tan_down"][...])
         sb_d[TG, at, :] = cotan_t
         grad_t = sf_d[PU, at, :]
         for c in chunks:
@@ -293,42 +290,110 @@
         pl.when(stage == 2 * layers - 2 + lag - t)(ready_backward)
 
 
-def curvature_kernel(sb_d, sb_f, out, hold, sems):
+BATCHES = ((4,), (3, 5), (2, 6), (1, 7, 0))
+
+
+def curvature_kernel(sb_d, sb_f, *refs):
+    mine, theirs = refs[: len(BATCHES)], refs[len(BATCHES) : 2 * len(BATCHES)]
+    hold = refs[-1]
+    hidden = sb_f.shape[2]
+    here = lax.axis_index("dp")
+    chip, core = here // 2, lax.rem(here, 2)
+    chips = lax.axis_size("dp") // 2
+    step = hold.shape[0]
+    part = step // 2
+    for kept, given, batch in zip(mine, theirs, BATCHES):
+        for i, far in enumerate(batch):
+            at = pl.ds(pl.multiple_of(lax.rem(chip + far, chips) * step, step), step)
+            left = jnp.concatenate((sb_d[X, :, at], sb_d[TX, :, at]), axis=0)
+            right = jnp.concatenate((sb_f[TP], sb_f[PR]), axis=0)
+            hold[:, :hidden] = dot_first(left, right)
+            left = jnp.concatenate((sb_d[TG, :, at], sb_d[G, :, at]), axis=0)
+            right = jnp.concatenate((sb_f[A], sb_f[TA]), axis=0)
+            hold[:, hidden:] = dot_first(left, right)
+            kept[i] = hold[pl.ds(pl.multiple_of(core * part, part), part), :].astype(bf16)
+            given[i] = hold[pl.ds(pl.multiple_of((1 - core) * part, part), part), :].astype(bf16)
+
+
+def curvature(sb_d, sb_f, groups):
     width, hidden = sb_d.shape[2], sb_f.shape[2]
-    step = hold.shape[1]
-    copies = []
-    for i in range(width // step):
-        at = slice(i * step, (i + 1) * step)
-        if i >= 2:
-            copies[i - 2].wait()
-        left = jnp.concatenate((sb_d[X, :, at], sb_d[TX, :, at]), axis=0)
-        right = jnp.concatenate((sb_f[TP], sb_f[PR]), axis=0)
-        hold[i % 2, :, :hidden] = dot_first(left, right).astype(bf16)
-        left = jnp.concatenate((sb_d[TG, :, at], sb_d[G, :, at]), axis=0)
-        right = jnp.concatenate((sb_f[A], sb_f[TA]), axis=0)
-        hold[i % 2, :, hidden:] = dot_first(left, right).astype(bf16)
-        copy = pltpu.make_async_copy(hold.at[i % 2], out.at[at, :], sems.at[i % 2])
-        copy.start()
-        copies.append(copy)
-    for copy in copies[-2:]:
-        copy.wait()
-
-
-def curvature(sb_d, sb_f):
-    width, hidden = sb_d.shape[2], sb_f.shape[2]
-    step = 128
-    return pl.pallas_call(
+    part = width // groups
+    parts = tuple(pltpu.VMEM((len(batch), part, 2 * hidden), bf16) for batch in BATCHES)
+    outs = pl.pallas_call(
         curvature_kernel,
-        out_shape=jax.ShapeDtypeStruct((width, 2 * hidden), bf16),
+        out_shape=parts + parts,
         in_specs=[IN_VMEM, IN_VMEM],
-        out_specs=ANYWHERE,
-        scratch_shapes=[
-            pltpu.VMEM((2, step, 2 * hidden), bf16),
-            pltpu.SemaphoreType.DMA((2,)),
-        ],
-        compiler_params=pltpu.CompilerParams(vmem_limit_bytes=16 << 20),
+        out_specs=(IN_VMEM,) * (2 * len(BATCHES)),
+        scratch_shapes=[pltpu.VMEM((2 * part, 2 * hidden), f32)],
+        compiler_params=pltpu.CompilerParams(vmem_limit_bytes=12 << 20),
         name="curvature",
     )(vmem(sb_d), vmem(sb_f))
+    return outs[: len(BATCHES)], outs[len(BATCHES) :]
+
+
+def routes(groups):
+    return (
+        [(i, (i + 2) % groups) for i in range(groups)],
+        [(i, (i - 2) % groups) for i in range(groups)],
+        [(i, i ^ 1) for i in range(groups)],
+    )
+
+
+def assemble(blocks, halves, groups, part, hidden):
+    pieces = [(array, i, (i,), far, other) for array, far, other in blocks for i in range(2)]
+    pieces += [(array, i, (), far, other) for array, i, far, other in halves]
+    arrays = [b[0] for b in blocks] + [h[0] for h in halves]
+    places = [p for p in range(len(blocks)) for _ in range(2)] + [len(blocks) + p for p in range(len(halves))]
+
+    def kernel(*refs):
+        sources, targets, sems = refs[: len(arrays)], refs[len(arrays) : -1], refs[-1]
+        here = lax.axis_index("dp")
+        chip, core = here // 2, lax.rem(here, 2)
+        chips = groups // 2
+        copies = []
+        for n, ((_, probe, index, far, other), place) in enumerate(zip(pieces, places)):
+            block = lax.rem(chip + far + chips, chips) * 2 + (1 - core if other else core)
+            row = pl.ds(pl.multiple_of(block * part, part), part)
+            source = sources[place].at[index] if index else sources[place]
+            copies.append(pltpu.make_async_copy(source, targets[probe].at[row, :], sems.at[n]))
+        for copy in copies:
+            copy.start()
+        for copy in copies:
+            copy.wait()
+
+    return pl.pallas_call(
+        kernel,
+        out_shape=tuple(pltpu.VMEM((groups * part, hidden), bf16) for _ in range(2)),
+        in_specs=[ANYWHERE] * len(arrays),
+        out_specs=(IN_VMEM,) * 2,
+        scratch_shapes=[pltpu.SemaphoreType.DMA((len(pieces),))],
+        compiler_params=pltpu.CompilerParams(vmem_limit_bytes=1 << 20),
+        name="assemble",
+    )(*arrays)
+
+
+def scatter(mine, theirs, groups, hidden):
+    ahead, behind, across = routes(groups)
+
+    def wide(kept, given):
+        return kept.astype(f32) + lax.ppermute(given, "dp", across).astype(f32)
+
+    far = wide(mine[0], theirs[0])[0].astype(bf16)
+    from_behind = lax.ppermute(far[:, :hidden], "dp", ahead)
+    from_ahead = lax.ppermute(far[:, hidden:], "dp", behind)
+    blank_half = ((0, 0), (0, hidden)), ((0, 0), (hidden, 0))
+    pair = wide(mine[1], theirs[1])
+    up = (pair[0] + jnp.pad(from_behind.astype(f32), blank_half[0])).astype(bf16)
+    down = (pair[1] + jnp.pad(from_ahead.astype(f32), blank_half[1])).astype(bf16)
+    for kept, given in zip(mine[2:], theirs[2:]):
+        from_behind = lax.ppermute(up, "dp", ahead)
+        from_ahead = lax.ppermute(down, "dp", behind)
+        pair = wide(kept, given)
+        up = (pair[0] + from_behind.astype(f32)).astype(bf16)
+        down = (pair[1] + from_ahead.astype(f32)).astype(bf16)
+    from_behind = lax.ppermute(up, "dp", ahead)
+    from_ahead = lax.ppermute(down, "dp", behind)
+    return pair[2] + from_behind.astype(f32) + from_ahead.astype(f32)
 
 
 def on_device(embedded, targets, w_up, w_down, probe_up, probe_down):
@@ -336,13 +401,23 @@
     groups = lax.axis_size("dp")
     tokens, width = embedded.shape
     hidden = w_up.shape[2]
+    part = probe_up.shape[1]
     rows = tokens // PIECES
     loss_scale = 1.0 / (tokens * groups)
     plan = Plan(layers, PIECES, LAG)
-
-    gathered = [
-        lax.all_gather(probe[0], "dp", axis=0, tiled=True) for probe in (probe_up, probe_down)
-    ]
+    ahead, behind, across = routes(groups)
+
+    def swap(array):
+        return lax.ppermute(array, "dp", across)
+
+    def ring(both):
+        return [lax.ppermute(both[0], "dp", ahead), lax.ppermute(both[1], "dp", behind)]
+
+    own = jnp.stack((probe_up[0], probe_down[0]))
+    moving = ring([own, own])
+    blocks = [(own, 0, False), (swap(own), 0, True)]
+    halves = []
+
     held = load((w_up[0], w_down[0], embedded, targets))
     *state, nothing = blank(
         (
@@ -355,36 +430,46 @@
         )
     )
     probes = None
-    got = (nothing,)
+    got = {"up": nothing}
     packet = pltpu.VMEM((rows, width), bf16)
+    ring_ticks = {0: 1, 2: 2, 3: 3, 4: 4}
     for t in range(plan.ticks):
         if t == LAG - 1:
-            probes = load(gathered)
-        up, down = plan.edges(t)
-        split_out = not disjoint(up + down)
+            probes = assemble(blocks, halves, groups, part, hidden)
+        waves = plan.waves(t)
         with_probes = plan.ready_forward(t) or plan.ready_backward(t)
-        operands = list(state) + list(held) + (list(probes) if with_probes else []) + list(got)
-        results = 2 if split_out else 1
+        operands = list(state) + list(held) + (list(probes) if with_probes else [])
+        operands += [got.get(name, nothing) for name in waves]
         outs = pl.pallas_call(
-            functools.partial(
-                tick_kernel, plan, t, len(got) == 2, split_out, with_probes, loss_scale, rows, width, hidden
-            ),
-            out_shape=tuple(pltpu.VMEM(s.shape, s.dtype) for s in state) + (packet,) * results,
+            functools.partial(tick_kernel, plan, t, with_probes, loss_scale, rows, width, hidden),
+            out_shape=tuple(pltpu.VMEM(s.shape, s.dtype) for s in state) + (packet,) * 2,
             in_specs=[IN_VMEM] * len(operands),
-            out_specs=(IN_VMEM,) * (5 + results),
+            out_specs=(IN_VMEM,) * 7,
             input_output_aliases={i: i for i in range(5)},
             compiler_params=pltpu.CompilerParams(vmem_limit_bytes=8 << 20),
-            cost_estimate=pl.CostEstimate(flops=1 << 28, bytes_accessed=1 << 23, transcendentals=0),
+            cost_estimate=pl.CostEstimate(flops=1 << 30, bytes_accessed=1 << 23, transcendentals=0),
             name="tick",
         )(*[vmem(o) for o in operands])
-        state, sent = outs[:5], outs[5:]
-        if split_out:
-            got = (lax.ppermute(sent[0], "pipe", up), lax.ppermute(sent[1], "pipe", down))
-        elif up + down:
-            got = (lax.ppermute(sent[0], "pipe", up + down),)
-
-    sums = curvature(state[0], state[1])
-    summed = lax.psum_scatter(sums, "dp", scatter_dimension=0, tiled=True).astype(f32)
+        state, sent = outs[:5], {"up": outs[5], "down": outs[6]}
+        got = {
+            name: lax.ppermute(sent[name.removeprefix("tan_")], "pipe", edges)
+            for name, edges in waves.items()
+            if edges
+        }
+        if t in ring_ticks:
+            step = ring_ticks[t]
+            got["up"], moving[0], moving[1] = lax.optimization_barrier((got["up"], *moving))
+            if step < 4:
+                arrived = moving
+                moving = ring(arrived if step < 3 else [arrived[0][0], arrived[1][1]])
+                for array, away in zip(arrived, (-step, step)):
+                    blocks += [(array, away, False), (swap(array), away, True)]
+            else:
+                for i, array in enumerate(moving):
+                    halves += [(array, i, step, False), (swap(array), i, step, True)]
+
+    mine, theirs = curvature(state[0], state[1], groups)
+    summed = scatter(mine, theirs, groups, hidden)
     curv_up = probe_up[0].astype(f32) * summed[:, :hidden]
     curv_down = probe_down[0].astype(f32) * summed[:, hidden:]
     return (curv_up[None], curv_down[None])

time: 690 us -> 645 us (0.935)
  the two profiles are of different devices: /device:TPU:6 before, /device:TPU:32 now
where the time goes in v2:
time: 645 us; the launch traced here: 635 us
  starting transfers between devices  396 us (61%)
  waiting for transfers between devices  148 us (23%)
  Pallas kernels  83.8 us (13%)
    ppermute x72, starting transfers between devices, on_device(): lax.ppermute(sent[name.removeprefix('tan_')], 'pipe', edges)  364 us
    ppermute x72, waiting for transfers between devices, on_device(): lax.ppermute(sent[name.removeprefix('tan_')], 'pipe', edges)  91.8 us
    pallas_call x42, Pallas kernels, on_device(): pl.pallas_call(functools.partial(tick_kernel, plan, t, with_probes, loss_...  73.5 us
    ppermute x3, waiting for transfers between devices, scatter(): from_behind = lax.ppermute(up, 'dp', ahead)  28.6 us
  transfers between devices with their start and end apart: 101, of which 32 were waited for; matrix products, arithmetic and copies ran while one was open for 0% of the time, Pallas kernels for 3%

profile of v2, /device:TPU:32, one launch (start us, length us, event | category | flops | bytes accessed | tf_op | source)
XLA Modules:
  0.0 635.0 jit_solution(10223518696771887203)
XLA Ops:
  4.7 3.5 load.1
  16.5 3.8 collective-permute-done.1.refs_2_
  25.9 3.4 collective-permute-start.3
  34.0 4.3 collective-permute-start.4
  40.1 3.3 collective-permute-start.9
  46.2 4.3 collective-permute-start.7
  53.0 3.2 collective-permute-start.12
  57.7 4.3 collective-permute-done.12.refs_16_
  64.2 8.2 %collective-permute-start.19 = (bf16[2,64,2048]{2,1,0:T(8,128)(2,1)S(1)}, bf16[2,64,2048]{2,1,0:T(8,128)(2,1)S(1)}, u32[]{:S(2)}, u32[]{:S(2)}) collective-permute-start(bf16[2,64,2048]{2,1,0:T(8,128)(2,1)S(1)} %collective-permute-done.9.refs_12_), channel_id=1, source_target_pairs={{0,1},{1,0},{2,3},{3,2},{4,5},{5,4},{6,7},{7,6},{8,9},{9,8},{10,11... | collective-permute-start | bytes 1572872 | tf_op jit(solution)/shard_map/ppermute | solution.py:411
  89.5 4.4 collective-permute-start.26
  99.0 4.3 collective-permute-start.28
  108.9 4.3 collective-permute-start.30
  117.7 34.1 %collective-permute-start.35 = (bf16[32,1024]{1,0:T(8,128)(2,1)S(1)}, bf16[32,1024]{1,0:T(8,128)(2,1)S(1)}, u32[]{:S(2)}, u32[]{:S(2)}) collective-permute-start(bf16[32,1024]{1,0:T(8,128)(2,1)S(1)} %get-tuple-element.392), channel_id=1, source_target_pairs={{192,208},{176,192},{160,176},{144,160},{193,209},{177,193},{161,1... | collective-permute-start | bytes 196616 | tf_op jit(solution)/shard_map/ppermute | solution.py:455
  153.4 18.4 %collective-permute-start.37 = (bf16[32,1024]{1,0:T(8,128)(2,1)S(1)}, bf16[32,1024]{1,0:T(8,128)(2,1)S(1)}, u32[]{:S(2)}, u32[]{:S(2)}) collective-permute-start(bf16[32,1024]{1,0:T(8,128)(2,1)S(1)} %get-tuple-element.398), channel_id=1, source_target_pairs={{208,224},{192,208},{176,192},{160,176},{209,225},{193,209},{177,1... | collective-permute-start | bytes 196616 | tf_op jit(solution)/shard_map/ppermute | solution.py:455
  173.1 18.4 %collective-permute-start.39 = (bf16[32,1024]{1,0:T(8,128)(2,1)S(1)}, bf16[32,1024]{1,0:T(8,128)(2,1)S(1)}, u32[]{:S(2)}, u32[]{:S(2)}) collective-permute-start(bf16[32,1024]{1,0:T(8,128)(2,1)S(1)} %get-tuple-element.404), channel_id=1, source_target_pairs={{224,240},{208,224},{192,208},{176,192},{225,241},{209,225},{193,2... | collective-permute-start | bytes 196616 | tf_op jit(solution)/shard_map/ppermute | solution.py:455
  199.5 4.3 collective-permute-start.49
  203.9 51.2 %collective-permute-start.50 = (bf16[32,1024]{1,0:T(8,128)(2,1)S(1)}, bf16[32,1024]{1,0:T(8,128)(2,1)S(1)}, u32[]{:S(2)}, u32[]{:S(2)}) collective-permute-start(bf16[32,1024]{1,0:T(8,128)(2,1)S(1)} %get-tuple-element.437), channel_id=1, source_target_pairs={{192,208},{176,192},{160,176},{144,160},{193,209},{177,193},{161,1... | collective-permute-start | bytes 196616 | tf_op jit(solution)/shard_map/ppermute | solution.py:455
  255.1 13.1 %collective-permute-start.51 = (bf16[32,1024]{1,0:T(8,128)(2,1)S(1)}, bf16[32,1024]{1,0:T(8,128)(2,1)S(1)}, u32[]{:S(2)}, u32[]{:S(2)}) collective-permute-start(bf16[32,1024]{1,0:T(8,128)(2,1)S(1)} %get-tuple-element.438), channel_id=1, source_target_pairs={{192,176},{208,192},{224,208},{240,224},{193,177},{209,193},{225,2... | collective-permute-start | bytes 196616 | tf_op jit(solution)/shard_map/ppermute | solution.py:455
  268.3 21.3 %collective-permute-start.52 = (bf16[32,1024]{1,0:T(8,128)(2,1)S(1)}, bf16[32,1024]{1,0:T(8,128)(2,1)S(1)}, u32[]{:S(2)}, u32[]{:S(2)}) collective-permute-start(bf16[32,1024]{1,0:T(8,128)(2,1)S(1)} %get-tuple-element.444), channel_id=1, source_target_pairs={{208,224},{192,208},{176,192},{160,176},{209,225},{193,209},{177,1... | collective-permute-start | bytes 196616 | tf_op jit(solution)/shard_map/ppermute | solution.py:455
  289.6 13.1 %collective-permute-start.53 = (bf16[32,1024]{1,0:T(8,128)(2,1)S(1)}, bf16[32,1024]{1,0:T(8,128)(2,1)S(1)}, u32[]{:S(2)}, u32[]{:S(2)}) collective-permute-start(bf16[32,1024]{1,0:T(8,128)(2,1)S(1)} %get-tuple-element.445), channel_id=1, source_target_pairs={{176,160},{192,176},{208,192},{224,208},{177,161},{193,177},{209,1... | collective-permute-start | bytes 196616 | tf_op jit(solution)/shard_map/ppermute | solution.py:455
  302.8 21.2 %collective-permute-start.54 = (bf16[32,1024]{1,0:T(8,128)(2,1)S(1)}, bf16[32,1024]{1,0:T(8,128)(2,1)S(1)}, u32[]{:S(2)}, u32[]{:S(2)}) collective-permute-start(bf16[32,1024]{1,0:T(8,128)(2,1)S(1)} %get-tuple-element.451), channel_id=1, source_target_pairs={{224,240},{208,224},{192,208},{176,192},{225,241},{209,225},{193,2... | collective-permute-start | bytes 196616 | tf_op jit(solution)/shard_map/ppermute | solution.py:455
  324.0 12.9 %collective-permute-start.55 = (bf16[32,1024]{1,0:T(8,128)(2,1)S(1)}, bf16[32,1024]{1,0:T(8,128)(2,1)S(1)}, u32[]{:S(2)}, u32[]{:S(2)}) collective-permute-start(bf16[32,1024]{1,0:T(8,128)(2,1)S(1)} %get-tuple-element.452), channel_id=1, source_target_pairs={{160,144},{176,160},{192,176},{208,192},{161,145},{177,161},{193,1... | collective-permute-start | bytes 196616 | tf_op jit(solution)/shard_map/ppermute | solution.py:455
  340.8 5.7 tick.66
  351.9 50.8 %collective-permute-start.66 = (bf16[32,1024]{1,0:T(8,128)(2,1)S(1)}, bf16[32,1024]{1,0:T(8,128)(2,1)S(1)}, u32[]{:S(2)}, u32[]{:S(2)}) collective-permute-start(bf16[32,1024]{1,0:T(8,128)(2,1)S(1)} %get-tuple-element.485), channel_id=1, source_target_pairs={{192,176},{208,192},{224,208},{240,224},{193,177},{209,193},{225,2... | collective-permute-start | bytes 196616 | tf_op jit(solution)/shard_map/ppermute | solution.py:455
  404.4 19.3 %collective-permute-start.68 = (bf16[32,1024]{1,0:T(8,128)(2,1)S(1)}, bf16[32,1024]{1,0:T(8,128)(2,1)S(1)}, u32[]{:S(2)}, u32[]{:S(2)}) collective-permute-start(bf16[32,1024]{1,0:T(8,128)(2,1)S(1)} %get-tuple-element.491), channel_id=1, source_target_pairs={{176,160},{192,176},{208,192},{224,208},{177,161},{193,177},{209,1... | collective-permute-start | bytes 196616 | tf_op jit(solution)/shard_map/ppermute | solution.py:455
  425.0 19.5 %collective-permute-start.70 = (bf16[32,1024]{1,0:T(8,128)(2,1)S(1)}, bf16[32,1024]{1,0:T(8,128)(2,1)S(1)}, u32[]{:S(2)}, u32[]{:S(2)}) collective-permute-start(bf16[32,1024]{1,0:T(8,128)(2,1)S(1)} %get-tuple-element.497), channel_id=1, source_target_pairs={{160,144},{176,160},{192,176},{208,192},{161,145},{177,161},{193,1... | collective-permute-start | bytes 196616 | tf_op jit(solution)/shard_map/ppermute | solution.py:455
  449.3 13.6 %collective-permute-done.75.refs_12_ = bf16[32,1024]{1,0:T(8,128)(2,1)S(1)} collective-permute-done((bf16[32,1024]{1,0:T(8,128)(2,1)S(1)}, bf16[32,1024]{1,0:T(8,128)(2,1)S(1)}, u32[]{:S(2)}, u32[]{:S(2)}) %collective-permute-start.75) | collective-permute-done | bytes 65568 | tf_op jit(solution)/shard_map/ppermute | solution.py:455
  463.0 3.4 tick.73
  468.4 4.2 collective-permute-done.77.refs_12_
  472.6 3.4 tick.74
  478.0 5.3 collective-permute-done.79.refs_12_
  483.3 3.6 tick.75
  488.9 4.4 collective-permute-done.81.refs_12_
  493.3 3.4 tick.76
  504.6 30.1 %collective-permute-done.85.refs_9_ = bf16[32,1024]{1,0:T(8,128)(2,1)S(1)} collective-permute-done((bf16[32,1024]{1,0:T(8,128)(2,1)S(1)}, bf16[32,1024]{1,0:T(8,128)(2,1)S(1)}, u32[]{:S(2)}, u32[]{:S(2)}) %collective-permute-start.85) | collective-permute-done | bytes 65568 | tf_op jit(solution)/shard_map/ppermute | solution.py:455
  534.6 3.5 tick.80
  539.4 7.0 %collective-permute-done.86.refs_9_ = bf16[32,1024]{1,0:T(8,128)(2,1)S(1)} collective-permute-done((bf16[32,1024]{1,0:T(8,128)(2,1)S(1)}, bf16[32,1024]{1,0:T(8,128)(2,1)S(1)}, u32[]{:S(2)}, u32[]{:S(2)}) %collective-permute-start.86) | collective-permute-done | bytes 65568 | tf_op jit(solution)/shard_map/ppermute | solution.py:455
  546.4 3.5 tick.81
  551.2 7.6 %collective-permute-done.87.refs_9_ = bf16[32,1024]{1,0:T(8,128)(2,1)S(1)} collective-permute-done((bf16[32,1024]{1,0:T(8,128)(2,1)S(1)}, bf16[32,1024]{1,0:T(8,128)(2,1)S(1)}, u32[]{:S(2)}, u32[]{:S(2)}) %collective-permute-start.87) | collective-permute-done | bytes 65568 | tf_op jit(solution)/shard_map/ppermute | solution.py:455
  558.8 3.5 tick.82
  563.5 4.9 collective-permute-done.88.refs_9_
  568.4 3.7 tick.83
  572.1 5.7 curvature.1
  583.1 5.3 collective-permute-done.93
  593.4 10.4 %collective-permute-done.94 = bf16[64,4096]{1,0:T(8,128)(2,1)S(1)} collective-permute-done((bf16[64,4096]{1,0:T(8,128)(2,1)S(1)}, bf16[64,4096]{1,0:T(8,128)(2,1)S(1)}, u32[]{:S(2)}, u32[]{:S(2)}) %collective-permute-start.94) | collective-permute-done | bytes 524320 | tf_op jit(solution)/shard_map/ppermute | solution.py:389
  603.8 3.1 collective-permute-done.98
  609.7 9.4 %collective-permute-done.95 = bf16[64,4096]{1,0:T(8,128)(2,1)S(1)} collective-permute-done((bf16[64,4096]{1,0:T(8,128)(2,1)S(1)}, bf16[64,4096]{1,0:T(8,128)(2,1)S(1)}, u32[]{:S(2)}, u32[]{:S(2)}) %collective-permute-start.95) | collective-permute-done | bytes 524320 | tf_op jit(solution)/shard_map/ppermute | solution.py:389
  623.0 8.8 %collective-permute-done.96 = bf16[64,4096]{1,0:T(8,128)(2,1)S(1)} collective-permute-done((bf16[64,4096]{1,0:T(8,128)(2,1)S(1)}, bf16[64,4096]{1,0:T(8,128)(2,1)S(1)}, u32[]{:S(2)}, u32[]{:S(2)}) %collective-permute-start.96) | collective-permute-done | bytes 524320 | tf_op jit(solution)/shard_map/ppermute | solution.py:394
  (218 shorter events, 130.6 us)
Async XLA Ops:
  2.6 13.9 %collective-permute-start.2 = (bf16[2,64,2048]{2,1,0:T(8,128)(2,1)S(1)}, bf16[2,64,2048]{2,1,0:T(8,128)(2,1)S(1)}, u32[]{:S(2)}, u32[]{:S(2)}) collective-permute-start(bf16[2,64,2048]{2,1,0:T(8,128)(2,1)S(1)} %constant_dynamic-update-slice_fusion.refs_0_), channel_id=1, source_target_pairs={{0,14},{1,15},{2,0},{3,1},{4,2},{5,3},{6,4},{7,5},{8,6},{9,7},{10,... | collective-permute-start | bytes 1572872 | tf_op jit(solution)/shard_map/ppermute | solution.py:414
  4.5 15.8 %collective-permute-start.1 = (bf16[2,64,2048]{2,1,0:T(8,128)(2,1)S(1)}, bf16[2,64,2048]{2,1,0:T(8,128)(2,1)S(1)}, u32[]{:S(2)}, u32[]{:S(2)}) collective-permute-start(bf16[2,64,2048]{2,1,0:T(8,128)(2,1)S(1)} %constant_dynamic-update-slice_fusion.refs_0_), channel_id=1, source_target_pairs={{0,2},{1,3},{2,4},{3,5},{4,6},{5,7},{6,8},{7,9},{8,10},{9,11},{10,... | collective-permute-start | bytes 1572872 | tf_op jit(solution)/shard_map/ppermute | solution.py:414
  20.3 19.9 %collective-permute-start.5 = (bf16[2,64,2048]{2,1,0:T(8,128)(2,1)S(1)}, bf16[2,64,2048]{2,1,0:T(8,128)(2,1)S(1)}, u32[]{:S(2)}, u32[]{:S(2)}) collective-permute-start(bf16[2,64,2048]{2,1,0:T(8,128)(2,1)S(1)} %collective-permute-done.1.refs_2_), channel_id=1, source_target_pairs={{0,2},{1,3},{2,4},{3,5},{4,6},{5,7},{6,8},{7,9},{8,10},{9,11},{10,... | collective-permute-start | bytes 1572872 | tf_op jit(solution)/shard_map/ppermute | solution.py:414
  20.3 19.9 %collective-permute-start.6 = (bf16[2,64,2048]{2,1,0:T(8,128)(2,1)S(1)}, bf16[2,64,2048]{2,1,0:T(8,128)(2,1)S(1)}, u32[]{:S(2)}, u32[]{:S(2)}) collective-permute-start(bf16[2,64,2048]{2,1,0:T(8,128)(2,1)S(1)} %collective-permute-done.2.refs_4_), channel_id=1, source_target_pairs={{0,14},{1,15},{2,0},{3,1},{4,2},{5,3},{6,4},{7,5},{8,6},{9,7},{10,... | collective-permute-start | bytes 1572872 | tf_op jit(solution)/shard_map/ppermute | solution.py:414
  40.1 12.2 %collective-permute-start.8 = (bf16[2,64,2048]{2,1,0:T(8,128)(2,1)S(1)}, bf16[2,64,2048]{2,1,0:T(8,128)(2,1)S(1)}, u32[]{:S(2)}, u32[]{:S(2)}) collective-permute-start(bf16[2,64,2048]{2,1,0:T(8,128)(2,1)S(1)} %collective-permute-done.5.refs_6_), channel_id=1, source_target_pairs={{0,2},{1,3},{2,4},{3,5},{4,6},{5,7},{6,8},{7,9},{8,10},{9,11},{10,... | collective-permute-start | bytes 1572872 | tf_op jit(solution)/shard_map/ppermute | solution.py:414
  40.1 12.9 %collective-permute-start.9 = (bf16[2,64,2048]{2,1,0:T(8,128)(2,1)S(1)}, bf16[2,64,2048]{2,1,0:T(8,128)(2,1)S(1)}, u32[]{:S(2)}, u32[]{:S(2)}) collective-permute-start(bf16[2,64,2048]{2,1,0:T(8,128)(2,1)S(1)} %collective-permute-done.6.refs_8_), channel_id=1, source_target_pairs={{0,14},{1,15},{2,0},{3,1},{4,2},{5,3},{6,4},{7,5},{8,6},{9,7},{10,... | collective-permute-start | bytes 1572872 | tf_op jit(solution)/shard_map/ppermute | solution.py:414
  50.5 6.4 %collective-permute-start.14 = (bf16[2,64,2048]{2,1,0:T(8,128)(2,1)S(1)}, bf16[2,64,2048]{2,1,0:T(8,128)(2,1)S(1)}, u32[]{:S(2)}, u32[]{:S(2)}) collective-permute-start(bf16[2,64,2048]{2,1,0:T(8,128)(2,1)S(1)} %collective-permute-done.1.refs_2_), channel_id=1, source_target_pairs={{0,1},{1,0},{2,3},{3,2},{4,5},{5,4},{6,7},{7,6},{8,9},{9,8},{10,11... | collective-permute-start | bytes 1572872 | tf_op jit(solution)/shard_map/ppermute | solution.py:411
  52.3 20.1 %collective-permute-start.15 = (bf16[2,64,2048]{2,1,0:T(8,128)(2,1)S(1)}, bf16[2,64,2048]{2,1,0:T(8,128)(2,1)S(1)}, u32[]{:S(2)}, u32[]{:S(2)}) collective-permute-start(bf16[2,64,2048]{2,1,0:T(8,128)(2,1)S(1)} %collective-permute-done.2.refs_4_), channel_id=1, source_target_pairs={{0,1},{1,0},{2,3},{3,2},{4,5},{5,4},{6,7},{7,6},{8,9},{9,8},{10,11... | collective-permute-start | bytes 1572872 | tf_op jit(solution)/shard_map/ppermute | solution.py:411
  52.3 20.3 %collective-permute-start.16 = (bf16[2,64,2048]{2,1,0:T(8,128)(2,1)S(1)}, bf16[2,64,2048]{2,1,0:T(8,128)(2,1)S(1)}, u32[]{:S(2)}, u32[]{:S(2)}) collective-permute-start(bf16[2,64,2048]{2,1,0:T(8,128)(2,1)S(1)} %collective-permute-done.5.refs_6_), channel_id=1, source_target_pairs={{0,1},{1,0},{2,3},{3,2},{4,5},{5,4},{6,7},{7,6},{8,9},{9,8},{10,11... | collective-permute-start | bytes 1572872 | tf_op jit(solution)/shard_map/ppermute | solution.py:411
  53.0 9.0 %collective-permute-start.12 = (bf16[64,2048]{1,0:T(8,128)(2,1)S(1)}, bf16[64,2048]{1,0:T(8,128)(2,1)S(1)}, u32[]{:S(2)}, u32[]{:S(2)}) collective-permute-start(bf16[64,2048]{1,0:T(8,128)(2,1)S(1)} %slice_bitcast_fusion.7), channel_id=1, source_target_pairs={{0,14},{1,15},{2,0},{3,1},{4,2},{5,3},{6,4},{7,5},{8,6},{9,7},{10,... | collective-permute-start | bytes 786440 | tf_op jit(solution)/shard_map/ppermute | solution.py:414
  56.3 8.0 %collective-permute-start.11 = (bf16[64,2048]{1,0:T(8,128)(2,1)S(1)}, bf16[64,2048]{1,0:T(8,128)(2,1)S(1)}, u32[]{:S(2)}, u32[]{:S(2)}) collective-permute-start(bf16[64,2048]{1,0:T(8,128)(2,1)S(1)} %slice_bitcast_fusion.8), channel_id=1, source_target_pairs={{0,2},{1,3},{2,4},{3,5},{4,6},{5,7},{6,8},{7,9},{8,10},{9,11},{10,... | collective-permute-start | bytes 786440 | tf_op jit(solution)/shard_map/ppermute | solution.py:414
  57.6 16.0 %collective-permute-start.17 = (bf16[2,64,2048]{2,1,0:T(8,128)(2,1)S(1)}, bf16[2,64,2048]{2,1,0:T(8,128)(2,1)S(1)}, u32[]{:S(2)}, u32[]{:S(2)}) collective-permute-start(bf16[2,64,2048]{2,1,0:T(8,128)(2,1)S(1)} %collective-permute-done.6.refs_8_), channel_id=1, source_target_pairs={{0,1},{1,0},{2,3},{3,2},{4,5},{5,4},{6,7},{7,6},{8,9},{9,8},{10,11... | collective-permute-start | bytes 1572872 | tf_op jit(solution)/shard_map/ppermute | solution.py:411
  62.0 12.7 %collective-permute-start.18 = (bf16[2,64,2048]{2,1,0:T(8,128)(2,1)S(1)}, bf16[2,64,2048]{2,1,0:T(8,128)(2,1)S(1)}, u32[]{:S(2)}, u32[]{:S(2)}) collective-permute-start(bf16[2,64,2048]{2,1,0:T(8,128)(2,1)S(1)} %collective-permute-done.8.refs_10_), channel_id=1, source_target_pairs={{0,1},{1,0},{2,3},{3,2},{4,5},{5,4},{6,7},{7,6},{8,9},{9,8},{10,11... | collective-permute-start | bytes 1572872 | tf_op jit(solution)/shard_map/ppermute | solution.py:411
  64.2 10.5 %collective-permute-start.19 = (bf16[2,64,2048]{2,1,0:T(8,128)(2,1)S(1)}, bf16[2,64,2048]{2,1,0:T(8,128)(2,1)S(1)}, u32[]{:S(2)}, u32[]{:S(2)}) collective-permute-start(bf16[2,64,2048]{2,1,0:T(8,128)(2,1)S(1)} %collective-permute-done.9.refs_12_), channel_id=1, source_target_pairs={{0,1},{1,0},{2,3},{3,2},{4,5},{5,4},{6,7},{7,6},{8,9},{9,8},{10,11... | collective-permute-start | bytes 1572872 | tf_op jit(solution)/shard_map/ppermute | solution.py:411
  89.5 6.3 collective-permute-start.26
  99.0 6.2 collective-permute-start.28
  117.7 34.8 %collective-permute-start.35 = (bf16[32,1024]{1,0:T(8,128)(2,1)S(1)}, bf16[32,1024]{1,0:T(8,128)(2,1)S(1)}, u32[]{:S(2)}, u32[]{:S(2)}) collective-permute-start(bf16[32,1024]{1,0:T(8,128)(2,1)S(1)} %get-tuple-element.392), channel_id=1, source_target_pairs={{192,208},{176,192},{160,176},{144,160},{193,209},{177,193},{161,1... | collective-permute-start | bytes 196616 | tf_op jit(solution)/shard_map/ppermute | solution.py:455
  153.4 19.0 %collective-permute-start.37 = (bf16[32,1024]{1,0:T(8,128)(2,1)S(1)}, bf16[32,1024]{1,0:T(8,128)(2,1)S(1)}, u32[]{:S(2)}, u32[]{:S(2)}) collective-permute-start(bf16[32,1024]{1,0:T(8,128)(2,1)S(1)} %get-tuple-element.398), channel_id=1, source_target_pairs={{208,224},{192,208},{176,192},{160,176},{209,225},{193,209},{177,1... | collective-permute-start | bytes 196616 | tf_op jit(solution)/shard_map/ppermute | solution.py:455
  173.1 19.0 %collective-permute-start.39 = (bf16[32,1024]{1,0:T(8,128)(2,1)S(1)}, bf16[32,1024]{1,0:T(8,128)(2,1)S(1)}, u32[]{:S(2)}, u32[]{:S(2)}) collective-permute-start(bf16[32,1024]{1,0:T(8,128)(2,1)S(1)} %get-tuple-element.404), channel_id=1, source_target_pairs={{224,240},{208,224},{192,208},{176,192},{225,241},{209,225},{193,2... | collective-permute-start | bytes 196616 | tf_op jit(solution)/shard_map/ppermute | solution.py:455
  203.9 64.3 %collective-permute-start.50 = (bf16[32,1024]{1,0:T(8,128)(2,1)S(1)}, bf16[32,1024]{1,0:T(8,128)(2,1)S(1)}, u32[]{:S(2)}, u32[]{:S(2)}) collective-permute-start(bf16[32,1024]{1,0:T(8,128)(2,1)S(1)} %get-tuple-element.437), channel_id=1, source_target_pairs={{192,208},{176,192},{160,176},{144,160},{193,209},{177,193},{161,1... | collective-permute-start | bytes 196616 | tf_op jit(solution)/shard_map/ppermute | solution.py:455
  255.1 13.1 %collective-permute-start.51 = (bf16[32,1024]{1,0:T(8,128)(2,1)S(1)}, bf16[32,1024]{1,0:T(8,128)(2,1)S(1)}, u32[]{:S(2)}, u32[]{:S(2)}) collective-permute-start(bf16[32,1024]{1,0:T(8,128)(2,1)S(1)} %get-tuple-element.438), channel_id=1, source_target_pairs={{192,176},{208,192},{224,208},{240,224},{193,177},{209,193},{225,2... | collective-permute-start | bytes 196616 | tf_op jit(solution)/shard_map/ppermute | solution.py:455
  268.3 34.4 %collective-permute-start.52 = (bf16[32,1024]{1,0:T(8,128)(2,1)S(1)}, bf16[32,1024]{1,0:T(8,128)(2,1)S(1)}, u32[]{:S(2)}, u32[]{:S(2)}) collective-permute-start(bf16[32,1024]{1,0:T(8,128)(2,1)S(1)} %get-tuple-element.444), channel_id=1, source_target_pairs={{208,224},{192,208},{176,192},{160,176},{209,225},{193,209},{177,1... | collective-permute-start | bytes 196616 | tf_op jit(solution)/shard_map/ppermute | solution.py:455
  289.6 13.1 %collective-permute-start.53 = (bf16[32,1024]{1,0:T(8,128)(2,1)S(1)}, bf16[32,1024]{1,0:T(8,128)(2,1)S(1)}, u32[]{:S(2)}, u32[]{:S(2)}) collective-permute-start(bf16[32,1024]{1,0:T(8,128)(2,1)S(1)} %get-tuple-element.445), channel_id=1, source_target_pairs={{176,160},{192,176},{208,192},{224,208},{177,161},{193,177},{209,1... | collective-permute-start | bytes 196616 | tf_op jit(solution)/shard_map/ppermute | solution.py:455
  302.8 34.1 %collective-permute-start.54 = (bf16[32,1024]{1,0:T(8,128)(2,1)S(1)}, bf16[32,1024]{1,0:T(8,128)(2,1)S(1)}, u32[]{:S(2)}, u32[]{:S(2)}) collective-permute-start(bf16[32,1024]{1,0:T(8,128)(2,1)S(1)} %get-tuple-element.451), channel_id=1, source_target_pairs={{224,240},{208,224},{192,208},{176,192},{225,241},{209,225},{193,2... | collective-permute-start | bytes 196616 | tf_op jit(solution)/shard_map/ppermute | solution.py:455
  324.0 12.9 %collective-permute-start.55 = (bf16[32,1024]{1,0:T(8,128)(2,1)S(1)}, bf16[32,1024]{1,0:T(8,128)(2,1)S(1)}, u32[]{:S(2)}, u32[]{:S(2)}) collective-permute-start(bf16[32,1024]{1,0:T(8,128)(2,1)S(1)} %get-tuple-element.452), channel_id=1, source_target_pairs={{160,144},{176,160},{192,176},{208,192},{161,145},{177,161},{193,1... | collective-permute-start | bytes 196616 | tf_op jit(solution)/shard_map/ppermute | solution.py:455
  351.2 51.4 %collective-permute-start.67 = (bf16[32,1024]{1,0:T(8,128)(2,1)S(1)}, bf16[32,1024]{1,0:T(8,128)(2,1)S(1)}, u32[]{:S(2)}, u32[]{:S(2)}) collective-permute-start(bf16[32,1024]{1,0:T(8,128)(2,1)S(1)} %get-tuple-element.485), channel_id=1, source_target_pairs={{80,64},{96,80},{112,96},{128,112},{81,65},{97,81},{113,97},{129,1... | collective-permute-start | bytes 196616 | tf_op jit(solution)/shard_map/ppermute | solution.py:455
  351.9 50.8 %collective-permute-start.66 = (bf16[32,1024]{1,0:T(8,128)(2,1)S(1)}, bf16[32,1024]{1,0:T(8,128)(2,1)S(1)}, u32[]{:S(2)}, u32[]{:S(2)}) collective-permute-start(bf16[32,1024]{1,0:T(8,128)(2,1)S(1)} %get-tuple-element.485), channel_id=1, source_target_pairs={{192,176},{208,192},{224,208},{240,224},{193,177},{209,193},{225,2... | collective-permute-start | bytes 196616 | tf_op jit(solution)/shard_map/ppermute | solution.py:455
  403.7 20.0 %collective-permute-start.69 = (bf16[32,1024]{1,0:T(8,128)(2,1)S(1)}, bf16[32,1024]{1,0:T(8,128)(2,1)S(1)}, u32[]{:S(2)}, u32[]{:S(2)}) collective-permute-start(bf16[32,1024]{1,0:T(8,128)(2,1)S(1)} %get-tuple-element.491), channel_id=1, source_target_pairs={{64,48},{80,64},{96,80},{112,96},{65,49},{81,65},{97,81},{113,97},... | collective-permute-start | bytes 196616 | tf_op jit(solution)/shard_map/ppermute | solution.py:455
  404.4 19.3 %collective-permute-start.68 = (bf16[32,1024]{1,0:T(8,128)(2,1)S(1)}, bf16[32,1024]{1,0:T(8,128)(2,1)S(1)}, u32[]{:S(2)}, u32[]{:S(2)}) collective-permute-start(bf16[32,1024]{1,0:T(8,128)(2,1)S(1)} %get-tuple-element.491), channel_id=1, source_target_pairs={{176,160},{192,176},{208,192},{224,208},{177,161},{193,177},{209,1... | collective-permute-start | bytes 196616 | tf_op jit(solution)/shard_map/ppermute | solution.py:455
  424.3 20.2 %collective-permute-start.71 = (bf16[32,1024]{1,0:T(8,128)(2,1)S(1)}, bf16[32,1024]{1,0:T(8,128)(2,1)S(1)}, u32[]{:S(2)}, u32[]{:S(2)}) collective-permute-start(bf16[32,1024]{1,0:T(8,128)(2,1)S(1)} %get-tuple-element.497), channel_id=1, source_target_pairs={{48,32},{64,48},{80,64},{96,80},{49,33},{65,49},{81,65},{97,81},{5... | collective-permute-start | bytes 196616 | tf_op jit(solution)/shard_map/ppermute | solution.py:455
  425.0 19.5 %collective-permute-start.70 = (bf16[32,1024]{1,0:T(8,128)(2,1)S(1)}, bf16[32,1024]{1,0:T(8,128)(2,1)S(1)}, u32[]{:S(2)}, u32[]{:S(2)}) collective-permute-start(bf16[32,1024]{1,0:T(8,128)(2,1)S(1)} %get-tuple-element.497), channel_id=1, source_target_pairs={{160,144},{176,160},{192,176},{208,192},{161,145},{177,161},{193,1... | collective-permute-start | bytes 196616 | tf_op jit(solution)/shard_map/ppermute | solution.py:455
  447.4 15.6 %collective-permute-start.75 = (bf16[32,1024]{1,0:T(8,128)(2,1)S(1)}, bf16[32,1024]{1,0:T(8,128)(2,1)S(1)}, u32[]{:S(2)}, u32[]{:S(2)}) collective-permute-start(bf16[32,1024]{1,0:T(8,128)(2,1)S(1)} %get-tuple-element.509), channel_id=1, source_target_pairs={{16,0},{32,16},{48,32},{64,48},{17,1},{33,17},{49,33},{65,49},{18,... | collective-permute-start | bytes 196616 | tf_op jit(solution)/shard_map/ppermute | solution.py:455
  448.7 14.3 %collective-permute-start.74 = (bf16[32,1024]{1,0:T(8,128)(2,1)S(1)}, bf16[32,1024]{1,0:T(8,128)(2,1)S(1)}, u32[]{:S(2)}, u32[]{:S(2)}) collective-permute-start(bf16[32,1024]{1,0:T(8,128)(2,1)S(1)} %get-tuple-element.509), channel_id=1, source_target_pairs={{128,112},{144,128},{160,144},{176,160},{129,113},{145,129},{161,1... | collective-permute-start | bytes 196616 | tf_op jit(solution)/shard_map/ppermute | solution.py:455
  476.0 7.3 %collective-permute-start.79 = (bf16[32,1024]{1,0:T(8,128)(2,1)S(1)}, bf16[32,1024]{1,0:T(8,128)(2,1)S(1)}, u32[]{:S(2)}, u32[]{:S(2)}) collective-permute-start(bf16[32,1024]{1,0:T(8,128)(2,1)S(1)} %get-tuple-element.521), channel_id=1, source_target_pairs={{16,0},{32,16},{17,1},{33,17},{18,2},{34,18},{19,3},{35,19},{20,4}... | collective-permute-start | bytes 196616 | tf_op jit(solution)/shard_map/ppermute | solution.py:455
  486.9 6.4 %collective-permute-start.81 = (bf16[32,1024]{1,0:T(8,128)(2,1)S(1)}, bf16[32,1024]{1,0:T(8,128)(2,1)S(1)}, u32[]{:S(2)}, u32[]{:S(2)}) collective-permute-start(bf16[32,1024]{1,0:T(8,128)(2,1)S(1)} %get-tuple-element.527), channel_id=1, source_target_pairs={{16,0},{17,1},{18,2},{19,3},{20,4},{21,5},{22,6},{23,7},{24,8},{25... | collective-permute-start | bytes 196616 | tf_op jit(solution)/shard_map/ppermute | solution.py:455
  503.3 31.4 %collective-permute-start.85 = (bf16[32,1024]{1,0:T(8,128)(2,1)S(1)}, bf16[32,1024]{1,0:T(8,128)(2,1)S(1)}, u32[]{:S(2)}, u32[]{:S(2)}) collective-permute-start(bf16[32,1024]{1,0:T(8,128)(2,1)S(1)} %get-tuple-element.551), channel_id=1, source_target_pairs={{16,0},{32,16},{48,32},{64,48},{17,1},{33,17},{49,33},{65,49},{18,... | collective-permute-start | bytes 196616 | tf_op jit(solution)/shard_map/ppermute | solution.py:455
  538.1 8.3 %collective-permute-start.86 = (bf16[32,1024]{1,0:T(8,128)(2,1)S(1)}, bf16[32,1024]{1,0:T(8,128)(2,1)S(1)}, u32[]{:S(2)}, u32[]{:S(2)}) collective-permute-start(bf16[32,1024]{1,0:T(8,128)(2,1)S(1)} %get-tuple-element.557), channel_id=1, source_target_pairs={{16,0},{32,16},{48,32},{17,1},{33,17},{49,33},{18,2},{34,18},{50,3... | collective-permute-start | bytes 196616 | tf_op jit(solution)/shard_map/ppermute | solution.py:455
  549.9 8.9 %collective-permute-start.87 = (bf16[32,1024]{1,0:T(8,128)(2,1)S(1)}, bf16[32,1024]{1,0:T(8,128)(2,1)S(1)}, u32[]{:S(2)}, u32[]{:S(2)}) collective-permute-start(bf16[32,1024]{1,0:T(8,128)(2,1)S(1)} %get-tuple-element.563), channel_id=1, source_target_pairs={{16,0},{32,16},{17,1},{33,17},{18,2},{34,18},{19,3},{35,19},{20,4}... | collective-permute-start | bytes 196616 | tf_op jit(solution)/shard_map/ppermute | solution.py:455
  577.9 15.2 %collective-permute-start.90 = (bf16[2,64,4096]{2,1,0:T(8,128)(2,1)S(1)}, bf16[2,64,4096]{2,1,0:T(8,128)(2,1)S(1)}, u32[]{:S(2)}, u32[]{:S(2)}) collective-permute-start(bf16[2,64,4096]{2,1,0:T(8,128)(2,1)S(1)} %get-tuple-element.575), channel_id=1, source_target_pairs={{0,1},{1,0},{2,3},{3,2},{4,5},{5,4},{6,7},{7,6},{8,9},{9,8},{10,11... | collective-permute-start | bytes 3145736 | tf_op jit(solution)/shard_map/ppermute | solution.py:379
  578.5 30.7 %collective-permute-start.89 = (bf16[3,64,4096]{2,1,0:T(8,128)(2,1)S(1)}, bf16[3,64,4096]{2,1,0:T(8,128)(2,1)S(1)}, u32[]{:S(2)}, u32[]{:S(2)}) collective-permute-start(bf16[3,64,4096]{2,1,0:T(8,128)(2,1)S(1)} %get-tuple-element.573), channel_id=1, source_target_pairs={{0,1},{1,0},{2,3},{3,2},{4,5},{5,4},{6,7},{7,6},{8,9},{9,8},{10,11... | collective-permute-start | bytes 4718600 | tf_op jit(solution)/shard_map/ppermute | solution.py:379
  580.0 8.4 %collective-permute-start.93 = (bf16[64,2048]{1,0:T(8,128)(2,1)S(1)}, bf16[64,2048]{1,0:T(8,128)(2,1)S(1)}, u32[]{:S(2)}, u32[]{:S(2)}) collective-permute-start(bf16[64,2048]{1,0:T(8,128)(2,1)S(1)} %get-tuple-element.588), channel_id=1, source_target_pairs={{0,2},{1,3},{2,4},{3,5},{4,6},{5,7},{6,8},{7,9},{8,10},{9,11},{10,... | collective-permute-start | bytes 786440 | tf_op jit(solution)/shard_map/ppermute | solution.py:382
  581.8 8.1 %collective-permute-start.97 = (bf16[64,2048]{1,0:T(8,128)(2,1)S(1)}, bf16[64,2048]{1,0:T(8,128)(2,1)S(1)}, u32[]{:S(2)}, u32[]{:S(2)}) collective-permute-start(bf16[64,2048]{1,0:T(8,128)(2,1)S(1)} %get-tuple-element.589), channel_id=1, source_target_pairs={{0,14},{1,15},{2,0},{3,1},{4,2},{5,3},{6,4},{7,5},{8,6},{9,7},{10,... | collective-permute-start | bytes 786440 | tf_op jit(solution)/shard_map/ppermute | solution.py:383
  590.1 13.7 %collective-permute-start.94 = (bf16[64,4096]{1,0:T(8,128)(2,1)S(1)}, bf16[64,4096]{1,0:T(8,128)(2,1)S(1)}, u32[]{:S(2)}, u32[]{:S(2)}) collective-permute-start(bf16[64,4096]{1,0:T(8,128)(2,1)S(1)} %get-tuple-element.584), channel_id=1, source_target_pairs={{0,2},{1,3},{2,4},{3,5},{4,6},{5,7},{6,8},{7,9},{8,10},{9,11},{10,... | collective-permute-start | bytes 1572872 | tf_op jit(solution)/shard_map/ppermute | solution.py:389
  593.1 13.7 %collective-permute-start.98 = (bf16[64,4096]{1,0:T(8,128)(2,1)S(1)}, bf16[64,4096]{1,0:T(8,128)(2,1)S(1)}, u32[]{:S(2)}, u32[]{:S(2)}) collective-permute-start(bf16[64,4096]{1,0:T(8,128)(2,1)S(1)} %get-tuple-element.585), channel_id=1, source_target_pairs={{0,14},{1,15},{2,0},{3,1},{4,2},{5,3},{6,4},{7,5},{8,6},{9,7},{10,... | collective-permute-start | bytes 1572872 | tf_op jit(solution)/shard_map/ppermute | solution.py:390
  607.1 12.0 %collective-permute-start.95 = (bf16[64,4096]{1,0:T(8,128)(2,1)S(1)}, bf16[64,4096]{1,0:T(8,128)(2,1)S(1)}, u32[]{:S(2)}, u32[]{:S(2)}) collective-permute-start(bf16[64,4096]{1,0:T(8,128)(2,1)S(1)} %get-tuple-element.582), channel_id=1, source_target_pairs={{0,2},{1,3},{2,4},{3,5},{4,6},{5,7},{6,8},{7,9},{8,10},{9,11},{10,... | collective-permute-start | bytes 1572872 | tf_op jit(solution)/shard_map/ppermute | solution.py:389
  608.9 11.7 %collective-permute-start.99 = (bf16[64,4096]{1,0:T(8,128)(2,1)S(1)}, bf16[64,4096]{1,0:T(8,128)(2,1)S(1)}, u32[]{:S(2)}, u32[]{:S(2)}) collective-permute-start(bf16[64,4096]{1,0:T(8,128)(2,1)S(1)} %get-tuple-element.583), channel_id=1, source_target_pairs={{0,14},{1,15},{2,0},{3,1},{4,2},{5,3},{6,4},{7,5},{8,6},{9,7},{10,... | collective-permute-start | bytes 1572872 | tf_op jit(solution)/shard_map/ppermute | solution.py:390
  620.9 10.9 %collective-permute-start.96 = (bf16[64,4096]{1,0:T(8,128)(2,1)S(1)}, bf16[64,4096]{1,0:T(8,128)(2,1)S(1)}, u32[]{:S(2)}, u32[]{:S(2)}) collective-permute-start(bf16[64,4096]{1,0:T(8,128)(2,1)S(1)} %get-tuple-element.580), channel_id=1, source_target_pairs={{0,2},{1,3},{2,4},{3,5},{4,6},{5,7},{6,8},{7,9},{8,10},{9,11},{10,... | collective-permute-start | bytes 1572872 | tf_op jit(solution)/shard_map/ppermute | solution.py:394
  622.7 10.8 %collective-permute-start.100 = (bf16[64,4096]{1,0:T(8,128)(2,1)S(1)}, bf16[64,4096]{1,0:T(8,128)(2,1)S(1)}, u32[]{:S(2)}, u32[]{:S(2)}) collective-permute-start(bf16[64,4096]{1,0:T(8,128)(2,1)S(1)} %get-tuple-element.581), channel_id=1, source_target_pairs={{0,14},{1,15},{2,0},{3,1},{4,2},{5,3},{6,4},{7,5},{8,6},{9,7},{10,... | collective-permute-start | bytes 1572872 | tf_op jit(solution)/shard_map/ppermute | solution.py:395
  (55 other events, 183.3 us)

commit v3 on v2

--- a/solution.py
+++ b/solution.py
@@ -125,6 +125,7 @@
 
     def waves(self, t):
         found = {}
+        count = min(self.pieces, self.layers - 1)
         for name, stages, way in (
             ("tan_up", self.forward_tan(t), 1),
             ("tan_down", self.backward_tan(t), -1),
@@ -132,7 +133,12 @@
             ("down", self.backward(t), -1),
         ):
             if stages:
-                found[name] = [(s, s + way) for s in stages if 0 <= s + way < self.layers]
+                useful = [(s, s + way) for s in stages if 0 <= s + way < self.layers]
+                lowest = min([min(e) for e in useful], default=0)
+                lowest = min(lowest, self.layers - 1 - count)
+                pairs = [(s, s + 1) for s in range(lowest, lowest + count)] if useful else []
+                found[name] = pairs if way > 0 else [(r, s) for s, r in pairs]
+                assert set(useful) <= set(found[name])
         return found
 
 
@@ -432,7 +438,7 @@
     probes = None
     got = {"up": nothing}
     packet = pltpu.VMEM((rows, width), bf16)
-    ring_ticks = {0: 1, 2: 2, 3: 3, 4: 4}
+    ring_ticks = {0: 1, 1: 2, 2: 3, 3: 4}
     for t in range(plan.ticks):
         if t == LAG - 1:
             probes = assemble(blocks, halves, groups, part, hidden)

time: 645 us -> 534 us (0.83)
  the two profiles are of different devices: /device:TPU:32 before, /device:TPU:6 now
where the time goes in v3:
time: 534 us; the launch traced here: 524 us
  waiting for transfers between devices  261 us (49%)
  starting transfers between devices  165 us (31%)
  Pallas kernels  90.8 us (17%)
    ppermute x72, waiting for transfers between devices, on_device(): lax.ppermute(sent[name.removeprefix('tan_')], 'pipe', edges)  213 us
    ppermute x72, starting transfers between devices, on_device(): lax.ppermute(sent[name.removeprefix('tan_')], 'pipe', edges)  134 us
    pallas_call x42, Pallas kernels, on_device(): pl.pallas_call(functools.partial(tick_kernel, plan, t, with_probes, loss_...  80.5 us
    ppermute x3, waiting for transfers between devices, scatter(): from_behind = lax.ppermute(up, 'dp', ahead)  30.6 us
    ppermute x4, starting transfers between devices, ring(): lax.ppermute(both[1], 'dp', behind)  15.4 us
  transfers between devices with their start and end apart: 101, of which 37 were waited for; matrix products, arithmetic and copies ran while one was open for 0% of the time, Pallas kernels for 3%

profile of v3, /device:TPU:6, one launch (start us, length us, event | category | flops | bytes accessed | tf_op | source)
XLA Modules:
  0.0 524.2 jit_solution(11197291990777963363)
XLA Ops:
  2.6 5.9 %collective-permute-start.2 = (bf16[2,64,2048]{2,1,0:T(8,128)(2,1)S(1)}, bf16[2,64,2048]{2,1,0:T(8,128)(2,1)S(1)}, u32[]{:S(2)}, u32[]{:S(2)}) collective-permute-start(bf16[2,64,2048]{2,1,0:T(8,128)(2,1)S(1)} %constant_dynamic-update-slice_fusion.refs_0_), channel_id=1, source_target_pairs={{0,14},{1,15},{2,0},{3,1},{4,2},{5,3},{6,4},{7,5},{8,6},{9,7},{10,... | collective-permute-start | bytes 1572872 | tf_op jit(solution)/shard_map/ppermute | solution.py:420
  8.5 3.5 load.1
  12.7 3.4 collective-permute-start
  19.7 3.4 collective-permute-done.1.refs_2_
  27.0 3.4 collective-permute-start.3
  33.1 3.7 collective-permute-done.4.refs_6_
  57.5 4.2 collective-permute-done.9.refs_9_
  65.1 4.0 collective-permute-start.12
  74.1 6.1 %collective-permute-start.22 = (bf16[32,1024]{1,0:T(8,128)(2,1)S(1)}, bf16[32,1024]{1,0:T(8,128)(2,1)S(1)}, u32[]{:S(2)}, u32[]{:S(2)}) collective-permute-start(bf16[32,1024]{1,0:T(8,128)(2,1)S(1)} %get-tuple-element.350), channel_id=1, source_target_pairs={{32,48},{48,64},{64,80},{80,96},{33,49},{49,65},{65,81},{81,97},{3... | collective-permute-start | bytes 196616 | tf_op jit(solution)/shard_map/ppermute | solution.py:461
  85.0 6.5 %collective-permute-start.23 = (bf16[32,1024]{1,0:T(8,128)(2,1)S(1)}, bf16[32,1024]{1,0:T(8,128)(2,1)S(1)}, u32[]{:S(2)}, u32[]{:S(2)}) collective-permute-start(bf16[32,1024]{1,0:T(8,128)(2,1)S(1)} %get-tuple-element.356), channel_id=1, source_target_pairs={{48,64},{64,80},{80,96},{96,112},{49,65},{65,81},{81,97},{97,113},... | collective-permute-start | bytes 196616 | tf_op jit(solution)/shard_map/ppermute | solution.py:461
  95.0 9.1 %collective-permute-start.24 = (bf16[32,1024]{1,0:T(8,128)(2,1)S(1)}, bf16[32,1024]{1,0:T(8,128)(2,1)S(1)}, u32[]{:S(2)}, u32[]{:S(2)}) collective-permute-start(bf16[32,1024]{1,0:T(8,128)(2,1)S(1)} %get-tuple-element.362), channel_id=1, source_target_pairs={{0,16},{16,32},{32,48},{48,64},{1,17},{17,33},{33,49},{49,65},{2,1... | collective-permute-start | bytes 196616 | tf_op jit(solution)/shard_map/ppermute | solution.py:461
  107.4 6.4 %collective-permute-start.26 = (bf16[32,1024]{1,0:T(8,128)(2,1)S(1)}, bf16[32,1024]{1,0:T(8,128)(2,1)S(1)}, u32[]{:S(2)}, u32[]{:S(2)}) collective-permute-start(bf16[32,1024]{1,0:T(8,128)(2,1)S(1)} %get-tuple-element.368), channel_id=1, source_target_pairs={{0,16},{16,32},{32,48},{48,64},{1,17},{17,33},{33,49},{49,65},{2,1... | collective-permute-start | bytes 196616 | tf_op jit(solution)/shard_map/ppermute | solution.py:461
  119.0 4.3 collective-permute-start.28
  128.7 6.4 %collective-permute-start.30 = (bf16[32,1024]{1,0:T(8,128)(2,1)S(1)}, bf16[32,1024]{1,0:T(8,128)(2,1)S(1)}, u32[]{:S(2)}, u32[]{:S(2)}) collective-permute-start(bf16[32,1024]{1,0:T(8,128)(2,1)S(1)} %get-tuple-element.380), channel_id=1, source_target_pairs={{0,16},{16,32},{32,48},{48,64},{1,17},{17,33},{33,49},{49,65},{2,1... | collective-permute-start | bytes 196616 | tf_op jit(solution)/shard_map/ppermute | solution.py:461
  140.3 6.4 %collective-permute-start.32 = (bf16[32,1024]{1,0:T(8,128)(2,1)S(1)}, bf16[32,1024]{1,0:T(8,128)(2,1)S(1)}, u32[]{:S(2)}, u32[]{:S(2)}) collective-permute-start(bf16[32,1024]{1,0:T(8,128)(2,1)S(1)} %get-tuple-element.386), channel_id=1, source_target_pairs={{16,32},{32,48},{48,64},{64,80},{17,33},{33,49},{49,65},{65,81},{1... | collective-permute-start | bytes 196616 | tf_op jit(solution)/shard_map/ppermute | solution.py:461
  151.9 6.4 %collective-permute-start.34 = (bf16[32,1024]{1,0:T(8,128)(2,1)S(1)}, bf16[32,1024]{1,0:T(8,128)(2,1)S(1)}, u32[]{:S(2)}, u32[]{:S(2)}) collective-permute-start(bf16[32,1024]{1,0:T(8,128)(2,1)S(1)} %get-tuple-element.392), channel_id=1, source_target_pairs={{32,48},{48,64},{64,80},{80,96},{33,49},{49,65},{65,81},{81,97},{3... | collective-permute-start | bytes 196616 | tf_op jit(solution)/shard_map/ppermute | solution.py:461
  163.9 6.4 %collective-permute-start.36 = (bf16[32,1024]{1,0:T(8,128)(2,1)S(1)}, bf16[32,1024]{1,0:T(8,128)(2,1)S(1)}, u32[]{:S(2)}, u32[]{:S(2)}) collective-permute-start(bf16[32,1024]{1,0:T(8,128)(2,1)S(1)} %get-tuple-element.398), channel_id=1, source_target_pairs={{48,64},{64,80},{80,96},{96,112},{49,65},{65,81},{81,97},{97,113},... | collective-permute-start | bytes 196616 | tf_op jit(solution)/shard_map/ppermute | solution.py:461
  181.2 4.6 collective-permute-start.49
  190.0 4.6 tick.64
  198.1 5.9 %tick.66 = (bf16[4,128,1024]{2,1,0:T(8,128)(2,1)S(1)}, bf16[4,128,2048]{2,1,0:T(8,128)(2,1)S(1)}, f32[6,128,1024]{2,1,0:T(8,128)S(1)}, f32[6,128,2048]{2,1,0:T(8...) custom-call(bf16[4,128,1024]{2,1,0:T(8,128)(2,1)S(1)} %get-tuple-ele, ...), custom_call_target="tpu_custom_call", output_to_operand_aliasing={{0}: (0, {}), {1}: (1, {}), {2}: (2, {}), {3}: (3, {}), {4}... | custom-call | flops 1073741824 | bytes 8388608 | tf_op jit(solution)/shard_map/tick/pallas_call | solution.py:449
  210.1 3.8 tick.69
  215.9 89.8 %collective-permute-done.69.refs_12_ = bf16[32,1024]{1,0:T(8,128)(2,1)S(1)} collective-permute-done((bf16[32,1024]{1,0:T(8,128)(2,1)S(1)}, bf16[32,1024]{1,0:T(8,128)(2,1)S(1)}, u32[]{:S(2)}, u32[]{:S(2)}) %collective-permute-start.69) | collective-permute-done | bytes 65568 | tf_op jit(solution)/shard_map/ppermute | solution.py:461
  305.7 3.4 tick.70
  311.7 6.6 %collective-permute-done.71.refs_12_ = bf16[32,1024]{1,0:T(8,128)(2,1)S(1)} collective-permute-done((bf16[32,1024]{1,0:T(8,128)(2,1)S(1)}, bf16[32,1024]{1,0:T(8,128)(2,1)S(1)}, u32[]{:S(2)}, u32[]{:S(2)}) %collective-permute-start.71) | collective-permute-done | bytes 65568 | tf_op jit(solution)/shard_map/ppermute | solution.py:461
  318.3 3.4 tick.71
  324.3 8.6 %collective-permute-done.73.refs_12_ = bf16[32,1024]{1,0:T(8,128)(2,1)S(1)} collective-permute-done((bf16[32,1024]{1,0:T(8,128)(2,1)S(1)}, bf16[32,1024]{1,0:T(8,128)(2,1)S(1)}, u32[]{:S(2)}, u32[]{:S(2)}) %collective-permute-start.73) | collective-permute-done | bytes 65568 | tf_op jit(solution)/shard_map/ppermute | solution.py:461
  332.9 3.8 tick.72
  339.3 5.7 %collective-permute-done.75.refs_12_ = bf16[32,1024]{1,0:T(8,128)(2,1)S(1)} collective-permute-done((bf16[32,1024]{1,0:T(8,128)(2,1)S(1)}, bf16[32,1024]{1,0:T(8,128)(2,1)S(1)}, u32[]{:S(2)}, u32[]{:S(2)}) %collective-permute-start.75) | collective-permute-done | bytes 65568 | tf_op jit(solution)/shard_map/ppermute | solution.py:461
  345.0 3.4 tick.73
  351.0 5.7 %collective-permute-done.77.refs_12_ = bf16[32,1024]{1,0:T(8,128)(2,1)S(1)} collective-permute-done((bf16[32,1024]{1,0:T(8,128)(2,1)S(1)}, bf16[32,1024]{1,0:T(8,128)(2,1)S(1)}, u32[]{:S(2)}, u32[]{:S(2)}) %collective-permute-start.77) | collective-permute-done | bytes 65568 | tf_op jit(solution)/shard_map/ppermute | solution.py:461
  360.6 5.0 collective-permute-done.79.refs_12_
  369.0 5.7 %collective-permute-done.81.refs_12_ = bf16[32,1024]{1,0:T(8,128)(2,1)S(1)} collective-permute-done((bf16[32,1024]{1,0:T(8,128)(2,1)S(1)}, bf16[32,1024]{1,0:T(8,128)(2,1)S(1)}, u32[]{:S(2)}, u32[]{:S(2)}) %collective-permute-start.81) | collective-permute-done | bytes 65568 | tf_op jit(solution)/shard_map/ppermute | solution.py:461
  378.7 18.2 %collective-permute-done.82.refs_11_ = bf16[32,1024]{1,0:T(8,128)(2,1)S(1)} collective-permute-done((bf16[32,1024]{1,0:T(8,128)(2,1)S(1)}, bf16[32,1024]{1,0:T(8,128)(2,1)S(1)}, u32[]{:S(2)}, u32[]{:S(2)}) %collective-permute-start.82) | collective-permute-done | bytes 65568 | tf_op jit(solution)/shard_map/ppermute | solution.py:461
  396.9 3.5 tick.77
  402.3 6.3 %collective-permute-done.83.refs_11_ = bf16[32,1024]{1,0:T(8,128)(2,1)S(1)} collective-permute-done((bf16[32,1024]{1,0:T(8,128)(2,1)S(1)}, bf16[32,1024]{1,0:T(8,128)(2,1)S(1)}, u32[]{:S(2)}, u32[]{:S(2)}) %collective-permute-start.83) | collective-permute-done | bytes 65568 | tf_op jit(solution)/shard_map/ppermute | solution.py:461
  408.6 3.9 tick.78
  414.4 6.3 %collective-permute-done.84.refs_11_ = bf16[32,1024]{1,0:T(8,128)(2,1)S(1)} collective-permute-done((bf16[32,1024]{1,0:T(8,128)(2,1)S(1)}, bf16[32,1024]{1,0:T(8,128)(2,1)S(1)}, u32[]{:S(2)}, u32[]{:S(2)}) %collective-permute-start.84) | collective-permute-done | bytes 65568 | tf_op jit(solution)/shard_map/ppermute | solution.py:461
  420.8 3.5 tick.79
  426.2 6.3 %collective-permute-done.85.refs_9_ = bf16[32,1024]{1,0:T(8,128)(2,1)S(1)} collective-permute-done((bf16[32,1024]{1,0:T(8,128)(2,1)S(1)}, bf16[32,1024]{1,0:T(8,128)(2,1)S(1)}, u32[]{:S(2)}, u32[]{:S(2)}) %collective-permute-start.85) | collective-permute-done | bytes 65568 | tf_op jit(solution)/shard_map/ppermute | solution.py:461
  432.5 3.5 tick.80
  437.9 6.3 %collective-permute-done.86.refs_9_ = bf16[32,1024]{1,0:T(8,128)(2,1)S(1)} collective-permute-done((bf16[32,1024]{1,0:T(8,128)(2,1)S(1)}, bf16[32,1024]{1,0:T(8,128)(2,1)S(1)}, u32[]{:S(2)}, u32[]{:S(2)}) %collective-permute-start.86) | collective-permute-done | bytes 65568 | tf_op jit(solution)/shard_map/ppermute | solution.py:461
  447.6 5.6 %collective-permute-done.87.refs_9_ = bf16[32,1024]{1,0:T(8,128)(2,1)S(1)} collective-permute-done((bf16[32,1024]{1,0:T(8,128)(2,1)S(1)}, bf16[32,1024]{1,0:T(8,128)(2,1)S(1)}, u32[]{:S(2)}, u32[]{:S(2)}) %collective-permute-start.87) | collective-permute-done | bytes 65568 | tf_op jit(solution)/shard_map/ppermute | solution.py:461
  455.7 6.3 %collective-permute-done.88.refs_9_ = bf16[32,1024]{1,0:T(8,128)(2,1)S(1)} collective-permute-done((bf16[32,1024]{1,0:T(8,128)(2,1)S(1)}, bf16[32,1024]{1,0:T(8,128)(2,1)S(1)}, u32[]{:S(2)}, u32[]{:S(2)}) %collective-permute-start.88) | collective-permute-done | bytes 65568 | tf_op jit(solution)/shard_map/ppermute | solution.py:461
  462.9 5.7 %curvature.1 = (bf16[1,64,4096]{2,1,0:T(8,128)(2,1)S(1)}, bf16[2,64,4096]{2,1,0:T(8,128)(2,1)S(1)}, bf16[2,64,4096]{2,1,0:T(8,128)(2,1)S(1)}, bf16[3,64,4096]{2,...) custom-call(bf16[4,128,1024]{2,1,0:T(8,128)(2,1)S(1)} %get-tuple-ele, ...), custom_call_target="tpu_custom_call" | custom-call | tf_op jit(solution)/shard_map/curvature/pallas_call | solution.py:328
  474.4 6.2 %collective-permute-done.93 = bf16[64,2048]{1,0:T(8,128)(2,1)S(1)} collective-permute-done((bf16[64,2048]{1,0:T(8,128)(2,1)S(1)}, bf16[64,2048]{1,0:T(8,128)(2,1)S(1)}, u32[]{:S(2)}, u32[]{:S(2)}) %collective-permute-start.93) | collective-permute-done | bytes 262176 | tf_op jit(solution)/shard_map/ppermute | solution.py:388
  484.4 11.1 %collective-permute-done.94 = bf16[64,4096]{1,0:T(8,128)(2,1)S(1)} collective-permute-done((bf16[64,4096]{1,0:T(8,128)(2,1)S(1)}, bf16[64,4096]{1,0:T(8,128)(2,1)S(1)}, u32[]{:S(2)}, u32[]{:S(2)}) %collective-permute-start.94) | collective-permute-done | bytes 524320 | tf_op jit(solution)/shard_map/ppermute | solution.py:395
  499.6 10.0 %collective-permute-done.95 = bf16[64,4096]{1,0:T(8,128)(2,1)S(1)} collective-permute-done((bf16[64,4096]{1,0:T(8,128)(2,1)S(1)}, bf16[64,4096]{1,0:T(8,128)(2,1)S(1)}, u32[]{:S(2)}, u32[]{:S(2)}) %collective-permute-start.95) | collective-permute-done | bytes 524320 | tf_op jit(solution)/shard_map/ppermute | solution.py:395
  513.2 9.5 %collective-permute-done.96 = bf16[64,4096]{1,0:T(8,128)(2,1)S(1)} collective-permute-done((bf16[64,4096]{1,0:T(8,128)(2,1)S(1)}, bf16[64,4096]{1,0:T(8,128)(2,1)S(1)}, u32[]{:S(2)}, u32[]{:S(2)}) %collective-permute-start.96) | collective-permute-done | bytes 524320 | tf_op jit(solution)/shard_map/ppermute | solution.py:400
  (218 shorter events, 160.1 us)
Async XLA Ops:
  2.6 17.1 %collective-permute-start.2 = (bf16[2,64,2048]{2,1,0:T(8,128)(2,1)S(1)}, bf16[2,64,2048]{2,1,0:T(8,128)(2,1)S(1)}, u32[]{:S(2)}, u32[]{:S(2)}) collective-permute-start(bf16[2,64,2048]{2,1,0:T(8,128)(2,1)S(1)} %constant_dynamic-update-slice_fusion.refs_0_), channel_id=1, source_target_pairs={{0,14},{1,15},{2,0},{3,1},{4,2},{5,3},{6,4},{7,5},{8,6},{9,7},{10,... | collective-permute-start | bytes 1572872 | tf_op jit(solution)/shard_map/ppermute | solution.py:420
  8.5 14.6 %collective-permute-start.1 = (bf16[2,64,2048]{2,1,0:T(8,128)(2,1)S(1)}, bf16[2,64,2048]{2,1,0:T(8,128)(2,1)S(1)}, u32[]{:S(2)}, u32[]{:S(2)}) collective-permute-start(bf16[2,64,2048]{2,1,0:T(8,128)(2,1)S(1)} %constant_dynamic-update-slice_fusion.refs_0_), channel_id=1, source_target_pairs={{0,2},{1,3},{2,4},{3,5},{4,6},{5,7},{6,8},{7,9},{8,10},{9,11},{10,... | collective-permute-start | bytes 1572872 | tf_op jit(solution)/shard_map/ppermute | solution.py:420
  23.1 13.7 %collective-permute-start.4 = (bf16[2,64,2048]{2,1,0:T(8,128)(2,1)S(1)}, bf16[2,64,2048]{2,1,0:T(8,128)(2,1)S(1)}, u32[]{:S(2)}, u32[]{:S(2)}) collective-permute-start(bf16[2,64,2048]{2,1,0:T(8,128)(2,1)S(1)} %collective-permute-done.1.refs_2_), channel_id=1, source_target_pairs={{0,2},{1,3},{2,4},{3,5},{4,6},{5,7},{6,8},{7,9},{8,10},{9,11},{10,... | collective-permute-start | bytes 1572872 | tf_op jit(solution)/shard_map/ppermute | solution.py:420
  23.1 13.7 %collective-permute-start.5 = (bf16[2,64,2048]{2,1,0:T(8,128)(2,1)S(1)}, bf16[2,64,2048]{2,1,0:T(8,128)(2,1)S(1)}, u32[]{:S(2)}, u32[]{:S(2)}) collective-permute-start(bf16[2,64,2048]{2,1,0:T(8,128)(2,1)S(1)} %collective-permute-done.2.refs_4_), channel_id=1, source_target_pairs={{0,14},{1,15},{2,0},{3,1},{4,2},{5,3},{6,4},{7,5},{8,6},{9,7},{10,... | collective-permute-start | bytes 1572872 | tf_op jit(solution)/shard_map/ppermute | solution.py:420
  36.8 12.8 %collective-permute-start.7 = (bf16[2,64,2048]{2,1,0:T(8,128)(2,1)S(1)}, bf16[2,64,2048]{2,1,0:T(8,128)(2,1)S(1)}, u32[]{:S(2)}, u32[]{:S(2)}) collective-permute-start(bf16[2,64,2048]{2,1,0:T(8,128)(2,1)S(1)} %collective-permute-done.4.refs_6_), channel_id=1, source_target_pairs={{0,2},{1,3},{2,4},{3,5},{4,6},{5,7},{6,8},{7,9},{8,10},{9,11},{10,... | collective-permute-start | bytes 1572872 | tf_op jit(solution)/shard_map/ppermute | solution.py:420
  36.8 12.8 %collective-permute-start.8 = (bf16[2,64,2048]{2,1,0:T(8,128)(2,1)S(1)}, bf16[2,64,2048]{2,1,0:T(8,128)(2,1)S(1)}, u32[]{:S(2)}, u32[]{:S(2)}) collective-permute-start(bf16[2,64,2048]{2,1,0:T(8,128)(2,1)S(1)} %collective-permute-done.5.refs_8_), channel_id=1, source_target_pairs={{0,14},{1,15},{2,0},{3,1},{4,2},{5,3},{6,4},{7,5},{8,6},{9,7},{10,... | collective-permute-start | bytes 1572872 | tf_op jit(solution)/shard_map/ppermute | solution.py:420
  44.1 8.6 %collective-permute-start.13 = (bf16[2,64,2048]{2,1,0:T(8,128)(2,1)S(1)}, bf16[2,64,2048]{2,1,0:T(8,128)(2,1)S(1)}, u32[]{:S(2)}, u32[]{:S(2)}) collective-permute-start(bf16[2,64,2048]{2,1,0:T(8,128)(2,1)S(1)} %constant_dynamic-update-slice_fusion.refs_0_), channel_id=1, source_target_pairs={{0,1},{1,0},{2,3},{3,2},{4,5},{5,4},{6,7},{7,6},{8,9},{9,8},{10,11... | collective-permute-start | bytes 1572872 | tf_op jit(solution)/shard_map/ppermute | solution.py:417
  44.2 11.4 %collective-permute-start.14 = (bf16[2,64,2048]{2,1,0:T(8,128)(2,1)S(1)}, bf16[2,64,2048]{2,1,0:T(8,128)(2,1)S(1)}, u32[]{:S(2)}, u32[]{:S(2)}) collective-permute-start(bf16[2,64,2048]{2,1,0:T(8,128)(2,1)S(1)} %collective-permute-done.1.refs_2_), channel_id=1, source_target_pairs={{0,1},{1,0},{2,3},{3,2},{4,5},{5,4},{6,7},{7,6},{8,9},{9,8},{10,11... | collective-permute-start | bytes 1572872 | tf_op jit(solution)/shard_map/ppermute | solution.py:417
  47.7 17.3 %collective-permute-start.15 = (bf16[2,64,2048]{2,1,0:T(8,128)(2,1)S(1)}, bf16[2,64,2048]{2,1,0:T(8,128)(2,1)S(1)}, u32[]{:S(2)}, u32[]{:S(2)}) collective-permute-start(bf16[2,64,2048]{2,1,0:T(8,128)(2,1)S(1)} %collective-permute-done.2.refs_4_), channel_id=1, source_target_pairs={{0,1},{1,0},{2,3},{3,2},{4,5},{5,4},{6,7},{7,6},{8,9},{9,8},{10,11... | collective-permute-start | bytes 1572872 | tf_op jit(solution)/shard_map/ppermute | solution.py:417
  49.6 19.5 %collective-permute-start.16 = (bf16[2,64,2048]{2,1,0:T(8,128)(2,1)S(1)}, bf16[2,64,2048]{2,1,0:T(8,128)(2,1)S(1)}, u32[]{:S(2)}, u32[]{:S(2)}) collective-permute-start(bf16[2,64,2048]{2,1,0:T(8,128)(2,1)S(1)} %collective-permute-done.4.refs_6_), channel_id=1, source_target_pairs={{0,1},{1,0},{2,3},{3,2},{4,5},{5,4},{6,7},{7,6},{8,9},{9,8},{10,11... | collective-permute-start | bytes 1572872 | tf_op jit(solution)/shard_map/ppermute | solution.py:417
  49.6 12.1 %collective-permute-start.11 = (bf16[64,2048]{1,0:T(8,128)(2,1)S(1)}, bf16[64,2048]{1,0:T(8,128)(2,1)S(1)}, u32[]{:S(2)}, u32[]{:S(2)}) collective-permute-start(bf16[64,2048]{1,0:T(8,128)(2,1)S(1)} %slice_bitcast_fusion.7), channel_id=1, source_target_pairs={{0,14},{1,15},{2,0},{3,1},{4,2},{5,3},{6,4},{7,5},{8,6},{9,7},{10,... | collective-permute-start | bytes 786440 | tf_op jit(solution)/shard_map/ppermute | solution.py:420
  52.6 9.6 %collective-permute-start.10 = (bf16[64,2048]{1,0:T(8,128)(2,1)S(1)}, bf16[64,2048]{1,0:T(8,128)(2,1)S(1)}, u32[]{:S(2)}, u32[]{:S(2)}) collective-permute-start(bf16[64,2048]{1,0:T(8,128)(2,1)S(1)} %slice_bitcast_fusion.8), channel_id=1, source_target_pairs={{0,2},{1,3},{2,4},{3,5},{4,6},{5,7},{6,8},{7,9},{8,10},{9,11},{10,... | collective-permute-start | bytes 786440 | tf_op jit(solution)/shard_map/ppermute | solution.py:420
  61.7 12.4 %collective-permute-start.17 = (bf16[2,64,2048]{2,1,0:T(8,128)(2,1)S(1)}, bf16[2,64,2048]{2,1,0:T(8,128)(2,1)S(1)}, u32[]{:S(2)}, u32[]{:S(2)}) collective-permute-start(bf16[2,64,2048]{2,1,0:T(8,128)(2,1)S(1)} %collective-permute-done.5.refs_8_), channel_id=1, source_target_pairs={{0,1},{1,0},{2,3},{3,2},{4,5},{5,4},{6,7},{7,6},{8,9},{9,8},{10,11... | collective-permute-start | bytes 1572872 | tf_op jit(solution)/shard_map/ppermute | solution.py:417
  61.7 18.6 %collective-permute-start.18 = (bf16[2,64,2048]{2,1,0:T(8,128)(2,1)S(1)}, bf16[2,64,2048]{2,1,0:T(8,128)(2,1)S(1)}, u32[]{:S(2)}, u32[]{:S(2)}) collective-permute-start(bf16[2,64,2048]{2,1,0:T(8,128)(2,1)S(1)} %collective-permute-done.7.refs_10_), channel_id=1, source_target_pairs={{0,1},{1,0},{2,3},{3,2},{4,5},{5,4},{6,7},{7,6},{8,9},{9,8},{10,11... | collective-permute-start | bytes 1572872 | tf_op jit(solution)/shard_map/ppermute | solution.py:417
  62.2 18.1 %collective-permute-start.19 = (bf16[2,64,2048]{2,1,0:T(8,128)(2,1)S(1)}, bf16[2,64,2048]{2,1,0:T(8,128)(2,1)S(1)}, u32[]{:S(2)}, u32[]{:S(2)}) collective-permute-start(bf16[2,64,2048]{2,1,0:T(8,128)(2,1)S(1)} %collective-permute-done.8.refs_12_), channel_id=1, source_target_pairs={{0,1},{1,0},{2,3},{3,2},{4,5},{5,4},{6,7},{7,6},{8,9},{9,8},{10,11... | collective-permute-start | bytes 1572872 | tf_op jit(solution)/shard_map/ppermute | solution.py:417
  69.1 11.2 %collective-permute-start.20 = (bf16[64,2048]{1,0:T(8,128)(2,1)S(1)}, bf16[64,2048]{1,0:T(8,128)(2,1)S(1)}, u32[]{:S(2)}, u32[]{:S(2)}) collective-permute-start(bf16[64,2048]{1,0:T(8,128)(2,1)S(1)} %collective-permute-done.10.refs_14_), channel_id=1, source_target_pairs={{0,1},{1,0},{2,3},{3,2},{4,5},{5,4},{6,7},{7,6},{8,9},{9,8},{10,11... | collective-permute-start | bytes 786440 | tf_op jit(solution)/shard_map/ppermute | solution.py:417
  71.4 8.9 %collective-permute-start.21 = (bf16[64,2048]{1,0:T(8,128)(2,1)S(1)}, bf16[64,2048]{1,0:T(8,128)(2,1)S(1)}, u32[]{:S(2)}, u32[]{:S(2)}) collective-permute-start(bf16[64,2048]{1,0:T(8,128)(2,1)S(1)} %collective-permute-done.11.refs_16_), channel_id=1, source_target_pairs={{0,1},{1,0},{2,3},{3,2},{4,5},{5,4},{6,7},{7,6},{8,9},{9,8},{10,11... | collective-permute-start | bytes 786440 | tf_op jit(solution)/shard_map/ppermute | solution.py:417
  85.0 8.4 %collective-permute-start.23 = (bf16[32,1024]{1,0:T(8,128)(2,1)S(1)}, bf16[32,1024]{1,0:T(8,128)(2,1)S(1)}, u32[]{:S(2)}, u32[]{:S(2)}) collective-permute-start(bf16[32,1024]{1,0:T(8,128)(2,1)S(1)} %get-tuple-element.356), channel_id=1, source_target_pairs={{48,64},{64,80},{80,96},{96,112},{49,65},{65,81},{81,97},{97,113},... | collective-permute-start | bytes 196616 | tf_op jit(solution)/shard_map/ppermute | solution.py:461
  94.4 9.8 %collective-permute-start.25 = (bf16[32,1024]{1,0:T(8,128)(2,1)S(1)}, bf16[32,1024]{1,0:T(8,128)(2,1)S(1)}, u32[]{:S(2)}, u32[]{:S(2)}) collective-permute-start(bf16[32,1024]{1,0:T(8,128)(2,1)S(1)} %get-tuple-element.362), channel_id=1, source_target_pairs={{64,80},{80,96},{96,112},{112,128},{65,81},{81,97},{97,113},{113,1... | collective-permute-start | bytes 196616 | tf_op jit(solution)/shard_map/ppermute | solution.py:461
  95.0 11.0 %collective-permute-start.24 = (bf16[32,1024]{1,0:T(8,128)(2,1)S(1)}, bf16[32,1024]{1,0:T(8,128)(2,1)S(1)}, u32[]{:S(2)}, u32[]{:S(2)}) collective-permute-start(bf16[32,1024]{1,0:T(8,128)(2,1)S(1)} %get-tuple-element.362), channel_id=1, source_target_pairs={{0,16},{16,32},{32,48},{48,64},{1,17},{17,33},{33,49},{49,65},{2,1... | collective-permute-start | bytes 196616 | tf_op jit(solution)/shard_map/ppermute | solution.py:461
  107.4 8.3 %collective-permute-start.26 = (bf16[32,1024]{1,0:T(8,128)(2,1)S(1)}, bf16[32,1024]{1,0:T(8,128)(2,1)S(1)}, u32[]{:S(2)}, u32[]{:S(2)}) collective-permute-start(bf16[32,1024]{1,0:T(8,128)(2,1)S(1)} %get-tuple-element.368), channel_id=1, source_target_pairs={{0,16},{16,32},{32,48},{48,64},{1,17},{17,33},{33,49},{49,65},{2,1... | collective-permute-start | bytes 196616 | tf_op jit(solution)/shard_map/ppermute | solution.py:461
  128.7 8.3 %collective-permute-start.30 = (bf16[32,1024]{1,0:T(8,128)(2,1)S(1)}, bf16[32,1024]{1,0:T(8,128)(2,1)S(1)}, u32[]{:S(2)}, u32[]{:S(2)}) collective-permute-start(bf16[32,1024]{1,0:T(8,128)(2,1)S(1)} %get-tuple-element.380), channel_id=1, source_target_pairs={{0,16},{16,32},{32,48},{48,64},{1,17},{17,33},{33,49},{49,65},{2,1... | collective-permute-start | bytes 196616 | tf_op jit(solution)/shard_map/ppermute | solution.py:461
  140.3 8.3 %collective-permute-start.32 = (bf16[32,1024]{1,0:T(8,128)(2,1)S(1)}, bf16[32,1024]{1,0:T(8,128)(2,1)S(1)}, u32[]{:S(2)}, u32[]{:S(2)}) collective-permute-start(bf16[32,1024]{1,0:T(8,128)(2,1)S(1)} %get-tuple-element.386), channel_id=1, source_target_pairs={{16,32},{32,48},{48,64},{64,80},{17,33},{33,49},{49,65},{65,81},{1... | collective-permute-start | bytes 196616 | tf_op jit(solution)/shard_map/ppermute | solution.py:461
  151.9 8.3 %collective-permute-start.34 = (bf16[32,1024]{1,0:T(8,128)(2,1)S(1)}, bf16[32,1024]{1,0:T(8,128)(2,1)S(1)}, u32[]{:S(2)}, u32[]{:S(2)}) collective-permute-start(bf16[32,1024]{1,0:T(8,128)(2,1)S(1)} %get-tuple-element.392), channel_id=1, source_target_pairs={{32,48},{48,64},{64,80},{80,96},{33,49},{49,65},{65,81},{81,97},{3... | collective-permute-start | bytes 196616 | tf_op jit(solution)/shard_map/ppermute | solution.py:461
  163.9 8.3 %collective-permute-start.36 = (bf16[32,1024]{1,0:T(8,128)(2,1)S(1)}, bf16[32,1024]{1,0:T(8,128)(2,1)S(1)}, u32[]{:S(2)}, u32[]{:S(2)}) collective-permute-start(bf16[32,1024]{1,0:T(8,128)(2,1)S(1)} %get-tuple-element.398), channel_id=1, source_target_pairs={{48,64},{64,80},{80,96},{96,112},{49,65},{65,81},{81,97},{97,113},... | collective-permute-start | bytes 196616 | tf_op jit(solution)/shard_map/ppermute | solution.py:461
  213.9 91.7 %collective-permute-start.69 = (bf16[32,1024]{1,0:T(8,128)(2,1)S(1)}, bf16[32,1024]{1,0:T(8,128)(2,1)S(1)}, u32[]{:S(2)}, u32[]{:S(2)}) collective-permute-start(bf16[32,1024]{1,0:T(8,128)(2,1)S(1)} %get-tuple-element.491), channel_id=1, source_target_pairs={{64,48},{80,64},{96,80},{112,96},{65,49},{81,65},{97,81},{113,97},... | collective-permute-start | bytes 196616 | tf_op jit(solution)/shard_map/ppermute | solution.py:461
  215.2 90.4 %collective-permute-start.68 = (bf16[32,1024]{1,0:T(8,128)(2,1)S(1)}, bf16[32,1024]{1,0:T(8,128)(2,1)S(1)}, u32[]{:S(2)}, u32[]{:S(2)}) collective-permute-start(bf16[32,1024]{1,0:T(8,128)(2,1)S(1)} %get-tuple-element.491), channel_id=1, source_target_pairs={{176,160},{192,176},{208,192},{224,208},{177,161},{193,177},{209,1... | collective-permute-start | bytes 196616 | tf_op jit(solution)/shard_map/ppermute | solution.py:461
  309.1 9.2 %collective-permute-start.71 = (bf16[32,1024]{1,0:T(8,128)(2,1)S(1)}, bf16[32,1024]{1,0:T(8,128)(2,1)S(1)}, u32[]{:S(2)}, u32[]{:S(2)}) collective-permute-start(bf16[32,1024]{1,0:T(8,128)(2,1)S(1)} %get-tuple-element.497), channel_id=1, source_target_pairs={{48,32},{64,48},{80,64},{96,80},{49,33},{65,49},{81,65},{97,81},{5... | collective-permute-start | bytes 196616 | tf_op jit(solution)/shard_map/ppermute | solution.py:461
  321.7 11.2 %collective-permute-start.73 = (bf16[32,1024]{1,0:T(8,128)(2,1)S(1)}, bf16[32,1024]{1,0:T(8,128)(2,1)S(1)}, u32[]{:S(2)}, u32[]{:S(2)}) collective-permute-start(bf16[32,1024]{1,0:T(8,128)(2,1)S(1)} %get-tuple-element.503), channel_id=1, source_target_pairs={{32,16},{48,32},{64,48},{80,64},{33,17},{49,33},{65,49},{81,65},{3... | collective-permute-start | bytes 196616 | tf_op jit(solution)/shard_map/ppermute | solution.py:461
  323.6 9.3 %collective-permute-start.72 = (bf16[32,1024]{1,0:T(8,128)(2,1)S(1)}, bf16[32,1024]{1,0:T(8,128)(2,1)S(1)}, u32[]{:S(2)}, u32[]{:S(2)}) collective-permute-start(bf16[32,1024]{1,0:T(8,128)(2,1)S(1)} %get-tuple-element.503), channel_id=1, source_target_pairs={{144,128},{160,144},{176,160},{192,176},{145,129},{161,145},{177,1... | collective-permute-start | bytes 196616 | tf_op jit(solution)/shard_map/ppermute | solution.py:461
  336.8 8.3 %collective-permute-start.75 = (bf16[32,1024]{1,0:T(8,128)(2,1)S(1)}, bf16[32,1024]{1,0:T(8,128)(2,1)S(1)}, u32[]{:S(2)}, u32[]{:S(2)}) collective-permute-start(bf16[32,1024]{1,0:T(8,128)(2,1)S(1)} %get-tuple-element.509), channel_id=1, source_target_pairs={{16,0},{32,16},{48,32},{64,48},{17,1},{33,17},{49,33},{65,49},{18,... | collective-permute-start | bytes 196616 | tf_op jit(solution)/shard_map/ppermute | solution.py:461
  348.5 8.3 %collective-permute-start.77 = (bf16[32,1024]{1,0:T(8,128)(2,1)S(1)}, bf16[32,1024]{1,0:T(8,128)(2,1)S(1)}, u32[]{:S(2)}, u32[]{:S(2)}) collective-permute-start(bf16[32,1024]{1,0:T(8,128)(2,1)S(1)} %get-tuple-element.515), channel_id=1, source_target_pairs={{16,0},{32,16},{48,32},{64,48},{17,1},{33,17},{49,33},{65,49},{18,... | collective-permute-start | bytes 196616 | tf_op jit(solution)/shard_map/ppermute | solution.py:461
  357.4 8.3 %collective-permute-start.79 = (bf16[32,1024]{1,0:T(8,128)(2,1)S(1)}, bf16[32,1024]{1,0:T(8,128)(2,1)S(1)}, u32[]{:S(2)}, u32[]{:S(2)}) collective-permute-start(bf16[32,1024]{1,0:T(8,128)(2,1)S(1)} %get-tuple-element.521), channel_id=1, source_target_pairs={{16,0},{32,16},{48,32},{64,48},{17,1},{33,17},{49,33},{65,49},{18,... | collective-permute-start | bytes 196616 | tf_op jit(solution)/shard_map/ppermute | solution.py:461
  366.4 8.3 %collective-permute-start.81 = (bf16[32,1024]{1,0:T(8,128)(2,1)S(1)}, bf16[32,1024]{1,0:T(8,128)(2,1)S(1)}, u32[]{:S(2)}, u32[]{:S(2)}) collective-permute-start(bf16[32,1024]{1,0:T(8,128)(2,1)S(1)} %get-tuple-element.527), channel_id=1, source_target_pairs={{16,0},{32,16},{48,32},{64,48},{17,1},{33,17},{49,33},{65,49},{18,... | collective-permute-start | bytes 196616 | tf_op jit(solution)/shard_map/ppermute | solution.py:461
  377.4 19.5 %collective-permute-start.82 = (bf16[32,1024]{1,0:T(8,128)(2,1)S(1)}, bf16[32,1024]{1,0:T(8,128)(2,1)S(1)}, u32[]{:S(2)}, u32[]{:S(2)}) collective-permute-start(bf16[32,1024]{1,0:T(8,128)(2,1)S(1)} %get-tuple-element.533), channel_id=1, source_target_pairs={{64,48},{80,64},{96,80},{112,96},{65,49},{81,65},{97,81},{113,97},... | collective-permute-start | bytes 196616 | tf_op jit(solution)/shard_map/ppermute | solution.py:461
  400.4 8.3 %collective-permute-start.83 = (bf16[32,1024]{1,0:T(8,128)(2,1)S(1)}, bf16[32,1024]{1,0:T(8,128)(2,1)S(1)}, u32[]{:S(2)}, u32[]{:S(2)}) collective-permute-start(bf16[32,1024]{1,0:T(8,128)(2,1)S(1)} %get-tuple-element.539), channel_id=1, source_target_pairs={{48,32},{64,48},{80,64},{96,80},{49,33},{65,49},{81,65},{97,81},{5... | collective-permute-start | bytes 196616 | tf_op jit(solution)/shard_map/ppermute | solution.py:461
  412.5 8.3 %collective-permute-start.84 = (bf16[32,1024]{1,0:T(8,128)(2,1)S(1)}, bf16[32,1024]{1,0:T(8,128)(2,1)S(1)}, u32[]{:S(2)}, u32[]{:S(2)}) collective-permute-start(bf16[32,1024]{1,0:T(8,128)(2,1)S(1)} %get-tuple-element.545), channel_id=1, source_target_pairs={{32,16},{48,32},{64,48},{80,64},{33,17},{49,33},{65,49},{81,65},{3... | collective-permute-start | bytes 196616 | tf_op jit(solution)/shard_map/ppermute | solution.py:461
  436.0 8.3 %collective-permute-start.86 = (bf16[32,1024]{1,0:T(8,128)(2,1)S(1)}, bf16[32,1024]{1,0:T(8,128)(2,1)S(1)}, u32[]{:S(2)}, u32[]{:S(2)}) collective-permute-start(bf16[32,1024]{1,0:T(8,128)(2,1)S(1)} %get-tuple-element.557), channel_id=1, source_target_pairs={{16,0},{32,16},{48,32},{64,48},{17,1},{33,17},{49,33},{65,49},{18,... | collective-permute-start | bytes 196616 | tf_op jit(solution)/shard_map/ppermute | solution.py:461
  468.7 15.4 %collective-permute-start.90 = (bf16[2,64,4096]{2,1,0:T(8,128)(2,1)S(1)}, bf16[2,64,4096]{2,1,0:T(8,128)(2,1)S(1)}, u32[]{:S(2)}, u32[]{:S(2)}) collective-permute-start(bf16[2,64,4096]{2,1,0:T(8,128)(2,1)S(1)} %get-tuple-element.575), channel_id=1, source_target_pairs={{0,1},{1,0},{2,3},{3,2},{4,5},{5,4},{6,7},{7,6},{8,9},{9,8},{10,11... | collective-permute-start | bytes 3145736 | tf_op jit(solution)/shard_map/ppermute | solution.py:385
  469.3 29.8 %collective-permute-start.89 = (bf16[3,64,4096]{2,1,0:T(8,128)(2,1)S(1)}, bf16[3,64,4096]{2,1,0:T(8,128)(2,1)S(1)}, u32[]{:S(2)}, u32[]{:S(2)}) collective-permute-start(bf16[3,64,4096]{2,1,0:T(8,128)(2,1)S(1)} %get-tuple-element.573), channel_id=1, source_target_pairs={{0,1},{1,0},{2,3},{3,2},{4,5},{5,4},{6,7},{7,6},{8,9},{9,8},{10,11... | collective-permute-start | bytes 4718600 | tf_op jit(solution)/shard_map/ppermute | solution.py:385
  470.8 9.9 %collective-permute-start.93 = (bf16[64,2048]{1,0:T(8,128)(2,1)S(1)}, bf16[64,2048]{1,0:T(8,128)(2,1)S(1)}, u32[]{:S(2)}, u32[]{:S(2)}) collective-permute-start(bf16[64,2048]{1,0:T(8,128)(2,1)S(1)} %get-tuple-element.588), channel_id=1, source_target_pairs={{0,2},{1,3},{2,4},{3,5},{4,6},{5,7},{6,8},{7,9},{8,10},{9,11},{10,... | collective-permute-start | bytes 786440 | tf_op jit(solution)/shard_map/ppermute | solution.py:388
  470.9 9.8 %collective-permute-start.97 = (bf16[64,2048]{1,0:T(8,128)(2,1)S(1)}, bf16[64,2048]{1,0:T(8,128)(2,1)S(1)}, u32[]{:S(2)}, u32[]{:S(2)}) collective-permute-start(bf16[64,2048]{1,0:T(8,128)(2,1)S(1)} %get-tuple-element.589), channel_id=1, source_target_pairs={{0,14},{1,15},{2,0},{3,1},{4,2},{5,3},{6,4},{7,5},{8,6},{9,7},{10,... | collective-permute-start | bytes 786440 | tf_op jit(solution)/shard_map/ppermute | solution.py:389
  480.8 14.7 %collective-permute-start.94 = (bf16[64,4096]{1,0:T(8,128)(2,1)S(1)}, bf16[64,4096]{1,0:T(8,128)(2,1)S(1)}, u32[]{:S(2)}, u32[]{:S(2)}) collective-permute-start(bf16[64,4096]{1,0:T(8,128)(2,1)S(1)} %get-tuple-element.584), channel_id=1, source_target_pairs={{0,2},{1,3},{2,4},{3,5},{4,6},{5,7},{6,8},{7,9},{8,10},{9,11},{10,... | collective-permute-start | bytes 1572872 | tf_op jit(solution)/shard_map/ppermute | solution.py:395
  481.4 14.1 %collective-permute-start.98 = (bf16[64,4096]{1,0:T(8,128)(2,1)S(1)}, bf16[64,4096]{1,0:T(8,128)(2,1)S(1)}, u32[]{:S(2)}, u32[]{:S(2)}) collective-permute-start(bf16[64,4096]{1,0:T(8,128)(2,1)S(1)} %get-tuple-element.585), channel_id=1, source_target_pairs={{0,14},{1,15},{2,0},{3,1},{4,2},{5,3},{6,4},{7,5},{8,6},{9,7},{10,... | collective-permute-start | bytes 1572872 | tf_op jit(solution)/shard_map/ppermute | solution.py:396
  495.8 13.8 %collective-permute-start.95 = (bf16[64,4096]{1,0:T(8,128)(2,1)S(1)}, bf16[64,4096]{1,0:T(8,128)(2,1)S(1)}, u32[]{:S(2)}, u32[]{:S(2)}) collective-permute-start(bf16[64,4096]{1,0:T(8,128)(2,1)S(1)} %get-tuple-element.582), channel_id=1, source_target_pairs={{0,2},{1,3},{2,4},{3,5},{4,6},{5,7},{6,8},{7,9},{8,10},{9,11},{10,... | collective-permute-start | bytes 1572872 | tf_op jit(solution)/shard_map/ppermute | solution.py:395
  496.2 13.3 %collective-permute-start.99 = (bf16[64,4096]{1,0:T(8,128)(2,1)S(1)}, bf16[64,4096]{1,0:T(8,128)(2,1)S(1)}, u32[]{:S(2)}, u32[]{:S(2)}) collective-permute-start(bf16[64,4096]{1,0:T(8,128)(2,1)S(1)} %get-tuple-element.583), channel_id=1, source_target_pairs={{0,14},{1,15},{2,0},{3,1},{4,2},{5,3},{6,4},{7,5},{8,6},{9,7},{10,... | collective-permute-start | bytes 1572872 | tf_op jit(solution)/shard_map/ppermute | solution.py:396
  509.8 12.9 %collective-permute-start.96 = (bf16[64,4096]{1,0:T(8,128)(2,1)S(1)}, bf16[64,4096]{1,0:T(8,128)(2,1)S(1)}, u32[]{:S(2)}, u32[]{:S(2)}) collective-permute-start(bf16[64,4096]{1,0:T(8,128)(2,1)S(1)} %get-tuple-element.580), channel_id=1, source_target_pairs={{0,2},{1,3},{2,4},{3,5},{4,6},{5,7},{6,8},{7,9},{8,10},{9,11},{10,... | collective-permute-start | bytes 1572872 | tf_op jit(solution)/shard_map/ppermute | solution.py:400
  510.1 12.6 %collective-permute-start.100 = (bf16[64,4096]{1,0:T(8,128)(2,1)S(1)}, bf16[64,4096]{1,0:T(8,128)(2,1)S(1)}, u32[]{:S(2)}, u32[]{:S(2)}) collective-permute-start(bf16[64,4096]{1,0:T(8,128)(2,1)S(1)} %get-tuple-element.581), channel_id=1, source_target_pairs={{0,14},{1,15},{2,0},{3,1},{4,2},{5,3},{6,4},{7,5},{8,6},{9,7},{10,... | collective-permute-start | bytes 1572872 | tf_op jit(solution)/shard_map/ppermute | solution.py:401
  (55 other events, 239.0 us)

commit v4 on v2

--- a/solution.py
+++ b/solution.py
@@ -132,8 +132,15 @@
             ("down", self.backward(t), -1),
         ):
             if stages:
-                found[name] = [(s, s + way) for s in stages if 0 <= s + way < self.layers]
+                useful = [(s, s + way) for s in stages if 0 <= s + way < self.layers]
+                if way < 0 and useful and useful[0][1] == 0:
+                    useful = [(s, s - 1) for s in range(1, min(self.pieces + 1, self.layers))]
+                found[name] = useful
         return found
+
+
+def sends(waves, way):
+    return bool(waves.get(way)) or bool(waves.get("tan_" + way))
 
 
 def tick_kernel(plan, t, with_probes, loss_scale, rows, width, hidden, *refs):
@@ -146,7 +153,9 @@
         refs = refs[2:]
     got = {name: refs.pop(0) for name in waves}
     sb_d, sb_f, sf_d, sf_f, sf_n = refs[:5]
-    put_up, put_down = refs[5:]
+    refs = refs[5:]
+    put_up = refs.pop(0) if sends(waves, "up") else None
+    put_down = refs.pop(0) if sends(waves, "down") else None
 
     layers, pieces, lag = plan.layers, plan.pieces, plan.lag
     stage = lax.axis_index("pipe")
@@ -184,9 +193,11 @@
             total = total + dot(active_b, w_down[c, :])
         result = total.astype(bf16)
 
-        @pl.when(jnp.logical_not(at_last))
-        def _():
-            put_up[...] = result
+        if put_up is not None:
+
+            @pl.when(jnp.logical_not(at_last))
+            def _():
+                put_up[...] = result
 
         @pl.when(at_last)
         def _():
@@ -220,9 +231,11 @@
             total = total + dot(active_tb, w_down[c, :])
         result = total.astype(bf16)
 
-        @pl.when(jnp.logical_not(at_last))
-        def _():
-            put_up[...] = result
+        if put_up is not None:
+
+            @pl.when(jnp.logical_not(at_last))
+            def _():
+                put_up[...] = result
 
         @pl.when(at_last)
         def _():
@@ -246,9 +259,11 @@
         sf_d[BN, at, :] = back
         result = (cotan.astype(f32) + back).astype(bf16)
 
-        @pl.when(jnp.logical_not(at_first))
-        def _():
-            put_down[...] = result
+        if put_down is not None:
+
+            @pl.when(jnp.logical_not(at_first))
+            def _():
+                put_down[...] = result
 
     def ready_backward():
         for c in chunks:
@@ -272,9 +287,11 @@
         back_t = narrow(RR, at) * sf_d[BN, at, :] + inverse * inner
         result = (cotan_t.astype(f32) + back_t).astype(bf16)
 
-        @pl.when(jnp.logical_not(at_first))
-        def _():
-            put_down[...] = result
+        if put_down is not None:
+
+            @pl.when(jnp.logical_not(at_first))
+            def _():
+                put_down[...] = result
 
     if plan.backward_tan(t):
         when_due(t - lag - (2 * layers - 1 - stage), backward_tan)
@@ -375,8 +392,13 @@
 def scatter(mine, theirs, groups, hidden):
     ahead, behind, across = routes(groups)
 
+    swapped = []
+
     def wide(kept, given):
-        return kept.astype(f32) + lax.ppermute(given, "dp", across).astype(f32)
+        if swapped:
+            given, swapped[-1] = lax.optimization_barrier((given, swapped[-1]))
+        swapped.append(lax.ppermute(given, "dp", across))
+        return kept.astype(f32) + swapped[-1].astype(f32)
 
     far = wide(mine[0], theirs[0])[0].astype(bf16)
     from_behind = lax.ppermute(far[:, :hidden], "dp", ahead)
@@ -407,8 +429,13 @@
     plan = Plan(layers, PIECES, LAG)
     ahead, behind, across = routes(groups)
 
+    swapped = []
+
     def swap(array):
-        return lax.ppermute(array, "dp", across)
+        if swapped:
+            array, swapped[-1] = lax.optimization_barrier((array, swapped[-1]))
+        swapped.append(lax.ppermute(array, "dp", across))
+        return swapped[-1]
 
     def ring(both):
         return [lax.ppermute(both[0], "dp", ahead), lax.ppermute(both[1], "dp", behind)]
@@ -432,25 +459,26 @@
     probes = None
     got = {"up": nothing}
     packet = pltpu.VMEM((rows, width), bf16)
-    ring_ticks = {0: 1, 2: 2, 3: 3, 4: 4}
+    ring_ticks = {0: 1, 1: 2, 2: 3, 3: 4}
     for t in range(plan.ticks):
         if t == LAG - 1:
             probes = assemble(blocks, halves, groups, part, hidden)
         waves = plan.waves(t)
+        ways = [way for way in ("up", "down") if sends(waves, way)]
         with_probes = plan.ready_forward(t) or plan.ready_backward(t)
         operands = list(state) + list(held) + (list(probes) if with_probes else [])
         operands += [got.get(name, nothing) for name in waves]
         outs = pl.pallas_call(
             functools.partial(tick_kernel, plan, t, with_probes, loss_scale, rows, width, hidden),
-            out_shape=tuple(pltpu.VMEM(s.shape, s.dtype) for s in state) + (packet,) * 2,
+            out_shape=tuple(pltpu.VMEM(s.shape, s.dtype) for s in state) + (packet,) * len(ways),
             in_specs=[IN_VMEM] * len(operands),
-            out_specs=(IN_VMEM,) * 7,
+            out_specs=(IN_VMEM,) * (5 + len(ways)),
             input_output_aliases={i: i for i in range(5)},
             compiler_params=pltpu.CompilerParams(vmem_limit_bytes=8 << 20),
             cost_estimate=pl.CostEstimate(flops=1 << 30, bytes_accessed=1 << 23, transcendentals=0),
             name="tick",
         )(*[vmem(o) for o in operands])
-        state, sent = outs[:5], {"up": outs[5], "down": outs[6]}
+        state, sent = outs[:5], dict(zip(ways, outs[5:]))
         got = {
             name: lax.ppermute(sent[name.removeprefix("tan_")], "pipe", edges)
             for name, edges in waves.items()

time: 645 us -> 499 us (0.77)
  the two profiles are of different devices: /device:TPU:32 before, /device:TPU:6 now
where the time goes in v4:
time: 499 us; the launch traced here: 489 us
  waiting for transfers between devices  275 us (55%)
  starting transfers between devices  136 us (27%)
  Pallas kernels  71.4 us (14%)
    ppermute x72, waiting for transfers between devices, on_device(): lax.ppermute(sent[name.removeprefix('tan_')], 'pipe', edges)  204 us
    ppermute x72, starting transfers between devices, on_device(): lax.ppermute(sent[name.removeprefix('tan_')], 'pipe', edges)  106 us
    pallas_call x42, Pallas kernels, on_device(): pl.pallas_call(functools.partial(tick_kernel, plan, t, with_probes, loss_...  61.1 us
    ppermute x3, waiting for transfers between devices, scatter(): from_behind = lax.ppermute(up, 'dp', ahead)  30.6 us
    ppermute x4, waiting for transfers between devices, ring(): lax.ppermute(both[0], 'dp', ahead)  20.9 us
    ppermute x4, starting transfers between devices, ring(): lax.ppermute(both[1], 'dp', behind)  15.5 us
  transfers between devices with their start and end apart: 101, of which 36 were waited for; matrix products, arithmetic and copies ran while one was open for 0% of the time, Pallas kernels for 2%

profile of v4, /device:TPU:6, one launch (start us, length us, event | category | flops | bytes accessed | tf_op | source)
XLA Modules:
  0.0 489.1 jit_solution(5088927046851007774)
XLA Ops:
  2.6 5.9 %collective-permute-start.2 = (bf16[2,64,2048]{2,1,0:T(8,128)(2,1)S(1)}, bf16[2,64,2048]{2,1,0:T(8,128)(2,1)S(1)}, u32[]{:S(2)}, u32[]{:S(2)}) collective-permute-start(bf16[2,64,2048]{2,1,0:T(8,128)(2,1)S(1)} %constant_dynamic-update-slice_fusion.refs_0_), channel_id=1, source_target_pairs={{0,14},{1,15},{2,0},{3,1},{4,2},{5,3},{6,4},{7,5},{8,6},{9,7},{10,... | collective-permute-start | bytes 1572872 | tf_op jit(solution)/shard_map/ppermute | solution.py:441
  8.5 3.5 load.1
  12.8 6.9 %collective-permute-done.2.refs_4_ = bf16[2,64,2048]{2,1,0:T(8,128)(2,1)S(1)} collective-permute-done((bf16[2,64,2048]{2,1,0:T(8,128)(2,1)S(1)}, bf16[2,64,2048]{2,1,0:T(8,128)(2,1)S(1)}, u32[]{:S(2)}, u32[]{:S(2)}) %collective-permute-start.2) | collective-permute-done | bytes 524320 | tf_op jit(solution)/shard_map/ppermute | solution.py:441
  19.7 3.4 collective-permute-done.1.refs_2_
  23.1 3.2 collective-permute-start.5
  27.0 11.6 %collective-permute-done.4.refs_6_ = bf16[2,64,2048]{2,1,0:T(8,128)(2,1)S(1)} collective-permute-done((bf16[2,64,2048]{2,1,0:T(8,128)(2,1)S(1)}, bf16[2,64,2048]{2,1,0:T(8,128)(2,1)S(1)}, u32[]{:S(2)}, u32[]{:S(2)}) %collective-permute-start.4) | collective-permute-done | bytes 524320 | tf_op jit(solution)/shard_map/ppermute | solution.py:441
  38.8 3.2 collective-permute-start.8
  43.3 6.3 %collective-permute-done.6.refs_9_ = bf16[32,1024]{1,0:T(8,128)(2,1)S(1)} collective-permute-done((bf16[32,1024]{1,0:T(8,128)(2,1)S(1)}, bf16[32,1024]{1,0:T(8,128)(2,1)S(1)}, u32[]{:S(2)}, u32[]{:S(2)}) %collective-permute-start.6) | collective-permute-done | bytes 65568 | tf_op jit(solution)/shard_map/ppermute | solution.py:483
  49.6 4.6 collective-permute-done.7.refs_10_
  56.5 3.1 collective-permute-start.11
  63.6 4.2 collective-permute-done.9.refs_9_
  72.9 3.4 collective-permute-start.12
  81.2 5.5 %collective-permute-start.22 = (bf16[32,1024]{1,0:T(8,128)(2,1)S(1)}, bf16[32,1024]{1,0:T(8,128)(2,1)S(1)}, u32[]{:S(2)}, u32[]{:S(2)}) collective-permute-start(bf16[32,1024]{1,0:T(8,128)(2,1)S(1)} %get-tuple-element.369), channel_id=1, source_target_pairs={{80,96},{64,80},{48,64},{32,48},{81,97},{65,81},{49,65},{33,49},{8... | collective-permute-start | bytes 196616 | tf_op jit(solution)/shard_map/ppermute | solution.py:483
  90.8 6.4 %collective-permute-start.23 = (bf16[32,1024]{1,0:T(8,128)(2,1)S(1)}, bf16[32,1024]{1,0:T(8,128)(2,1)S(1)}, u32[]{:S(2)}, u32[]{:S(2)}) collective-permute-start(bf16[32,1024]{1,0:T(8,128)(2,1)S(1)} %get-tuple-element.375), channel_id=1, source_target_pairs={{96,112},{80,96},{64,80},{48,64},{97,113},{81,97},{65,81},{49,65},... | collective-permute-start | bytes 196616 | tf_op jit(solution)/shard_map/ppermute | solution.py:483
  106.1 4.8 collective-permute-done.28.refs_11_
  114.0 4.9 collective-permute-start.30
  123.5 6.4 %collective-permute-start.32 = (bf16[32,1024]{1,0:T(8,128)(2,1)S(1)}, bf16[32,1024]{1,0:T(8,128)(2,1)S(1)}, u32[]{:S(2)}, u32[]{:S(2)}) collective-permute-start(bf16[32,1024]{1,0:T(8,128)(2,1)S(1)} %get-tuple-element.405), channel_id=1, source_target_pairs={{64,80},{48,64},{32,48},{16,32},{65,81},{49,65},{33,49},{17,33},{6... | collective-permute-start | bytes 196616 | tf_op jit(solution)/shard_map/ppermute | solution.py:483
  134.5 6.4 %collective-permute-start.34 = (bf16[32,1024]{1,0:T(8,128)(2,1)S(1)}, bf16[32,1024]{1,0:T(8,128)(2,1)S(1)}, u32[]{:S(2)}, u32[]{:S(2)}) collective-permute-start(bf16[32,1024]{1,0:T(8,128)(2,1)S(1)} %get-tuple-element.411), channel_id=1, source_target_pairs={{80,96},{64,80},{48,64},{32,48},{81,97},{65,81},{49,65},{33,49},{8... | collective-permute-start | bytes 196616 | tf_op jit(solution)/shard_map/ppermute | solution.py:483
  145.6 6.4 %collective-permute-start.36 = (bf16[32,1024]{1,0:T(8,128)(2,1)S(1)}, bf16[32,1024]{1,0:T(8,128)(2,1)S(1)}, u32[]{:S(2)}, u32[]{:S(2)}) collective-permute-start(bf16[32,1024]{1,0:T(8,128)(2,1)S(1)} %get-tuple-element.417), channel_id=1, source_target_pairs={{96,112},{80,96},{64,80},{48,64},{97,113},{81,97},{65,81},{49,65},... | collective-permute-start | bytes 196616 | tf_op jit(solution)/shard_map/ppermute | solution.py:483
  162.0 4.3 collective-permute-start.49
  170.5 4.9 tick.64
  178.9 5.7 %tick.66 = (bf16[4,128,1024]{2,1,0:T(8,128)(2,1)S(1)}, bf16[4,128,2048]{2,1,0:T(8,128)(2,1)S(1)}, f32[6,128,1024]{2,1,0:T(8,128)S(1)}, f32[6,128,2048]{2,1,0:T(8...) custom-call(bf16[4,128,1024]{2,1,0:T(8,128)(2,1)S(1)} %get-tuple-ele, ...), custom_call_target="tpu_custom_call", output_to_operand_aliasing={{0}: (0, {}), {1}: (1, {}), {2}: (2, {}), {3}: (3, {}), {4}... | custom-call | flops 1073741824 | bytes 8388608 | tf_op jit(solution)/shard_map/tick/pallas_call | solution.py:471
  189.4 4.6 tick.69
  196.0 94.9 %collective-permute-done.69.refs_12_ = bf16[32,1024]{1,0:T(8,128)(2,1)S(1)} collective-permute-done((bf16[32,1024]{1,0:T(8,128)(2,1)S(1)}, bf16[32,1024]{1,0:T(8,128)(2,1)S(1)}, u32[]{:S(2)}, u32[]{:S(2)}) %collective-permute-start.69) | collective-permute-done | bytes 65568 | tf_op jit(solution)/shard_map/ppermute | solution.py:483
  296.3 8.0 %collective-permute-done.71.refs_12_ = bf16[32,1024]{1,0:T(8,128)(2,1)S(1)} collective-permute-done((bf16[32,1024]{1,0:T(8,128)(2,1)S(1)}, bf16[32,1024]{1,0:T(8,128)(2,1)S(1)}, u32[]{:S(2)}, u32[]{:S(2)}) %collective-permute-start.71) | collective-permute-done | bytes 65568 | tf_op jit(solution)/shard_map/ppermute | solution.py:483
  309.7 5.7 %collective-permute-done.73.refs_12_ = bf16[32,1024]{1,0:T(8,128)(2,1)S(1)} collective-permute-done((bf16[32,1024]{1,0:T(8,128)(2,1)S(1)}, bf16[32,1024]{1,0:T(8,128)(2,1)S(1)}, u32[]{:S(2)}, u32[]{:S(2)}) %collective-permute-start.73) | collective-permute-done | bytes 65568 | tf_op jit(solution)/shard_map/ppermute | solution.py:483
  315.4 3.0 tick.72
  321.0 5.7 %collective-permute-done.75.refs_12_ = bf16[32,1024]{1,0:T(8,128)(2,1)S(1)} collective-permute-done((bf16[32,1024]{1,0:T(8,128)(2,1)S(1)}, bf16[32,1024]{1,0:T(8,128)(2,1)S(1)}, u32[]{:S(2)}, u32[]{:S(2)}) %collective-permute-start.75) | collective-permute-done | bytes 65568 | tf_op jit(solution)/shard_map/ppermute | solution.py:483
  332.1 5.7 %collective-permute-done.77.refs_12_ = bf16[32,1024]{1,0:T(8,128)(2,1)S(1)} collective-permute-done((bf16[32,1024]{1,0:T(8,128)(2,1)S(1)}, bf16[32,1024]{1,0:T(8,128)(2,1)S(1)}, u32[]{:S(2)}, u32[]{:S(2)}) %collective-permute-start.77) | collective-permute-done | bytes 65568 | tf_op jit(solution)/shard_map/ppermute | solution.py:483
  341.1 4.9 %collective-permute-done.79.refs_12_ = bf16[32,1024]{1,0:T(8,128)(2,1)S(1)} collective-permute-done((bf16[32,1024]{1,0:T(8,128)(2,1)S(1)}, bf16[32,1024]{1,0:T(8,128)(2,1)S(1)}, u32[]{:S(2)}, u32[]{:S(2)}) %collective-permute-start.79) | collective-permute-done | bytes 65568 | tf_op jit(solution)/shard_map/ppermute | solution.py:483
  348.8 5.7 %collective-permute-done.81.refs_12_ = bf16[32,1024]{1,0:T(8,128)(2,1)S(1)} collective-permute-done((bf16[32,1024]{1,0:T(8,128)(2,1)S(1)}, bf16[32,1024]{1,0:T(8,128)(2,1)S(1)}, u32[]{:S(2)}, u32[]{:S(2)}) %collective-permute-start.81) | collective-permute-done | bytes 65568 | tf_op jit(solution)/shard_map/ppermute | solution.py:483
  357.9 8.1 %collective-permute-done.82.refs_11_ = bf16[32,1024]{1,0:T(8,128)(2,1)S(1)} collective-permute-done((bf16[32,1024]{1,0:T(8,128)(2,1)S(1)}, bf16[32,1024]{1,0:T(8,128)(2,1)S(1)}, u32[]{:S(2)}, u32[]{:S(2)}) %collective-permute-start.82) | collective-permute-done | bytes 65568 | tf_op jit(solution)/shard_map/ppermute | solution.py:483
  370.8 6.3 %collective-permute-done.83.refs_11_ = bf16[32,1024]{1,0:T(8,128)(2,1)S(1)} collective-permute-done((bf16[32,1024]{1,0:T(8,128)(2,1)S(1)}, bf16[32,1024]{1,0:T(8,128)(2,1)S(1)}, u32[]{:S(2)}, u32[]{:S(2)}) %collective-permute-start.83) | collective-permute-done | bytes 65568 | tf_op jit(solution)/shard_map/ppermute | solution.py:483
  377.1 3.3 tick.78
  382.4 6.3 %collective-permute-done.84.refs_11_ = bf16[32,1024]{1,0:T(8,128)(2,1)S(1)} collective-permute-done((bf16[32,1024]{1,0:T(8,128)(2,1)S(1)}, bf16[32,1024]{1,0:T(8,128)(2,1)S(1)}, u32[]{:S(2)}, u32[]{:S(2)}) %collective-permute-start.84) | collective-permute-done | bytes 65568 | tf_op jit(solution)/shard_map/ppermute | solution.py:483
  393.6 6.3 %collective-permute-done.85.refs_9_ = bf16[32,1024]{1,0:T(8,128)(2,1)S(1)} collective-permute-done((bf16[32,1024]{1,0:T(8,128)(2,1)S(1)}, bf16[32,1024]{1,0:T(8,128)(2,1)S(1)}, u32[]{:S(2)}, u32[]{:S(2)}) %collective-permute-start.85) | collective-permute-done | bytes 65568 | tf_op jit(solution)/shard_map/ppermute | solution.py:483
  404.7 6.3 %collective-permute-done.86.refs_9_ = bf16[32,1024]{1,0:T(8,128)(2,1)S(1)} collective-permute-done((bf16[32,1024]{1,0:T(8,128)(2,1)S(1)}, bf16[32,1024]{1,0:T(8,128)(2,1)S(1)}, u32[]{:S(2)}, u32[]{:S(2)}) %collective-permute-start.86) | collective-permute-done | bytes 65568 | tf_op jit(solution)/shard_map/ppermute | solution.py:483
  413.7 5.6 %collective-permute-done.87.refs_9_ = bf16[32,1024]{1,0:T(8,128)(2,1)S(1)} collective-permute-done((bf16[32,1024]{1,0:T(8,128)(2,1)S(1)}, bf16[32,1024]{1,0:T(8,128)(2,1)S(1)}, u32[]{:S(2)}, u32[]{:S(2)}) %collective-permute-start.87) | collective-permute-done | bytes 65568 | tf_op jit(solution)/shard_map/ppermute | solution.py:483
  421.2 6.3 %collective-permute-done.88.refs_9_ = bf16[32,1024]{1,0:T(8,128)(2,1)S(1)} collective-permute-done((bf16[32,1024]{1,0:T(8,128)(2,1)S(1)}, bf16[32,1024]{1,0:T(8,128)(2,1)S(1)}, u32[]{:S(2)}, u32[]{:S(2)}) %collective-permute-start.88) | collective-permute-done | bytes 65568 | tf_op jit(solution)/shard_map/ppermute | solution.py:483
  427.7 5.8 %curvature.1 = (bf16[1,64,4096]{2,1,0:T(8,128)(2,1)S(1)}, bf16[2,64,4096]{2,1,0:T(8,128)(2,1)S(1)}, bf16[2,64,4096]{2,1,0:T(8,128)(2,1)S(1)}, bf16[3,64,4096]{2,...) custom-call(bf16[4,128,1024]{2,1,0:T(8,128)(2,1)S(1)} %get-tuple-ele, ...), custom_call_target="tpu_custom_call" | custom-call | tf_op jit(solution)/shard_map/curvature/pallas_call | solution.py:339
  435.9 3.2 collective-permute-start.97
  439.4 6.3 %collective-permute-done.93 = bf16[64,2048]{1,0:T(8,128)(2,1)S(1)} collective-permute-done((bf16[64,2048]{1,0:T(8,128)(2,1)S(1)}, bf16[64,2048]{1,0:T(8,128)(2,1)S(1)}, u32[]{:S(2)}, u32[]{:S(2)}) %collective-permute-start.93) | collective-permute-done | bytes 262176 | tf_op jit(solution)/shard_map/ppermute | solution.py:404
  445.9 3.2 collective-permute-start.98
  449.4 11.1 %collective-permute-done.94 = bf16[64,4096]{1,0:T(8,128)(2,1)S(1)} collective-permute-done((bf16[64,4096]{1,0:T(8,128)(2,1)S(1)}, bf16[64,4096]{1,0:T(8,128)(2,1)S(1)}, u32[]{:S(2)}, u32[]{:S(2)}) %collective-permute-start.94) | collective-permute-done | bytes 524320 | tf_op jit(solution)/shard_map/ppermute | solution.py:411
  460.9 3.2 collective-permute-start.99
  464.6 10.0 %collective-permute-done.95 = bf16[64,4096]{1,0:T(8,128)(2,1)S(1)} collective-permute-done((bf16[64,4096]{1,0:T(8,128)(2,1)S(1)}, bf16[64,4096]{1,0:T(8,128)(2,1)S(1)}, u32[]{:S(2)}, u32[]{:S(2)}) %collective-permute-start.95) | collective-permute-done | bytes 524320 | tf_op jit(solution)/shard_map/ppermute | solution.py:411
  474.9 3.2 collective-permute-start.100
  478.1 9.5 %collective-permute-done.96 = bf16[64,4096]{1,0:T(8,128)(2,1)S(1)} collective-permute-done((bf16[64,4096]{1,0:T(8,128)(2,1)S(1)}, bf16[64,4096]{1,0:T(8,128)(2,1)S(1)}, u32[]{:S(2)}, u32[]{:S(2)}) %collective-permute-start.96) | collective-permute-done | bytes 524320 | tf_op jit(solution)/shard_map/ppermute | solution.py:416
  (218 shorter events, 129.4 us)
Async XLA Ops:
  2.6 17.1 %collective-permute-start.2 = (bf16[2,64,2048]{2,1,0:T(8,128)(2,1)S(1)}, bf16[2,64,2048]{2,1,0:T(8,128)(2,1)S(1)}, u32[]{:S(2)}, u32[]{:S(2)}) collective-permute-start(bf16[2,64,2048]{2,1,0:T(8,128)(2,1)S(1)} %constant_dynamic-update-slice_fusion.refs_0_), channel_id=1, source_target_pairs={{0,14},{1,15},{2,0},{3,1},{4,2},{5,3},{6,4},{7,5},{8,6},{9,7},{10,... | collective-permute-start | bytes 1572872 | tf_op jit(solution)/shard_map/ppermute | solution.py:441
  8.5 14.6 %collective-permute-start.1 = (bf16[2,64,2048]{2,1,0:T(8,128)(2,1)S(1)}, bf16[2,64,2048]{2,1,0:T(8,128)(2,1)S(1)}, u32[]{:S(2)}, u32[]{:S(2)}) collective-permute-start(bf16[2,64,2048]{2,1,0:T(8,128)(2,1)S(1)} %constant_dynamic-update-slice_fusion.refs_0_), channel_id=1, source_target_pairs={{0,2},{1,3},{2,4},{3,5},{4,6},{5,7},{6,8},{7,9},{8,10},{9,11},{10,... | collective-permute-start | bytes 1572872 | tf_op jit(solution)/shard_map/ppermute | solution.py:441
  8.5 14.6 %collective-permute-start.13 = (bf16[2,64,2048]{2,1,0:T(8,128)(2,1)S(1)}, bf16[2,64,2048]{2,1,0:T(8,128)(2,1)S(1)}, u32[]{:S(2)}, u32[]{:S(2)}) collective-permute-start(bf16[2,64,2048]{2,1,0:T(8,128)(2,1)S(1)} %constant_dynamic-update-slice_fusion.refs_0_), channel_id=1, source_target_pairs={{0,1},{1,0},{2,3},{3,2},{4,5},{5,4},{6,7},{7,6},{8,9},{9,8},{10,11... | collective-permute-start | bytes 1572872 | tf_op jit(solution)/shard_map/ppermute | solution.py:437
  23.1 15.5 %collective-permute-start.4 = (bf16[2,64,2048]{2,1,0:T(8,128)(2,1)S(1)}, bf16[2,64,2048]{2,1,0:T(8,128)(2,1)S(1)}, u32[]{:S(2)}, u32[]{:S(2)}) collective-permute-start(bf16[2,64,2048]{2,1,0:T(8,128)(2,1)S(1)} %collective-permute-done.1.refs_2_), channel_id=1, source_target_pairs={{0,2},{1,3},{2,4},{3,5},{4,6},{5,7},{6,8},{7,9},{8,10},{9,11},{10,... | collective-permute-start | bytes 1572872 | tf_op jit(solution)/shard_map/ppermute | solution.py:441
  23.1 15.5 %collective-permute-start.5 = (bf16[2,64,2048]{2,1,0:T(8,128)(2,1)S(1)}, bf16[2,64,2048]{2,1,0:T(8,128)(2,1)S(1)}, u32[]{:S(2)}, u32[]{:S(2)}) collective-permute-start(bf16[2,64,2048]{2,1,0:T(8,128)(2,1)S(1)} %collective-permute-done.2.refs_4_), channel_id=1, source_target_pairs={{0,14},{1,15},{2,0},{3,1},{4,2},{5,3},{6,4},{7,5},{8,6},{9,7},{10,... | collective-permute-start | bytes 1572872 | tf_op jit(solution)/shard_map/ppermute | solution.py:441
  26.4 12.3 %collective-permute-start.15 = (bf16[2,64,2048]{2,1,0:T(8,128)(2,1)S(1)}, bf16[2,64,2048]{2,1,0:T(8,128)(2,1)S(1)}, u32[]{:S(2)}, u32[]{:S(2)}) collective-permute-start(bf16[2,64,2048]{2,1,0:T(8,128)(2,1)S(1)} %collective-permute-done.2.refs_4_), channel_id=1, source_target_pairs={{0,1},{1,0},{2,3},{3,2},{4,5},{5,4},{6,7},{7,6},{8,9},{9,8},{10,11... | collective-permute-start | bytes 1572872 | tf_op jit(solution)/shard_map/ppermute | solution.py:437
  38.7 15.6 %collective-permute-start.7 = (bf16[2,64,2048]{2,1,0:T(8,128)(2,1)S(1)}, bf16[2,64,2048]{2,1,0:T(8,128)(2,1)S(1)}, u32[]{:S(2)}, u32[]{:S(2)}) collective-permute-start(bf16[2,64,2048]{2,1,0:T(8,128)(2,1)S(1)} %collective-permute-done.4.refs_6_), channel_id=1, source_target_pairs={{0,2},{1,3},{2,4},{3,5},{4,6},{5,7},{6,8},{7,9},{8,10},{9,11},{10,... | collective-permute-start | bytes 1572872 | tf_op jit(solution)/shard_map/ppermute | solution.py:441
  38.8 15.5 %collective-permute-start.8 = (bf16[2,64,2048]{2,1,0:T(8,128)(2,1)S(1)}, bf16[2,64,2048]{2,1,0:T(8,128)(2,1)S(1)}, u32[]{:S(2)}, u32[]{:S(2)}) collective-permute-start(bf16[2,64,2048]{2,1,0:T(8,128)(2,1)S(1)} %collective-permute-done.5.refs_8_), channel_id=1, source_target_pairs={{0,14},{1,15},{2,0},{3,1},{4,2},{5,3},{6,4},{7,5},{8,6},{9,7},{10,... | collective-permute-start | bytes 1572872 | tf_op jit(solution)/shard_map/ppermute | solution.py:441
  42.0 12.2 %collective-permute-start.17 = (bf16[2,64,2048]{2,1,0:T(8,128)(2,1)S(1)}, bf16[2,64,2048]{2,1,0:T(8,128)(2,1)S(1)}, u32[]{:S(2)}, u32[]{:S(2)}) collective-permute-start(bf16[2,64,2048]{2,1,0:T(8,128)(2,1)S(1)} %collective-permute-done.5.refs_8_), channel_id=1, source_target_pairs={{0,1},{1,0},{2,3},{3,2},{4,5},{5,4},{6,7},{7,6},{8,9},{9,8},{10,11... | collective-permute-start | bytes 1572872 | tf_op jit(solution)/shard_map/ppermute | solution.py:437
  42.0 7.6 %collective-permute-start.6 = (bf16[32,1024]{1,0:T(8,128)(2,1)S(1)}, bf16[32,1024]{1,0:T(8,128)(2,1)S(1)}, u32[]{:S(2)}, u32[]{:S(2)}) collective-permute-start(bf16[32,1024]{1,0:T(8,128)(2,1)S(1)} %get-tuple-element.333), channel_id=1, source_target_pairs={{32,48},{16,32},{0,16},{33,49},{17,33},{1,17},{34,50},{18,34},{2,1... | collective-permute-start | bytes 196616 | tf_op jit(solution)/shard_map/ppermute | solution.py:483
  56.1 12.9 %collective-permute-start.19 = (bf16[2,64,2048]{2,1,0:T(8,128)(2,1)S(1)}, bf16[2,64,2048]{2,1,0:T(8,128)(2,1)S(1)}, u32[]{:S(2)}, u32[]{:S(2)}) collective-permute-start(bf16[2,64,2048]{2,1,0:T(8,128)(2,1)S(1)} %collective-permute-done.8.refs_12_), channel_id=1, source_target_pairs={{0,1},{1,0},{2,3},{3,2},{4,5},{5,4},{6,7},{7,6},{8,9},{9,8},{10,11... | collective-permute-start | bytes 1572872 | tf_op jit(solution)/shard_map/ppermute | solution.py:437
  56.5 11.4 %collective-permute-start.11 = (bf16[64,2048]{1,0:T(8,128)(2,1)S(1)}, bf16[64,2048]{1,0:T(8,128)(2,1)S(1)}, u32[]{:S(2)}, u32[]{:S(2)}) collective-permute-start(bf16[64,2048]{1,0:T(8,128)(2,1)S(1)} %slice_bitcast_fusion.7), channel_id=1, source_target_pairs={{0,14},{1,15},{2,0},{3,1},{4,2},{5,3},{6,4},{7,5},{8,6},{9,7},{10,... | collective-permute-start | bytes 786440 | tf_op jit(solution)/shard_map/ppermute | solution.py:441
  59.6 9.5 %collective-permute-start.10 = (bf16[64,2048]{1,0:T(8,128)(2,1)S(1)}, bf16[64,2048]{1,0:T(8,128)(2,1)S(1)}, u32[]{:S(2)}, u32[]{:S(2)}) collective-permute-start(bf16[64,2048]{1,0:T(8,128)(2,1)S(1)} %slice_bitcast_fusion.8), channel_id=1, source_target_pairs={{0,2},{1,3},{2,4},{3,5},{4,6},{5,7},{6,8},{7,9},{8,10},{9,11},{10,... | collective-permute-start | bytes 786440 | tf_op jit(solution)/shard_map/ppermute | solution.py:441
  70.6 16.1 %collective-permute-start.21 = (bf16[64,2048]{1,0:T(8,128)(2,1)S(1)}, bf16[64,2048]{1,0:T(8,128)(2,1)S(1)}, u32[]{:S(2)}, u32[]{:S(2)}) collective-permute-start(bf16[64,2048]{1,0:T(8,128)(2,1)S(1)} %collective-permute-done.11.refs_16_), channel_id=1, source_target_pairs={{0,1},{1,0},{2,3},{3,2},{4,5},{5,4},{6,7},{7,6},{8,9},{9,8},{10,11... | collective-permute-start | bytes 786440 | tf_op jit(solution)/shard_map/ppermute | solution.py:437
  81.2 7.4 %collective-permute-start.22 = (bf16[32,1024]{1,0:T(8,128)(2,1)S(1)}, bf16[32,1024]{1,0:T(8,128)(2,1)S(1)}, u32[]{:S(2)}, u32[]{:S(2)}) collective-permute-start(bf16[32,1024]{1,0:T(8,128)(2,1)S(1)} %get-tuple-element.369), channel_id=1, source_target_pairs={{80,96},{64,80},{48,64},{32,48},{81,97},{65,81},{49,65},{33,49},{8... | collective-permute-start | bytes 196616 | tf_op jit(solution)/shard_map/ppermute | solution.py:483
  90.8 8.3 %collective-permute-start.23 = (bf16[32,1024]{1,0:T(8,128)(2,1)S(1)}, bf16[32,1024]{1,0:T(8,128)(2,1)S(1)}, u32[]{:S(2)}, u32[]{:S(2)}) collective-permute-start(bf16[32,1024]{1,0:T(8,128)(2,1)S(1)} %get-tuple-element.375), channel_id=1, source_target_pairs={{96,112},{80,96},{64,80},{48,64},{97,113},{81,97},{65,81},{49,65},... | collective-permute-start | bytes 196616 | tf_op jit(solution)/shard_map/ppermute | solution.py:483
  122.8 7.1 %collective-permute-start.33 = (bf16[32,1024]{1,0:T(8,128)(2,1)S(1)}, bf16[32,1024]{1,0:T(8,128)(2,1)S(1)}, u32[]{:S(2)}, u32[]{:S(2)}) collective-permute-start(bf16[32,1024]{1,0:T(8,128)(2,1)S(1)} %get-tuple-element.405), channel_id=1, source_target_pairs={{176,192},{160,176},{144,160},{128,144},{177,193},{161,177},{145,1... | collective-permute-start | bytes 196616 | tf_op jit(solution)/shard_map/ppermute | solution.py:483
  123.5 8.3 %collective-permute-start.32 = (bf16[32,1024]{1,0:T(8,128)(2,1)S(1)}, bf16[32,1024]{1,0:T(8,128)(2,1)S(1)}, u32[]{:S(2)}, u32[]{:S(2)}) collective-permute-start(bf16[32,1024]{1,0:T(8,128)(2,1)S(1)} %get-tuple-element.405), channel_id=1, source_target_pairs={{64,80},{48,64},{32,48},{16,32},{65,81},{49,65},{33,49},{17,33},{6... | collective-permute-start | bytes 196616 | tf_op jit(solution)/shard_map/ppermute | solution.py:483
  133.8 7.1 %collective-permute-start.35 = (bf16[32,1024]{1,0:T(8,128)(2,1)S(1)}, bf16[32,1024]{1,0:T(8,128)(2,1)S(1)}, u32[]{:S(2)}, u32[]{:S(2)}) collective-permute-start(bf16[32,1024]{1,0:T(8,128)(2,1)S(1)} %get-tuple-element.411), channel_id=1, source_target_pairs={{192,208},{176,192},{160,176},{144,160},{193,209},{177,193},{161,1... | collective-permute-start | bytes 196616 | tf_op jit(solution)/shard_map/ppermute | solution.py:483
  134.5 8.3 %collective-permute-start.34 = (bf16[32,1024]{1,0:T(8,128)(2,1)S(1)}, bf16[32,1024]{1,0:T(8,128)(2,1)S(1)}, u32[]{:S(2)}, u32[]{:S(2)}) collective-permute-start(bf16[32,1024]{1,0:T(8,128)(2,1)S(1)} %get-tuple-element.411), channel_id=1, source_target_pairs={{80,96},{64,80},{48,64},{32,48},{81,97},{65,81},{49,65},{33,49},{8... | collective-permute-start | bytes 196616 | tf_op jit(solution)/shard_map/ppermute | solution.py:483
  144.9 7.1 %collective-permute-start.37 = (bf16[32,1024]{1,0:T(8,128)(2,1)S(1)}, bf16[32,1024]{1,0:T(8,128)(2,1)S(1)}, u32[]{:S(2)}, u32[]{:S(2)}) collective-permute-start(bf16[32,1024]{1,0:T(8,128)(2,1)S(1)} %get-tuple-element.417), channel_id=1, source_target_pairs={{208,224},{192,208},{176,192},{160,176},{209,225},{193,209},{177,1... | collective-permute-start | bytes 196616 | tf_op jit(solution)/shard_map/ppermute | solution.py:483
  145.6 8.3 %collective-permute-start.36 = (bf16[32,1024]{1,0:T(8,128)(2,1)S(1)}, bf16[32,1024]{1,0:T(8,128)(2,1)S(1)}, u32[]{:S(2)}, u32[]{:S(2)}) collective-permute-start(bf16[32,1024]{1,0:T(8,128)(2,1)S(1)} %get-tuple-element.417), channel_id=1, source_target_pairs={{96,112},{80,96},{64,80},{48,64},{97,113},{81,97},{65,81},{49,65},... | collective-permute-start | bytes 196616 | tf_op jit(solution)/shard_map/ppermute | solution.py:483
  194.0 96.9 %collective-permute-start.69 = (bf16[32,1024]{1,0:T(8,128)(2,1)S(1)}, bf16[32,1024]{1,0:T(8,128)(2,1)S(1)}, u32[]{:S(2)}, u32[]{:S(2)}) collective-permute-start(bf16[32,1024]{1,0:T(8,128)(2,1)S(1)} %get-tuple-element.510), channel_id=1, source_target_pairs={{64,48},{80,64},{96,80},{112,96},{65,49},{81,65},{97,81},{113,97},... | collective-permute-start | bytes 196616 | tf_op jit(solution)/shard_map/ppermute | solution.py:483
  195.3 95.6 %collective-permute-start.68 = (bf16[32,1024]{1,0:T(8,128)(2,1)S(1)}, bf16[32,1024]{1,0:T(8,128)(2,1)S(1)}, u32[]{:S(2)}, u32[]{:S(2)}) collective-permute-start(bf16[32,1024]{1,0:T(8,128)(2,1)S(1)} %get-tuple-element.510), channel_id=1, source_target_pairs={{176,160},{192,176},{208,192},{224,208},{177,161},{193,177},{209,1... | collective-permute-start | bytes 196616 | tf_op jit(solution)/shard_map/ppermute | solution.py:483
  293.7 10.6 %collective-permute-start.71 = (bf16[32,1024]{1,0:T(8,128)(2,1)S(1)}, bf16[32,1024]{1,0:T(8,128)(2,1)S(1)}, u32[]{:S(2)}, u32[]{:S(2)}) collective-permute-start(bf16[32,1024]{1,0:T(8,128)(2,1)S(1)} %get-tuple-element.516), channel_id=1, source_target_pairs={{48,32},{64,48},{80,64},{96,80},{49,33},{65,49},{81,65},{97,81},{5... | collective-permute-start | bytes 196616 | tf_op jit(solution)/shard_map/ppermute | solution.py:483
  295.7 8.7 %collective-permute-start.70 = (bf16[32,1024]{1,0:T(8,128)(2,1)S(1)}, bf16[32,1024]{1,0:T(8,128)(2,1)S(1)}, u32[]{:S(2)}, u32[]{:S(2)}) collective-permute-start(bf16[32,1024]{1,0:T(8,128)(2,1)S(1)} %get-tuple-element.516), channel_id=1, source_target_pairs={{160,144},{176,160},{192,176},{208,192},{161,145},{177,161},{193,1... | collective-permute-start | bytes 196616 | tf_op jit(solution)/shard_map/ppermute | solution.py:483
  307.1 8.3 %collective-permute-start.73 = (bf16[32,1024]{1,0:T(8,128)(2,1)S(1)}, bf16[32,1024]{1,0:T(8,128)(2,1)S(1)}, u32[]{:S(2)}, u32[]{:S(2)}) collective-permute-start(bf16[32,1024]{1,0:T(8,128)(2,1)S(1)} %get-tuple-element.522), channel_id=1, source_target_pairs={{32,16},{48,32},{64,48},{80,64},{33,17},{49,33},{65,49},{81,65},{3... | collective-permute-start | bytes 196616 | tf_op jit(solution)/shard_map/ppermute | solution.py:483
  318.4 8.3 %collective-permute-start.75 = (bf16[32,1024]{1,0:T(8,128)(2,1)S(1)}, bf16[32,1024]{1,0:T(8,128)(2,1)S(1)}, u32[]{:S(2)}, u32[]{:S(2)}) collective-permute-start(bf16[32,1024]{1,0:T(8,128)(2,1)S(1)} %get-tuple-element.528), channel_id=1, source_target_pairs={{16,0},{32,16},{48,32},{64,48},{17,1},{33,17},{49,33},{65,49},{18,... | collective-permute-start | bytes 196616 | tf_op jit(solution)/shard_map/ppermute | solution.py:483
  329.5 8.3 %collective-permute-start.77 = (bf16[32,1024]{1,0:T(8,128)(2,1)S(1)}, bf16[32,1024]{1,0:T(8,128)(2,1)S(1)}, u32[]{:S(2)}, u32[]{:S(2)}) collective-permute-start(bf16[32,1024]{1,0:T(8,128)(2,1)S(1)} %get-tuple-element.534), channel_id=1, source_target_pairs={{16,0},{32,16},{48,32},{64,48},{17,1},{33,17},{49,33},{65,49},{18,... | collective-permute-start | bytes 196616 | tf_op jit(solution)/shard_map/ppermute | solution.py:483
  337.8 8.3 %collective-permute-start.79 = (bf16[32,1024]{1,0:T(8,128)(2,1)S(1)}, bf16[32,1024]{1,0:T(8,128)(2,1)S(1)}, u32[]{:S(2)}, u32[]{:S(2)}) collective-permute-start(bf16[32,1024]{1,0:T(8,128)(2,1)S(1)} %get-tuple-element.540), channel_id=1, source_target_pairs={{16,0},{32,16},{48,32},{64,48},{17,1},{33,17},{49,33},{65,49},{18,... | collective-permute-start | bytes 196616 | tf_op jit(solution)/shard_map/ppermute | solution.py:483
  346.2 8.3 %collective-permute-start.81 = (bf16[32,1024]{1,0:T(8,128)(2,1)S(1)}, bf16[32,1024]{1,0:T(8,128)(2,1)S(1)}, u32[]{:S(2)}, u32[]{:S(2)}) collective-permute-start(bf16[32,1024]{1,0:T(8,128)(2,1)S(1)} %get-tuple-element.546), channel_id=1, source_target_pairs={{16,0},{32,16},{48,32},{64,48},{17,1},{33,17},{49,33},{65,49},{18,... | collective-permute-start | bytes 196616 | tf_op jit(solution)/shard_map/ppermute | solution.py:483
  356.6 9.4 %collective-permute-start.82 = (bf16[32,1024]{1,0:T(8,128)(2,1)S(1)}, bf16[32,1024]{1,0:T(8,128)(2,1)S(1)}, u32[]{:S(2)}, u32[]{:S(2)}) collective-permute-start(bf16[32,1024]{1,0:T(8,128)(2,1)S(1)} %get-tuple-element.552), channel_id=1, source_target_pairs={{64,48},{80,64},{96,80},{112,96},{65,49},{81,65},{97,81},{113,97},... | collective-permute-start | bytes 196616 | tf_op jit(solution)/shard_map/ppermute | solution.py:483
  368.9 8.3 %collective-permute-start.83 = (bf16[32,1024]{1,0:T(8,128)(2,1)S(1)}, bf16[32,1024]{1,0:T(8,128)(2,1)S(1)}, u32[]{:S(2)}, u32[]{:S(2)}) collective-permute-start(bf16[32,1024]{1,0:T(8,128)(2,1)S(1)} %get-tuple-element.558), channel_id=1, source_target_pairs={{48,32},{64,48},{80,64},{96,80},{49,33},{65,49},{81,65},{97,81},{5... | collective-permute-start | bytes 196616 | tf_op jit(solution)/shard_map/ppermute | solution.py:483
  380.5 8.3 %collective-permute-start.84 = (bf16[32,1024]{1,0:T(8,128)(2,1)S(1)}, bf16[32,1024]{1,0:T(8,128)(2,1)S(1)}, u32[]{:S(2)}, u32[]{:S(2)}) collective-permute-start(bf16[32,1024]{1,0:T(8,128)(2,1)S(1)} %get-tuple-element.564), channel_id=1, source_target_pairs={{32,16},{48,32},{64,48},{80,64},{33,17},{49,33},{65,49},{81,65},{3... | collective-permute-start | bytes 196616 | tf_op jit(solution)/shard_map/ppermute | solution.py:483
  391.6 8.3 %collective-permute-start.85 = (bf16[32,1024]{1,0:T(8,128)(2,1)S(1)}, bf16[32,1024]{1,0:T(8,128)(2,1)S(1)}, u32[]{:S(2)}, u32[]{:S(2)}) collective-permute-start(bf16[32,1024]{1,0:T(8,128)(2,1)S(1)} %get-tuple-element.570), channel_id=1, source_target_pairs={{16,0},{32,16},{48,32},{64,48},{17,1},{33,17},{49,33},{65,49},{18,... | collective-permute-start | bytes 196616 | tf_op jit(solution)/shard_map/ppermute | solution.py:483
  402.8 8.3 %collective-permute-start.86 = (bf16[32,1024]{1,0:T(8,128)(2,1)S(1)}, bf16[32,1024]{1,0:T(8,128)(2,1)S(1)}, u32[]{:S(2)}, u32[]{:S(2)}) collective-permute-start(bf16[32,1024]{1,0:T(8,128)(2,1)S(1)} %get-tuple-element.576), channel_id=1, source_target_pairs={{16,0},{32,16},{48,32},{64,48},{17,1},{33,17},{49,33},{65,49},{18,... | collective-permute-start | bytes 196616 | tf_op jit(solution)/shard_map/ppermute | solution.py:483
  411.0 8.3 %collective-permute-start.87 = (bf16[32,1024]{1,0:T(8,128)(2,1)S(1)}, bf16[32,1024]{1,0:T(8,128)(2,1)S(1)}, u32[]{:S(2)}, u32[]{:S(2)}) collective-permute-start(bf16[32,1024]{1,0:T(8,128)(2,1)S(1)} %get-tuple-element.582), channel_id=1, source_target_pairs={{16,0},{32,16},{48,32},{64,48},{17,1},{33,17},{49,33},{65,49},{18,... | collective-permute-start | bytes 196616 | tf_op jit(solution)/shard_map/ppermute | solution.py:483
  419.3 8.3 %collective-permute-start.88 = (bf16[32,1024]{1,0:T(8,128)(2,1)S(1)}, bf16[32,1024]{1,0:T(8,128)(2,1)S(1)}, u32[]{:S(2)}, u32[]{:S(2)}) collective-permute-start(bf16[32,1024]{1,0:T(8,128)(2,1)S(1)} %get-tuple-element.588), channel_id=1, source_target_pairs={{16,0},{32,16},{48,32},{64,48},{17,1},{33,17},{49,33},{65,49},{18,... | collective-permute-start | bytes 196616 | tf_op jit(solution)/shard_map/ppermute | solution.py:483
  435.8 9.9 %collective-permute-start.93 = (bf16[64,2048]{1,0:T(8,128)(2,1)S(1)}, bf16[64,2048]{1,0:T(8,128)(2,1)S(1)}, u32[]{:S(2)}, u32[]{:S(2)}) collective-permute-start(bf16[64,2048]{1,0:T(8,128)(2,1)S(1)} %get-tuple-element.610), channel_id=1, source_target_pairs={{0,2},{1,3},{2,4},{3,5},{4,6},{5,7},{6,8},{7,9},{8,10},{9,11},{10,... | collective-permute-start | bytes 786440 | tf_op jit(solution)/shard_map/ppermute | solution.py:404
  435.9 9.8 %collective-permute-start.97 = (bf16[64,2048]{1,0:T(8,128)(2,1)S(1)}, bf16[64,2048]{1,0:T(8,128)(2,1)S(1)}, u32[]{:S(2)}, u32[]{:S(2)}) collective-permute-start(bf16[64,2048]{1,0:T(8,128)(2,1)S(1)} %get-tuple-element.611), channel_id=1, source_target_pairs={{0,14},{1,15},{2,0},{3,1},{4,2},{5,3},{6,4},{7,5},{8,6},{9,7},{10,... | collective-permute-start | bytes 786440 | tf_op jit(solution)/shard_map/ppermute | solution.py:405
  439.1 10.0 %collective-permute-start.91 = (bf16[2,64,4096]{2,1,0:T(8,128)(2,1)S(1)}, bf16[2,64,4096]{2,1,0:T(8,128)(2,1)S(1)}, u32[]{:S(2)}, u32[]{:S(2)}) collective-permute-start(bf16[2,64,4096]{2,1,0:T(8,128)(2,1)S(1)} %get-tuple-element.597), channel_id=1, source_target_pairs={{0,1},{1,0},{2,3},{3,2},{4,5},{5,4},{6,7},{7,6},{8,9},{9,8},{10,11... | collective-permute-start | bytes 3145736 | tf_op jit(solution)/shard_map/ppermute | solution.py:400
  445.8 14.7 %collective-permute-start.94 = (bf16[64,4096]{1,0:T(8,128)(2,1)S(1)}, bf16[64,4096]{1,0:T(8,128)(2,1)S(1)}, u32[]{:S(2)}, u32[]{:S(2)}) collective-permute-start(bf16[64,4096]{1,0:T(8,128)(2,1)S(1)} %get-tuple-element.606), channel_id=1, source_target_pairs={{0,2},{1,3},{2,4},{3,5},{4,6},{5,7},{6,8},{7,9},{8,10},{9,11},{10,... | collective-permute-start | bytes 1572872 | tf_op jit(solution)/shard_map/ppermute | solution.py:411
  445.9 14.6 %collective-permute-start.98 = (bf16[64,4096]{1,0:T(8,128)(2,1)S(1)}, bf16[64,4096]{1,0:T(8,128)(2,1)S(1)}, u32[]{:S(2)}, u32[]{:S(2)}) collective-permute-start(bf16[64,4096]{1,0:T(8,128)(2,1)S(1)} %get-tuple-element.607), channel_id=1, source_target_pairs={{0,14},{1,15},{2,0},{3,1},{4,2},{5,3},{6,4},{7,5},{8,6},{9,7},{10,... | collective-permute-start | bytes 1572872 | tf_op jit(solution)/shard_map/ppermute | solution.py:412
  449.2 14.9 %collective-permute-start.92 = (bf16[3,64,4096]{2,1,0:T(8,128)(2,1)S(1)}, bf16[3,64,4096]{2,1,0:T(8,128)(2,1)S(1)}, u32[]{:S(2)}, u32[]{:S(2)}) collective-permute-start(bf16[3,64,4096]{2,1,0:T(8,128)(2,1)S(1)} %get-tuple-element.598), channel_id=1, source_target_pairs={{0,1},{1,0},{2,3},{3,2},{4,5},{5,4},{6,7},{7,6},{8,9},{9,8},{10,11... | collective-permute-start | bytes 4718600 | tf_op jit(solution)/shard_map/ppermute | solution.py:400
  460.8 13.8 %collective-permute-start.95 = (bf16[64,4096]{1,0:T(8,128)(2,1)S(1)}, bf16[64,4096]{1,0:T(8,128)(2,1)S(1)}, u32[]{:S(2)}, u32[]{:S(2)}) collective-permute-start(bf16[64,4096]{1,0:T(8,128)(2,1)S(1)} %get-tuple-element.604), channel_id=1, source_target_pairs={{0,2},{1,3},{2,4},{3,5},{4,6},{5,7},{6,8},{7,9},{8,10},{9,11},{10,... | collective-permute-start | bytes 1572872 | tf_op jit(solution)/shard_map/ppermute | solution.py:411
  460.9 13.7 %collective-permute-start.99 = (bf16[64,4096]{1,0:T(8,128)(2,1)S(1)}, bf16[64,4096]{1,0:T(8,128)(2,1)S(1)}, u32[]{:S(2)}, u32[]{:S(2)}) collective-permute-start(bf16[64,4096]{1,0:T(8,128)(2,1)S(1)} %get-tuple-element.605), channel_id=1, source_target_pairs={{0,14},{1,15},{2,0},{3,1},{4,2},{5,3},{6,4},{7,5},{8,6},{9,7},{10,... | collective-permute-start | bytes 1572872 | tf_op jit(solution)/shard_map/ppermute | solution.py:412
  474.8 12.8 %collective-permute-start.96 = (bf16[64,4096]{1,0:T(8,128)(2,1)S(1)}, bf16[64,4096]{1,0:T(8,128)(2,1)S(1)}, u32[]{:S(2)}, u32[]{:S(2)}) collective-permute-start(bf16[64,4096]{1,0:T(8,128)(2,1)S(1)} %get-tuple-element.602), channel_id=1, source_target_pairs={{0,2},{1,3},{2,4},{3,5},{4,6},{5,7},{6,8},{7,9},{8,10},{9,11},{10,... | collective-permute-start | bytes 1572872 | tf_op jit(solution)/shard_map/ppermute | solution.py:416
  474.9 12.8 %collective-permute-start.100 = (bf16[64,4096]{1,0:T(8,128)(2,1)S(1)}, bf16[64,4096]{1,0:T(8,128)(2,1)S(1)}, u32[]{:S(2)}, u32[]{:S(2)}) collective-permute-start(bf16[64,4096]{1,0:T(8,128)(2,1)S(1)} %get-tuple-element.603), channel_id=1, source_target_pairs={{0,14},{1,15},{2,0},{3,1},{4,2},{5,3},{6,4},{7,5},{8,6},{9,7},{10,... | collective-permute-start | bytes 1572872 | tf_op jit(solution)/shard_map/ppermute | solution.py:417
  (55 other events, 173.4 us)

commit v5 on v4

--- a/solution.py
+++ b/solution.py
@@ -8,7 +8,7 @@
 from jax.sharding import PartitionSpec as P
 
 PIECES = 4
-LAG = 7
+LAG = 3
 CHUNK = 512
 
 epsilon = 1e-05
@@ -118,10 +118,13 @@
         return self.stages(2 * self.layers - 1 - t + self.lag, -1)
 
     def ready_forward(self, t):
-        return 0 <= t - (self.lag - 1) < self.layers
+        found = [(t - (self.lag - 1) - half * (self.pieces // 2), half) for half in range(2)]
+        return [(s, half) for s, half in found if 0 <= s < self.layers]
 
     def ready_backward(self, t):
-        return 0 <= 2 * self.layers - 2 + self.lag - t < self.layers
+        last = 2 * self.layers - 2 + self.lag - t
+        found = [(last + half * (self.pieces // 2), half) for half in range(2)]
+        return [(s, half) for s, half in found if 0 <= s < self.layers]
 
     def waves(self, t):
         found = {}
@@ -133,6 +136,8 @@
         ):
             if stages:
                 useful = [(s, s + way) for s in stages if 0 <= s + way < self.layers]
+                if useful == [(self.layers - 2, self.layers - 1)] and self.layers > 2:
+                    useful = [(s, s + 1) for s in (self.layers - 2, self.layers - 3)]
                 if way < 0 and useful and useful[0][1] == 0:
                     useful = [(s, s - 1) for s in range(1, min(self.pieces + 1, self.layers))]
                 found[name] = useful
@@ -143,11 +148,10 @@
     return bool(waves.get(way)) or bool(waves.get("tan_" + way))
 
 
-def tick_kernel(plan, t, with_probes, loss_scale, rows, width, hidden, *refs):
+def tick_kernel(plan, t, waves, with_probes, loss_scale, rows, width, hidden, *refs):
     refs = list(refs[5:])
-    waves = plan.waves(t)
-    w_up, w_down, source, goal = refs[:4]
-    refs = refs[4:]
+    w_up, w_down, t_up, t_down, source, goal = refs[:6]
+    refs = refs[6:]
     if with_probes:
         u_up, u_down = refs[:2]
         refs = refs[2:]
@@ -204,11 +208,11 @@
             gap = result.astype(f32) - goal[at, :].astype(f32)
             sb_d[G, at, :] = (gap * loss_scale).astype(bf16)
 
-    def ready_forward():
+    def ready_forward(at):
         for c in chunks:
-            sf_f[XU, :, c] = dot(sb_d[X], u_up[:, c])
+            sf_f[XU, at, c] = dot(sb_d[X, at, :], u_up[:, c])
         for c in [slice(c, c + CHUNK) for c in range(0, width, CHUNK)]:
-            sf_d[AV, :, c] = dot_last(sb_f[A], u_down[c, :])
+            sf_d[AV, at, c] = dot_last(sb_f[A, at, :], u_down[c, :])
 
     def forward_tan(at):
         tangent = got["tan_up"][...].astype(f32)
@@ -246,11 +250,11 @@
         sb_d[G, at, :] = cotan
         grad = jnp.zeros((rows, width), f32)
         for c in chunks:
-            grad_act = dot_last(cotan, w_down[c, :])
+            grad_act = dot(cotan, t_down[:, c])
             sf_f[CC, at, c] = grad_act * sf_f[CURVE, at, c]
             grad_pre = (grad_act * sf_f[SLOPE, at, c]).astype(bf16)
             sb_f[PR, at, c] = grad_pre
-            grad = grad + dot_last(grad_pre, w_up[:, c])
+            grad = grad + dot(grad_pre, t_up[c, :])
         sf_d[QN, at, :] = grad
         normed = sf_d[XH, at, :]
         along = mean(grad * normed)
@@ -265,22 +269,22 @@
             def _():
                 put_down[...] = result
 
-    def ready_backward():
+    def ready_backward(at):
         for c in chunks:
-            sf_f[GV, :, c] = dot(sb_d[G], u_down[:, c])
+            sf_f[GV, at, c] = dot(sb_d[G, at, :], u_down[:, c])
         for c in [slice(c, c + CHUNK) for c in range(0, width, CHUNK)]:
-            sf_d[PU, :, c] = dot_last(sb_f[PR], u_up[c, :])
+            sf_d[PU, at, c] = dot_last(sb_f[PR, at, :], u_up[c, :])
 
     def backward_tan(at):
         cotan_t = jnp.where(at_last, sb_d[TG, at, :], got["tan_down"][...])
         sb_d[TG, at, :] = cotan_t
         grad_t = sf_d[PU, at, :]
         for c in chunks:
-            grad_act_t = dot_last(cotan_t, w_down[c, :]) + sf_f[GV, at, c]
+            grad_act_t = dot(cotan_t, t_down[:, c]) + sf_f[GV, at, c]
             grad_pre_t = grad_act_t * sf_f[SLOPE, at, c] + sf_f[CC, at, c] * sf_f[TY, at, c]
             grad_pre_tb = grad_pre_t.astype(bf16)
             sb_f[TP, at, c] = grad_pre_tb
-            grad_t = grad_t + dot_last(grad_pre_tb, w_up[:, c])
+            grad_t = grad_t + dot(grad_pre_tb, t_up[c, :])
         normed, normed_t, inverse = sf_d[XH, at, :], sf_d[TXF, at, :], narrow(INV, at)
         along_t = mean(grad_t * normed + sf_d[QN, at, :] * normed_t)
         inner = grad_t - mean(grad_t) - normed_t * narrow(M1, at) - normed * along_t
@@ -293,18 +297,39 @@
             def _():
                 put_down[...] = result
 
-    if plan.backward_tan(t):
+    if "tan_down" in waves:
         when_due(t - lag - (2 * layers - 1 - stage), backward_tan)
-    if plan.forward_tan(t):
+    if "tan_up" in waves:
         when_due(t - lag - stage, forward_tan)
-    if plan.backward(t):
+    if "down" in waves:
         when_due(t - (2 * layers - 1 - stage), backward)
-    if plan.forward(t):
+    if "up" in waves:
         when_due(t - stage, forward)
-    if plan.ready_forward(t):
-        pl.when(stage == t - (lag - 1))(ready_forward)
-    if plan.ready_backward(t):
-        pl.when(stage == 2 * layers - 2 + lag - t)(ready_backward)
+    if with_probes:
+        group = pieces // 2 * rows
+        for due, work in ((plan.ready_forward(t), ready_forward), (plan.ready_backward(t), ready_backward)):
+            for layer, half in due:
+                at = slice(half * group, (half + 1) * group)
+                pl.when(stage == layer)(functools.partial(work, at))
+
+
+def transposed(arrays):
+    count = len(arrays)
+
+    def kernel(*refs):
+        for source, target in zip(refs[:count], refs[count:]):
+            for c in range(0, source.shape[0], 256):
+                target[:, c : c + 256] = source[c : c + 256, :].T
+
+    return pl.pallas_call(
+        kernel,
+        out_shape=tuple(pltpu.VMEM(a.shape[::-1], a.dtype) for a in arrays),
+        in_specs=[IN_VMEM] * count,
+        out_specs=(IN_VMEM,) * count,
+        compiler_params=pltpu.CompilerParams(vmem_limit_bytes=4 << 20),
+        cost_estimate=pl.CostEstimate(flops=1 << 30, bytes_accessed=1 << 24, transcendentals=0),
+        name="transposed",
+    )(*[vmem(a) for a in arrays])
 
 
 BATCHES = ((4,), (3, 5), (2, 6), (1, 7, 0))
@@ -445,7 +470,9 @@
     blocks = [(own, 0, False), (swap(own), 0, True)]
     halves = []
 
-    held = load((w_up[0], w_down[0], embedded, targets))
+    weights, ends = [], load((w_up[0], w_down[0], embedded, targets))
+    weights, ends = list(ends[:2]), list(ends[2:])
+    turned = weights
     *state, nothing = blank(
         (
             ((4, tokens, width), bf16),
@@ -459,17 +486,17 @@
     probes = None
     got = {"up": nothing}
     packet = pltpu.VMEM((rows, width), bf16)
-    ring_ticks = {0: 1, 1: 2, 2: 3, 3: 4}
-    for t in range(plan.ticks):
-        if t == LAG - 1:
-            probes = assemble(blocks, halves, groups, part, hidden)
-        waves = plan.waves(t)
+
+    def keep(arrived, step):
+        for array, away in zip(arrived, (-step, step)):
+            blocks.extend([(array, away, False), (swap(array), away, True)])
+
+    def part_of_tick(t, waves, with_probes, got, state):
         ways = [way for way in ("up", "down") if sends(waves, way)]
-        with_probes = plan.ready_forward(t) or plan.ready_backward(t)
-        operands = list(state) + list(held) + (list(probes) if with_probes else [])
+        operands = list(state) + weights + list(turned) + ends + (list(probes) if with_probes else [])
         operands += [got.get(name, nothing) for name in waves]
         outs = pl.pallas_call(
-            functools.partial(tick_kernel, plan, t, with_probes, loss_scale, rows, width, hidden),
+            functools.partial(tick_kernel, plan, t, waves, with_probes, loss_scale, rows, width, hidden),
             out_shape=tuple(pltpu.VMEM(s.shape, s.dtype) for s in state) + (packet,) * len(ways),
             in_specs=[IN_VMEM] * len(operands),
             out_specs=(IN_VMEM,) * (5 + len(ways)),
@@ -479,22 +506,42 @@
             name="tick",
         )(*[vmem(o) for o in operands])
         state, sent = outs[:5], dict(zip(ways, outs[5:]))
-        got = {
+        arrived = {
             name: lax.ppermute(sent[name.removeprefix("tan_")], "pipe", edges)
             for name, edges in waves.items()
             if edges
         }
-        if t in ring_ticks:
-            step = ring_ticks[t]
-            got["up"], moving[0], moving[1] = lax.optimization_barrier((got["up"], *moving))
-            if step < 4:
-                arrived = moving
-                moving = ring(arrived if step < 3 else [arrived[0][0], arrived[1][1]])
-                for array, away in zip(arrived, (-step, step)):
-                    blocks += [(array, away, False), (swap(array), away, True)]
-            else:
-                for i, array in enumerate(moving):
-                    halves += [(array, i, step, False), (swap(array), i, step, True)]
+        return state, arrived
+
+    for t in range(plan.ticks):
+        waves = plan.waves(t)
+        arrived = {}
+        ready = bool(plan.ready_forward(t) or plan.ready_backward(t))
+        leading = {name: edges for name, edges in waves.items() if name.startswith("tan_")}
+        following = {name: edges for name, edges in waves.items() if name not in leading}
+        if leading:
+            state, more = part_of_tick(t, leading, False, got, state)
+            arrived.update(more)
+        if following or ready:
+            state, more = part_of_tick(t, following, ready, got, state)
+            arrived.update(more)
+        got = arrived
+        if t == 0:
+            got["up"], *moving = lax.optimization_barrier((got["up"], *moving))
+            moved, moving = moving, ring(moving)
+            keep(moved, 1)
+        if t == 1:
+            got["up"], *moving = lax.optimization_barrier((got["up"], *moving))
+            moved, moving = moving, ring(moving)
+            keep(moved, 2)
+            weights[0], moved[0] = lax.optimization_barrier((weights[0], moved[0]))
+            turned = transposed(weights)
+            *turned, moving[0], moving[1] = lax.optimization_barrier((*turned, *moving))
+            moved, moving = moving, ring([moving[0][0], moving[1][1]])
+            keep(moved, 3)
+            for i, array in enumerate(moving):
+                halves += [(array, i, 4, False), (swap(array), i, 4, True)]
+            probes = assemble(blocks, halves, groups, part, hidden)
 
     mine, theirs = curvature(state[0], state[1], groups)
     summed = scatter(mine, theirs, groups, hidden)

time: 499 us -> 497 us (level)
  Pallas kernels: 71.4 us -> 91.4 us
  starting transfers between devices: 136 us -> 120 us
    pallas_call x42 -> x72, Pallas kernels: 61.1 us -> 81.2 us  [the longest x71 78.7 us: part_of_tick(): pl.pallas_call(functools.partial(tick_kernel, plan, t, waves, with_probes...]
    ppermute x72, waiting for transfers between devices: 204 us -> 186 us  [part_of_tick(): lax.ppermute(sent[name.removeprefix('tan_')], 'pipe', edges)]
    ppermute x72, starting transfers between devices: 106 us -> 89.5 us  [part_of_tick(): lax.ppermute(sent[name.removeprefix('tan_')], 'pipe', edges)]
    ppermute x4, waiting for transfers between devices: 6.94 us -> 15.9 us  [ring(): lax.ppermute(both[1], 'dp', behind)]
  transfers between devices with their start and end apart: 101 -> 101, of which waited for: 36 -> 32; matrix products, arithmetic and copies ran while one was open for 0% -> 0% of each run, Pallas kernels for 2% -> 17%
where the time goes in v5:
time: 497 us; the launch traced here: 489 us
  waiting for transfers between devices  271 us (55%)
  starting transfers between devices  120 us (24%)
  Pallas kernels  91.4 us (18%)
    ppermute x72, waiting for transfers between devices, part_of_tick(): lax.ppermute(sent[name.removeprefix('tan_')], 'pipe', edges)  186 us
    ppermute x72, starting transfers between devices, part_of_tick(): lax.ppermute(sent[name.removeprefix('tan_')], 'pipe', edges)  89.5 us
    pallas_call x71, Pallas kernels, part_of_tick(): pl.pallas_call(functools.partial(tick_kernel, plan, t, waves, with_probes...  78.7 us
    ppermute x3, waiting for transfers between devices, scatter(): from_behind = lax.ppermute(up, 'dp', ahead)  30.3 us
    ppermute x4, waiting for transfers between devices, ring(): lax.ppermute(both[0], 'dp', ahead)  24.9 us
    ppermute x4, waiting for transfers between devices, ring(): lax.ppermute(both[1], 'dp', behind)  15.9 us
    ppermute x4, starting transfers between devices, ring(): lax.ppermute(both[1], 'dp', behind)  15.4 us
    ppermute x3, starting transfers between devices, scatter(): from_ahead = lax.ppermute(down, 'dp', behind)  9.98 us
  transfers between devices with their start and end apart: 101, of which 32 were waited for; matrix products, arithmetic and copies ran while one was open for 0% of the time, Pallas kernels for 17%

profile of v5, /device:TPU:6, one launch (start us, length us, event | category | flops | bytes accessed | tf_op | source)
XLA Modules:
  0.0 489.3 jit_solution(11343601128791085884)
XLA Ops:
  2.6 5.9 %collective-permute-start.2 = (bf16[2,64,2048]{2,1,0:T(8,128)(2,1)S(1)}, bf16[2,64,2048]{2,1,0:T(8,128)(2,1)S(1)}, u32[]{:S(2)}, u32[]{:S(2)}) collective-permute-start(bf16[2,64,2048]{2,1,0:T(8,128)(2,1)S(1)} %constant_dynamic-update-slice_fusion.refs_0_), channel_id=1, source_target_pairs={{0,14},{1,15},{2,0},{3,1},{4,2},{5,3},{6,4},{7,5},{8,6},{9,7},{10,... | collective-permute-start | bytes 1572872 | tf_op jit(solution)/shard_map/ppermute | solution.py:466
  8.5 3.5 load.1
  12.8 6.9 %collective-permute-done.2.refs_4_ = bf16[2,64,2048]{2,1,0:T(8,128)(2,1)S(1)} collective-permute-done((bf16[2,64,2048]{2,1,0:T(8,128)(2,1)S(1)}, bf16[2,64,2048]{2,1,0:T(8,128)(2,1)S(1)}, u32[]{:S(2)}, u32[]{:S(2)}) %collective-permute-start.2) | collective-permute-done | bytes 524320 | tf_op jit(solution)/shard_map/ppermute | solution.py:466
  19.7 3.4 collective-permute-done.1.refs_2_
  23.1 3.2 collective-permute-start.5
  27.0 11.6 %collective-permute-done.4.refs_6_ = bf16[2,64,2048]{2,1,0:T(8,128)(2,1)S(1)} collective-permute-done((bf16[2,64,2048]{2,1,0:T(8,128)(2,1)S(1)}, bf16[2,64,2048]{2,1,0:T(8,128)(2,1)S(1)}, u32[]{:S(2)}, u32[]{:S(2)}) %collective-permute-start.4) | collective-permute-done | bytes 524320 | tf_op jit(solution)/shard_map/ppermute | solution.py:466
  38.7 2.9 collective-permute-start.7
  42.0 2.4 transposed.1
  44.5 9.0 %collective-permute-done.7.refs_12_ = bf16[2,64,2048]{2,1,0:T(8,128)(2,1)S(1)} collective-permute-done((bf16[2,64,2048]{2,1,0:T(8,128)(2,1)S(1)}, bf16[2,64,2048]{2,1,0:T(8,128)(2,1)S(1)}, u32[]{:S(2)}, u32[]{:S(2)}) %collective-permute-start.7) | collective-permute-done | bytes 524320 | tf_op jit(solution)/shard_map/ppermute | solution.py:466
  53.5 3.4 collective-permute-done.6.refs_10_
  59.1 3.3 collective-permute-start.17
  62.4 6.4 %collective-permute-done.15.refs_14_ = bf16[64,2048]{1,0:T(8,128)(2,1)S(1)} collective-permute-done((bf16[64,2048]{1,0:T(8,128)(2,1)S(1)}, bf16[64,2048]{1,0:T(8,128)(2,1)S(1)}, u32[]{:S(2)}, u32[]{:S(2)}) %collective-permute-start.15) | collective-permute-done | bytes 262176 | tf_op jit(solution)/shard_map/ppermute | solution.py:466
  75.0 5.2 %collective-permute-done.19.refs_13_ = bf16[32,1024]{1,0:T(8,128)(2,1)S(1)} collective-permute-done((bf16[32,1024]{1,0:T(8,128)(2,1)S(1)}, bf16[32,1024]{1,0:T(8,128)(2,1)S(1)}, u32[]{:S(2)}, u32[]{:S(2)}) %collective-permute-start.19) | collective-permute-done | bytes 65568 | tf_op jit(solution)/shard_map/ppermute | solution.py:510
  80.2 2.5 tick.75
  85.3 3.5 collective-permute-done.21.refs_13_
  91.0 4.0 collective-permute-start.23
  96.3 3.5 collective-permute-done.23.refs_13_
  99.8 4.2 tick.79
  112.3 6.1 %collective-permute-start.27 = (bf16[32,1024]{1,0:T(8,128)(2,1)S(1)}, bf16[32,1024]{1,0:T(8,128)(2,1)S(1)}, u32[]{:S(2)}, u32[]{:S(2)}) collective-permute-start(bf16[32,1024]{1,0:T(8,128)(2,1)S(1)} %get-tuple-element.573), channel_id=1, source_target_pairs={{96,112},{80,96},{64,80},{48,64},{97,113},{81,97},{65,81},{49,65},... | collective-permute-start | bytes 196616 | tf_op jit(solution)/shard_map/ppermute | solution.py:510
  128.7 4.5 collective-permute-start.30
  137.1 6.4 %collective-permute-start.32 = (bf16[32,1024]{1,0:T(8,128)(2,1)S(1)}, bf16[32,1024]{1,0:T(8,128)(2,1)S(1)}, u32[]{:S(2)}, u32[]{:S(2)}) collective-permute-start(bf16[32,1024]{1,0:T(8,128)(2,1)S(1)} %get-tuple-element.603), channel_id=1, source_target_pairs={{96,112},{80,96},{64,80},{48,64},{97,113},{81,97},{65,81},{49,65},... | collective-permute-start | bytes 196616 | tf_op jit(solution)/shard_map/ppermute | solution.py:510
  150.0 4.4 tick.94
  158.0 5.1 %tick.99 = (bf16[4,128,1024]{2,1,0:T(8,128)(2,1)S(1)}, bf16[4,128,2048]{2,1,0:T(8,128)(2,1)S(1)}, f32[6,128,1024]{2,1,0:T(8,128)S(1)}, f32[6,128,2048]{2,1,0:T(8...) custom-call(bf16[4,128,1024]{2,1,0:T(8,128)(2,1)S(1)} %get-tuple-ele, ...), custom_call_target="tpu_custom_call", output_to_operand_aliasing={{0}: (0, {}), {1}: (1, {}), {2}: (2, {}), {3}: (3, {}), {4}... | custom-call | flops 1073741824 | bytes 8388608 | tf_op jit(solution)/shard_map/tick/pallas_call | solution.py:498
  166.7 5.2 %tick.103 = (bf16[4,128,1024]{2,1,0:T(8,128)(2,1)S(1)}, bf16[4,128,2048]{2,1,0:T(8,128)(2,1)S(1)}, f32[6,128,1024]{2,1,0:T(8,128)S(1)}, f32[6,128,2048]{2,1,0:T(...) custom-call(bf16[4,128,1024]{2,1,0:T(8,128)(2,1)S(1)} %get-tuple-ele, ...), custom_call_target="tpu_custom_call", output_to_operand_aliasing={{0}: (0, {}), {1}: (1, {}), {2}: (2, {}), {3}: (3, {}), {4}... | custom-call | flops 1073741824 | bytes 8388608 | tf_op jit(solution)/shard_map/tick/pallas_call | solution.py:498
  176.1 4.2 tick.107
  183.8 5.8 %tick.111 = (bf16[4,128,1024]{2,1,0:T(8,128)(2,1)S(1)}, bf16[4,128,2048]{2,1,0:T(8,128)(2,1)S(1)}, f32[6,128,1024]{2,1,0:T(8,128)S(1)}, f32[6,128,2048]{2,1,0:T(...) custom-call(bf16[4,128,1024]{2,1,0:T(8,128)(2,1)S(1)} %get-tuple-ele, ...), custom_call_target="tpu_custom_call", output_to_operand_aliasing={{0}: (0, {}), {1}: (1, {}), {2}: (2, {}), {3}: (3, {}), {4}... | custom-call | flops 1073741824 | bytes 8388608 | tf_op jit(solution)/shard_map/tick/pallas_call | solution.py:498
  193.2 4.9 tick.116
  201.6 5.8 %tick.121 = (bf16[4,128,1024]{2,1,0:T(8,128)(2,1)S(1)}, bf16[4,128,2048]{2,1,0:T(8,128)(2,1)S(1)}, f32[6,128,1024]{2,1,0:T(8,128)S(1)}, f32[6,128,2048]{2,1,0:T(...) custom-call(bf16[4,128,1024]{2,1,0:T(8,128)(2,1)S(1)} %get-tuple-ele, ...), custom_call_target="tpu_custom_call", output_to_operand_aliasing={{0}: (0, {}), {1}: (1, {}), {2}: (2, {}), {3}: (3, {}), {4}... | custom-call | flops 1073741824 | bytes 8388608 | tf_op jit(solution)/shard_map/tick/pallas_call | solution.py:498
  210.9 99.7 %collective-permute-done.73.refs_13_ = bf16[32,1024]{1,0:T(8,128)(2,1)S(1)} collective-permute-done((bf16[32,1024]{1,0:T(8,128)(2,1)S(1)}, bf16[32,1024]{1,0:T(8,128)(2,1)S(1)}, u32[]{:S(2)}, u32[]{:S(2)}) %collective-permute-start.73) | collective-permute-done | bytes 65568 | tf_op jit(solution)/shard_map/ppermute | solution.py:510
  315.2 7.8 %collective-permute-done.75.refs_13_ = bf16[32,1024]{1,0:T(8,128)(2,1)S(1)} collective-permute-done((bf16[32,1024]{1,0:T(8,128)(2,1)S(1)}, bf16[32,1024]{1,0:T(8,128)(2,1)S(1)}, u32[]{:S(2)}, u32[]{:S(2)}) %collective-permute-start.75) | collective-permute-done | bytes 65568 | tf_op jit(solution)/shard_map/ppermute | solution.py:510
  328.3 34.9 %collective-permute-done.77.refs_13_ = bf16[32,1024]{1,0:T(8,128)(2,1)S(1)} collective-permute-done((bf16[32,1024]{1,0:T(8,128)(2,1)S(1)}, bf16[32,1024]{1,0:T(8,128)(2,1)S(1)}, u32[]{:S(2)}, u32[]{:S(2)}) %collective-permute-start.77) | collective-permute-done | bytes 65568 | tf_op jit(solution)/shard_map/ppermute | solution.py:510
  363.3 4.0 tick.129
  373.2 2.4 collective-permute-done.79.refs_13_
  377.5 2.5 collective-permute-start.81
  380.0 2.4 tick.132
  398.7 2.3 collective-permute-done.84.refs_11_
  404.9 6.3 %collective-permute-done.86.refs_11_ = bf16[32,1024]{1,0:T(8,128)(2,1)S(1)} collective-permute-done((bf16[32,1024]{1,0:T(8,128)(2,1)S(1)}, bf16[32,1024]{1,0:T(8,128)(2,1)S(1)}, u32[]{:S(2)}, u32[]{:S(2)}) %collective-permute-start.86) | collective-permute-done | bytes 65568 | tf_op jit(solution)/shard_map/ppermute | solution.py:510
  413.3 6.3 %collective-permute-done.87.refs_11_ = bf16[32,1024]{1,0:T(8,128)(2,1)S(1)} collective-permute-done((bf16[32,1024]{1,0:T(8,128)(2,1)S(1)}, bf16[32,1024]{1,0:T(8,128)(2,1)S(1)}, u32[]{:S(2)}, u32[]{:S(2)}) %collective-permute-start.87) | collective-permute-done | bytes 65568 | tf_op jit(solution)/shard_map/ppermute | solution.py:510
  421.5 6.3 %collective-permute-done.88.refs_11_ = bf16[32,1024]{1,0:T(8,128)(2,1)S(1)} collective-permute-done((bf16[32,1024]{1,0:T(8,128)(2,1)S(1)}, bf16[32,1024]{1,0:T(8,128)(2,1)S(1)}, u32[]{:S(2)}, u32[]{:S(2)}) %collective-permute-start.88) | collective-permute-done | bytes 65568 | tf_op jit(solution)/shard_map/ppermute | solution.py:510
  427.9 5.7 %curvature.1 = (bf16[1,64,4096]{2,1,0:T(8,128)(2,1)S(1)}, bf16[2,64,4096]{2,1,0:T(8,128)(2,1)S(1)}, bf16[2,64,4096]{2,1,0:T(8,128)(2,1)S(1)}, bf16[3,64,4096]{2,...) custom-call(bf16[4,128,1024]{2,1,0:T(8,128)(2,1)S(1)} %get-tuple-ele, ...), custom_call_target="tpu_custom_call" | custom-call | tf_op jit(solution)/shard_map/curvature/pallas_call | solution.py:364
  436.0 3.2 collective-permute-start.97
  439.5 6.3 %collective-permute-done.93 = bf16[64,2048]{1,0:T(8,128)(2,1)S(1)} collective-permute-done((bf16[64,2048]{1,0:T(8,128)(2,1)S(1)}, bf16[64,2048]{1,0:T(8,128)(2,1)S(1)}, u32[]{:S(2)}, u32[]{:S(2)}) %collective-permute-start.93) | collective-permute-done | bytes 262176 | tf_op jit(solution)/shard_map/ppermute | solution.py:429
  446.1 3.5 collective-permute-start.98
  449.8 10.8 %collective-permute-done.94 = bf16[64,4096]{1,0:T(8,128)(2,1)S(1)} collective-permute-done((bf16[64,4096]{1,0:T(8,128)(2,1)S(1)}, bf16[64,4096]{1,0:T(8,128)(2,1)S(1)}, u32[]{:S(2)}, u32[]{:S(2)}) %collective-permute-start.94) | collective-permute-done | bytes 524320 | tf_op jit(solution)/shard_map/ppermute | solution.py:436
  461.0 3.3 collective-permute-start.99
  464.8 9.9 %collective-permute-done.95 = bf16[64,4096]{1,0:T(8,128)(2,1)S(1)} collective-permute-done((bf16[64,4096]{1,0:T(8,128)(2,1)S(1)}, bf16[64,4096]{1,0:T(8,128)(2,1)S(1)}, u32[]{:S(2)}, u32[]{:S(2)}) %collective-permute-start.95) | collective-permute-done | bytes 524320 | tf_op jit(solution)/shard_map/ppermute | solution.py:436
  475.0 3.2 collective-permute-start.100
  478.2 9.5 %collective-permute-done.96 = bf16[64,4096]{1,0:T(8,128)(2,1)S(1)} collective-permute-done((bf16[64,4096]{1,0:T(8,128)(2,1)S(1)}, bf16[64,4096]{1,0:T(8,128)(2,1)S(1)}, u32[]{:S(2)}, u32[]{:S(2)}) %collective-permute-start.96) | collective-permute-done | bytes 524320 | tf_op jit(solution)/shard_map/ppermute | solution.py:441
  (252 shorter events, 118.6 us)
Async XLA Ops:
  2.6 17.1 %collective-permute-start.2 = (bf16[2,64,2048]{2,1,0:T(8,128)(2,1)S(1)}, bf16[2,64,2048]{2,1,0:T(8,128)(2,1)S(1)}, u32[]{:S(2)}, u32[]{:S(2)}) collective-permute-start(bf16[2,64,2048]{2,1,0:T(8,128)(2,1)S(1)} %constant_dynamic-update-slice_fusion.refs_0_), channel_id=1, source_target_pairs={{0,14},{1,15},{2,0},{3,1},{4,2},{5,3},{6,4},{7,5},{8,6},{9,7},{10,... | collective-permute-start | bytes 1572872 | tf_op jit(solution)/shard_map/ppermute | solution.py:466
  8.5 14.6 %collective-permute-start.1 = (bf16[2,64,2048]{2,1,0:T(8,128)(2,1)S(1)}, bf16[2,64,2048]{2,1,0:T(8,128)(2,1)S(1)}, u32[]{:S(2)}, u32[]{:S(2)}) collective-permute-start(bf16[2,64,2048]{2,1,0:T(8,128)(2,1)S(1)} %constant_dynamic-update-slice_fusion.refs_0_), channel_id=1, source_target_pairs={{0,2},{1,3},{2,4},{3,5},{4,6},{5,7},{6,8},{7,9},{8,10},{9,11},{10,... | collective-permute-start | bytes 1572872 | tf_op jit(solution)/shard_map/ppermute | solution.py:466
  8.5 14.6 %collective-permute-start.8 = (bf16[2,64,2048]{2,1,0:T(8,128)(2,1)S(1)}, bf16[2,64,2048]{2,1,0:T(8,128)(2,1)S(1)}, u32[]{:S(2)}, u32[]{:S(2)}) collective-permute-start(bf16[2,64,2048]{2,1,0:T(8,128)(2,1)S(1)} %constant_dynamic-update-slice_fusion.refs_0_), channel_id=1, source_target_pairs={{0,1},{1,0},{2,3},{3,2},{4,5},{5,4},{6,7},{7,6},{8,9},{9,8},{10,11... | collective-permute-start | bytes 1572872 | tf_op jit(solution)/shard_map/ppermute | solution.py:462
  23.1 15.5 %collective-permute-start.4 = (bf16[2,64,2048]{2,1,0:T(8,128)(2,1)S(1)}, bf16[2,64,2048]{2,1,0:T(8,128)(2,1)S(1)}, u32[]{:S(2)}, u32[]{:S(2)}) collective-permute-start(bf16[2,64,2048]{2,1,0:T(8,128)(2,1)S(1)} %collective-permute-done.1.refs_2_), channel_id=1, source_target_pairs={{0,2},{1,3},{2,4},{3,5},{4,6},{5,7},{6,8},{7,9},{8,10},{9,11},{10,... | collective-permute-start | bytes 1572872 | tf_op jit(solution)/shard_map/ppermute | solution.py:466
  23.1 15.5 %collective-permute-start.5 = (bf16[2,64,2048]{2,1,0:T(8,128)(2,1)S(1)}, bf16[2,64,2048]{2,1,0:T(8,128)(2,1)S(1)}, u32[]{:S(2)}, u32[]{:S(2)}) collective-permute-start(bf16[2,64,2048]{2,1,0:T(8,128)(2,1)S(1)} %collective-permute-done.2.refs_4_), channel_id=1, source_target_pairs={{0,14},{1,15},{2,0},{3,1},{4,2},{5,3},{6,4},{7,5},{8,6},{9,7},{10,... | collective-permute-start | bytes 1572872 | tf_op jit(solution)/shard_map/ppermute | solution.py:466
  26.4 12.3 %collective-permute-start.10 = (bf16[2,64,2048]{2,1,0:T(8,128)(2,1)S(1)}, bf16[2,64,2048]{2,1,0:T(8,128)(2,1)S(1)}, u32[]{:S(2)}, u32[]{:S(2)}) collective-permute-start(bf16[2,64,2048]{2,1,0:T(8,128)(2,1)S(1)} %collective-permute-done.2.refs_4_), channel_id=1, source_target_pairs={{0,1},{1,0},{2,3},{3,2},{4,5},{5,4},{6,7},{7,6},{8,9},{9,8},{10,11... | collective-permute-start | bytes 1572872 | tf_op jit(solution)/shard_map/ppermute | solution.py:462
  38.7 14.8 %collective-permute-start.7 = (bf16[2,64,2048]{2,1,0:T(8,128)(2,1)S(1)}, bf16[2,64,2048]{2,1,0:T(8,128)(2,1)S(1)}, u32[]{:S(2)}, u32[]{:S(2)}) collective-permute-start(bf16[2,64,2048]{2,1,0:T(8,128)(2,1)S(1)} %collective-permute-done.5.refs_8_), channel_id=1, source_target_pairs={{0,14},{1,15},{2,0},{3,1},{4,2},{5,3},{6,4},{7,5},{8,6},{9,7},{10,... | collective-permute-start | bytes 1572872 | tf_op jit(solution)/shard_map/ppermute | solution.py:466
  41.6 15.3 %collective-permute-start.6 = (bf16[2,64,2048]{2,1,0:T(8,128)(2,1)S(1)}, bf16[2,64,2048]{2,1,0:T(8,128)(2,1)S(1)}, u32[]{:S(2)}, u32[]{:S(2)}) collective-permute-start(bf16[2,64,2048]{2,1,0:T(8,128)(2,1)S(1)} %collective-permute-done.4.refs_6_), channel_id=1, source_target_pairs={{0,2},{1,3},{2,4},{3,5},{4,6},{5,7},{6,8},{7,9},{8,10},{9,11},{10,... | collective-permute-start | bytes 1572872 | tf_op jit(solution)/shard_map/ppermute | solution.py:466
  41.6 15.3 %collective-permute-start.12 = (bf16[2,64,2048]{2,1,0:T(8,128)(2,1)S(1)}, bf16[2,64,2048]{2,1,0:T(8,128)(2,1)S(1)}, u32[]{:S(2)}, u32[]{:S(2)}) collective-permute-start(bf16[2,64,2048]{2,1,0:T(8,128)(2,1)S(1)} %collective-permute-done.5.refs_8_), channel_id=1, source_target_pairs={{0,1},{1,0},{2,3},{3,2},{4,5},{5,4},{6,7},{7,6},{8,9},{9,8},{10,11... | collective-permute-start | bytes 1572872 | tf_op jit(solution)/shard_map/ppermute | solution.py:462
  58.8 10.0 %collective-permute-start.14 = (bf16[2,64,2048]{2,1,0:T(8,128)(2,1)S(1)}, bf16[2,64,2048]{2,1,0:T(8,128)(2,1)S(1)}, u32[]{:S(2)}, u32[]{:S(2)}) collective-permute-start(bf16[2,64,2048]{2,1,0:T(8,128)(2,1)S(1)} %collective-permute-done.7.refs_12_), channel_id=1, source_target_pairs={{0,1},{1,0},{2,3},{3,2},{4,5},{5,4},{6,7},{7,6},{8,9},{9,8},{10,11... | collective-permute-start | bytes 1572872 | tf_op jit(solution)/shard_map/ppermute | solution.py:462
  59.0 9.9 %collective-permute-start.15 = (bf16[64,2048]{1,0:T(8,128)(2,1)S(1)}, bf16[64,2048]{1,0:T(8,128)(2,1)S(1)}, u32[]{:S(2)}, u32[]{:S(2)}) collective-permute-start(bf16[64,2048]{1,0:T(8,128)(2,1)S(1)} %slice_bitcast_fusion.8), channel_id=1, source_target_pairs={{0,2},{1,3},{2,4},{3,5},{4,6},{5,7},{6,8},{7,9},{8,10},{9,11},{10,... | collective-permute-start | bytes 786440 | tf_op jit(solution)/shard_map/ppermute | solution.py:466
  59.1 9.8 %collective-permute-start.17 = (bf16[64,2048]{1,0:T(8,128)(2,1)S(1)}, bf16[64,2048]{1,0:T(8,128)(2,1)S(1)}, u32[]{:S(2)}, u32[]{:S(2)}) collective-permute-start(bf16[64,2048]{1,0:T(8,128)(2,1)S(1)} %slice_bitcast_fusion.7), channel_id=1, source_target_pairs={{0,14},{1,15},{2,0},{3,1},{4,2},{5,3},{6,4},{7,5},{8,6},{9,7},{10,... | collective-permute-start | bytes 786440 | tf_op jit(solution)/shard_map/ppermute | solution.py:466
  74.3 10.3 %collective-permute-start.20 = (bf16[32,1024]{1,0:T(8,128)(2,1)S(1)}, bf16[32,1024]{1,0:T(8,128)(2,1)S(1)}, u32[]{:S(2)}, u32[]{:S(2)}) collective-permute-start(bf16[32,1024]{1,0:T(8,128)(2,1)S(1)} %get-tuple-element.531), channel_id=1, source_target_pairs={{0,16},{1,17},{2,18},{3,19},{4,20},{5,21},{6,22},{7,23},{8,24},{9,... | collective-permute-start | bytes 196616 | tf_op jit(solution)/shard_map/ppermute | solution.py:510
  84.7 10.4 %collective-permute-start.22 = (bf16[32,1024]{1,0:T(8,128)(2,1)S(1)}, bf16[32,1024]{1,0:T(8,128)(2,1)S(1)}, u32[]{:S(2)}, u32[]{:S(2)}) collective-permute-start(bf16[32,1024]{1,0:T(8,128)(2,1)S(1)} %get-tuple-element.543), channel_id=1, source_target_pairs={{16,32},{0,16},{17,33},{1,17},{18,34},{2,18},{19,35},{3,19},{20,36... | collective-permute-start | bytes 196616 | tf_op jit(solution)/shard_map/ppermute | solution.py:510
  91.0 8.8 %collective-permute-start.23 = (bf16[32,1024]{1,0:T(8,128)(2,1)S(1)}, bf16[32,1024]{1,0:T(8,128)(2,1)S(1)}, u32[]{:S(2)}, u32[]{:S(2)}) collective-permute-start(bf16[32,1024]{1,0:T(8,128)(2,1)S(1)} %get-tuple-element.549), channel_id=1, source_target_pairs={{64,80},{48,64},{32,48},{16,32},{65,81},{49,65},{33,49},{17,33},{6... | collective-permute-start | bytes 196616 | tf_op jit(solution)/shard_map/ppermute | solution.py:510
  95.0 10.9 %collective-permute-start.24 = (bf16[32,1024]{1,0:T(8,128)(2,1)S(1)}, bf16[32,1024]{1,0:T(8,128)(2,1)S(1)}, u32[]{:S(2)}, u32[]{:S(2)}) collective-permute-start(bf16[32,1024]{1,0:T(8,128)(2,1)S(1)} %get-tuple-element.555), channel_id=1, source_target_pairs={{32,48},{16,32},{0,16},{33,49},{17,33},{1,17},{34,50},{18,34},{2,1... | collective-permute-start | bytes 196616 | tf_op jit(solution)/shard_map/ppermute | solution.py:510
  108.2 10.3 %collective-permute-start.26 = (bf16[32,1024]{1,0:T(8,128)(2,1)S(1)}, bf16[32,1024]{1,0:T(8,128)(2,1)S(1)}, u32[]{:S(2)}, u32[]{:S(2)}) collective-permute-start(bf16[32,1024]{1,0:T(8,128)(2,1)S(1)} %get-tuple-element.567), channel_id=1, source_target_pairs={{48,64},{32,48},{16,32},{0,16},{49,65},{33,49},{17,33},{1,17},{50,... | collective-permute-start | bytes 196616 | tf_op jit(solution)/shard_map/ppermute | solution.py:510
  112.3 10.1 %collective-permute-start.27 = (bf16[32,1024]{1,0:T(8,128)(2,1)S(1)}, bf16[32,1024]{1,0:T(8,128)(2,1)S(1)}, u32[]{:S(2)}, u32[]{:S(2)}) collective-permute-start(bf16[32,1024]{1,0:T(8,128)(2,1)S(1)} %get-tuple-element.573), channel_id=1, source_target_pairs={{96,112},{80,96},{64,80},{48,64},{97,113},{81,97},{65,81},{49,65},... | collective-permute-start | bytes 196616 | tf_op jit(solution)/shard_map/ppermute | solution.py:510
  124.6 8.6 %collective-permute-start.29 = (bf16[32,1024]{1,0:T(8,128)(2,1)S(1)}, bf16[32,1024]{1,0:T(8,128)(2,1)S(1)}, u32[]{:S(2)}, u32[]{:S(2)}) collective-permute-start(bf16[32,1024]{1,0:T(8,128)(2,1)S(1)} %get-tuple-element.585), channel_id=1, source_target_pairs={{112,128},{96,112},{80,96},{64,80},{113,129},{97,113},{81,97},{65,... | collective-permute-start | bytes 196616 | tf_op jit(solution)/shard_map/ppermute | solution.py:510
  133.5 10.0 %collective-permute-start.31 = (bf16[32,1024]{1,0:T(8,128)(2,1)S(1)}, bf16[32,1024]{1,0:T(8,128)(2,1)S(1)}, u32[]{:S(2)}, u32[]{:S(2)}) collective-permute-start(bf16[32,1024]{1,0:T(8,128)(2,1)S(1)} %get-tuple-element.597), channel_id=1, source_target_pairs={{128,144},{112,128},{96,112},{80,96},{129,145},{113,129},{97,113},... | collective-permute-start | bytes 196616 | tf_op jit(solution)/shard_map/ppermute | solution.py:510
  137.1 8.3 %collective-permute-start.32 = (bf16[32,1024]{1,0:T(8,128)(2,1)S(1)}, bf16[32,1024]{1,0:T(8,128)(2,1)S(1)}, u32[]{:S(2)}, u32[]{:S(2)}) collective-permute-start(bf16[32,1024]{1,0:T(8,128)(2,1)S(1)} %get-tuple-element.603), channel_id=1, source_target_pairs={{96,112},{80,96},{64,80},{48,64},{97,113},{81,97},{65,81},{49,65},... | collective-permute-start | bytes 196616 | tf_op jit(solution)/shard_map/ppermute | solution.py:510
  166.0 7.2 %collective-permute-start.49 = (bf16[32,1024]{1,0:T(8,128)(2,1)S(1)}, bf16[32,1024]{1,0:T(8,128)(2,1)S(1)}, u32[]{:S(2)}, u32[]{:S(2)}) collective-permute-start(bf16[32,1024]{1,0:T(8,128)(2,1)S(1)} %get-tuple-element.700), channel_id=1, source_target_pairs={{224,240},{208,224},{192,208},{176,192},{225,241},{209,225},{193,2... | collective-permute-start | bytes 196616 | tf_op jit(solution)/shard_map/ppermute | solution.py:510
  208.9 101.7 %collective-permute-start.73 = (bf16[32,1024]{1,0:T(8,128)(2,1)S(1)}, bf16[32,1024]{1,0:T(8,128)(2,1)S(1)}, u32[]{:S(2)}, u32[]{:S(2)}) collective-permute-start(bf16[32,1024]{1,0:T(8,128)(2,1)S(1)} %get-tuple-element.829), channel_id=1, source_target_pairs={{64,48},{80,64},{96,80},{112,96},{65,49},{81,65},{97,81},{113,97},... | collective-permute-start | bytes 196616 | tf_op jit(solution)/shard_map/ppermute | solution.py:510
  210.2 104.2 %collective-permute-start.74 = (bf16[32,1024]{1,0:T(8,128)(2,1)S(1)}, bf16[32,1024]{1,0:T(8,128)(2,1)S(1)}, u32[]{:S(2)}, u32[]{:S(2)}) collective-permute-start(bf16[32,1024]{1,0:T(8,128)(2,1)S(1)} %get-tuple-element.835), channel_id=1, source_target_pairs={{96,80},{112,96},{128,112},{144,128},{97,81},{113,97},{129,113},{1... | collective-permute-start | bytes 196616 | tf_op jit(solution)/shard_map/ppermute | solution.py:510
  312.5 10.5 %collective-permute-start.75 = (bf16[32,1024]{1,0:T(8,128)(2,1)S(1)}, bf16[32,1024]{1,0:T(8,128)(2,1)S(1)}, u32[]{:S(2)}, u32[]{:S(2)}) collective-permute-start(bf16[32,1024]{1,0:T(8,128)(2,1)S(1)} %get-tuple-element.841), channel_id=1, source_target_pairs={{48,32},{64,48},{80,64},{96,80},{49,33},{65,49},{81,65},{97,81},{5... | collective-permute-start | bytes 196616 | tf_op jit(solution)/shard_map/ppermute | solution.py:510
  314.5 12.5 %collective-permute-start.76 = (bf16[32,1024]{1,0:T(8,128)(2,1)S(1)}, bf16[32,1024]{1,0:T(8,128)(2,1)S(1)}, u32[]{:S(2)}, u32[]{:S(2)}) collective-permute-start(bf16[32,1024]{1,0:T(8,128)(2,1)S(1)} %get-tuple-element.847), channel_id=1, source_target_pairs={{80,64},{96,80},{112,96},{128,112},{81,65},{97,81},{113,97},{129,1... | collective-permute-start | bytes 196616 | tf_op jit(solution)/shard_map/ppermute | solution.py:510
  325.1 38.2 %collective-permute-start.77 = (bf16[32,1024]{1,0:T(8,128)(2,1)S(1)}, bf16[32,1024]{1,0:T(8,128)(2,1)S(1)}, u32[]{:S(2)}, u32[]{:S(2)}) collective-permute-start(bf16[32,1024]{1,0:T(8,128)(2,1)S(1)} %get-tuple-element.853), channel_id=1, source_target_pairs={{32,16},{48,32},{64,48},{80,64},{33,17},{49,33},{65,49},{81,65},{3... | collective-permute-start | bytes 196616 | tf_op jit(solution)/shard_map/ppermute | solution.py:510
  327.0 42.2 %collective-permute-start.78 = (bf16[32,1024]{1,0:T(8,128)(2,1)S(1)}, bf16[32,1024]{1,0:T(8,128)(2,1)S(1)}, u32[]{:S(2)}, u32[]{:S(2)}) collective-permute-start(bf16[32,1024]{1,0:T(8,128)(2,1)S(1)} %get-tuple-element.859), channel_id=1, source_target_pairs={{64,48},{80,64},{96,80},{112,96},{65,49},{81,65},{97,81},{113,97},... | collective-permute-start | bytes 196616 | tf_op jit(solution)/shard_map/ppermute | solution.py:510
  367.3 8.3 %collective-permute-start.79 = (bf16[32,1024]{1,0:T(8,128)(2,1)S(1)}, bf16[32,1024]{1,0:T(8,128)(2,1)S(1)}, u32[]{:S(2)}, u32[]{:S(2)}) collective-permute-start(bf16[32,1024]{1,0:T(8,128)(2,1)S(1)} %get-tuple-element.865), channel_id=1, source_target_pairs={{16,0},{32,16},{48,32},{64,48},{17,1},{33,17},{49,33},{65,49},{18,... | collective-permute-start | bytes 196616 | tf_op jit(solution)/shard_map/ppermute | solution.py:510
  371.2 8.8 %collective-permute-start.80 = (bf16[32,1024]{1,0:T(8,128)(2,1)S(1)}, bf16[32,1024]{1,0:T(8,128)(2,1)S(1)}, u32[]{:S(2)}, u32[]{:S(2)}) collective-permute-start(bf16[32,1024]{1,0:T(8,128)(2,1)S(1)} %get-tuple-element.871), channel_id=1, source_target_pairs={{48,32},{64,48},{80,64},{96,80},{49,33},{65,49},{81,65},{97,81},{5... | collective-permute-start | bytes 196616 | tf_op jit(solution)/shard_map/ppermute | solution.py:510
  377.5 8.3 %collective-permute-start.81 = (bf16[32,1024]{1,0:T(8,128)(2,1)S(1)}, bf16[32,1024]{1,0:T(8,128)(2,1)S(1)}, u32[]{:S(2)}, u32[]{:S(2)}) collective-permute-start(bf16[32,1024]{1,0:T(8,128)(2,1)S(1)} %get-tuple-element.877), channel_id=1, source_target_pairs={{16,0},{32,16},{48,32},{64,48},{17,1},{33,17},{49,33},{65,49},{18,... | collective-permute-start | bytes 196616 | tf_op jit(solution)/shard_map/ppermute | solution.py:510
  382.4 8.3 %collective-permute-start.82 = (bf16[32,1024]{1,0:T(8,128)(2,1)S(1)}, bf16[32,1024]{1,0:T(8,128)(2,1)S(1)}, u32[]{:S(2)}, u32[]{:S(2)}) collective-permute-start(bf16[32,1024]{1,0:T(8,128)(2,1)S(1)} %get-tuple-element.883), channel_id=1, source_target_pairs={{32,16},{48,32},{64,48},{80,64},{33,17},{49,33},{65,49},{81,65},{3... | collective-permute-start | bytes 196616 | tf_op jit(solution)/shard_map/ppermute | solution.py:510
  387.9 8.8 %collective-permute-start.83 = (bf16[32,1024]{1,0:T(8,128)(2,1)S(1)}, bf16[32,1024]{1,0:T(8,128)(2,1)S(1)}, u32[]{:S(2)}, u32[]{:S(2)}) collective-permute-start(bf16[32,1024]{1,0:T(8,128)(2,1)S(1)} %get-tuple-element.889), channel_id=1, source_target_pairs={{16,0},{32,16},{48,32},{64,48},{17,1},{33,17},{49,33},{65,49},{18,... | collective-permute-start | bytes 196616 | tf_op jit(solution)/shard_map/ppermute | solution.py:510
  392.7 8.3 %collective-permute-start.84 = (bf16[32,1024]{1,0:T(8,128)(2,1)S(1)}, bf16[32,1024]{1,0:T(8,128)(2,1)S(1)}, u32[]{:S(2)}, u32[]{:S(2)}) collective-permute-start(bf16[32,1024]{1,0:T(8,128)(2,1)S(1)} %get-tuple-element.895), channel_id=1, source_target_pairs={{16,0},{32,16},{48,32},{64,48},{17,1},{33,17},{49,33},{65,49},{18,... | collective-permute-start | bytes 196616 | tf_op jit(solution)/shard_map/ppermute | solution.py:510
  396.6 8.3 %collective-permute-start.85 = (bf16[32,1024]{1,0:T(8,128)(2,1)S(1)}, bf16[32,1024]{1,0:T(8,128)(2,1)S(1)}, u32[]{:S(2)}, u32[]{:S(2)}) collective-permute-start(bf16[32,1024]{1,0:T(8,128)(2,1)S(1)} %get-tuple-element.901), channel_id=1, source_target_pairs={{16,0},{32,16},{48,32},{64,48},{17,1},{33,17},{49,33},{65,49},{18,... | collective-permute-start | bytes 196616 | tf_op jit(solution)/shard_map/ppermute | solution.py:510
  402.9 8.3 %collective-permute-start.86 = (bf16[32,1024]{1,0:T(8,128)(2,1)S(1)}, bf16[32,1024]{1,0:T(8,128)(2,1)S(1)}, u32[]{:S(2)}, u32[]{:S(2)}) collective-permute-start(bf16[32,1024]{1,0:T(8,128)(2,1)S(1)} %get-tuple-element.907), channel_id=1, source_target_pairs={{16,0},{32,16},{48,32},{64,48},{17,1},{33,17},{49,33},{65,49},{18,... | collective-permute-start | bytes 196616 | tf_op jit(solution)/shard_map/ppermute | solution.py:510
  411.3 8.3 %collective-permute-start.87 = (bf16[32,1024]{1,0:T(8,128)(2,1)S(1)}, bf16[32,1024]{1,0:T(8,128)(2,1)S(1)}, u32[]{:S(2)}, u32[]{:S(2)}) collective-permute-start(bf16[32,1024]{1,0:T(8,128)(2,1)S(1)} %get-tuple-element.918), channel_id=1, source_target_pairs={{16,0},{32,16},{48,32},{64,48},{17,1},{33,17},{49,33},{65,49},{18,... | collective-permute-start | bytes 196616 | tf_op jit(solution)/shard_map/ppermute | solution.py:510
  419.6 8.3 %collective-permute-start.88 = (bf16[32,1024]{1,0:T(8,128)(2,1)S(1)}, bf16[32,1024]{1,0:T(8,128)(2,1)S(1)}, u32[]{:S(2)}, u32[]{:S(2)}) collective-permute-start(bf16[32,1024]{1,0:T(8,128)(2,1)S(1)} %get-tuple-element.924), channel_id=1, source_target_pairs={{16,0},{32,16},{48,32},{64,48},{17,1},{33,17},{49,33},{65,49},{18,... | collective-permute-start | bytes 196616 | tf_op jit(solution)/shard_map/ppermute | solution.py:510
  435.9 9.9 %collective-permute-start.93 = (bf16[64,2048]{1,0:T(8,128)(2,1)S(1)}, bf16[64,2048]{1,0:T(8,128)(2,1)S(1)}, u32[]{:S(2)}, u32[]{:S(2)}) collective-permute-start(bf16[64,2048]{1,0:T(8,128)(2,1)S(1)} %get-tuple-element.946), channel_id=1, source_target_pairs={{0,2},{1,3},{2,4},{3,5},{4,6},{5,7},{6,8},{7,9},{8,10},{9,11},{10,... | collective-permute-start | bytes 786440 | tf_op jit(solution)/shard_map/ppermute | solution.py:429
  436.0 9.8 %collective-permute-start.97 = (bf16[64,2048]{1,0:T(8,128)(2,1)S(1)}, bf16[64,2048]{1,0:T(8,128)(2,1)S(1)}, u32[]{:S(2)}, u32[]{:S(2)}) collective-permute-start(bf16[64,2048]{1,0:T(8,128)(2,1)S(1)} %get-tuple-element.947), channel_id=1, source_target_pairs={{0,14},{1,15},{2,0},{3,1},{4,2},{5,3},{6,4},{7,5},{8,6},{9,7},{10,... | collective-permute-start | bytes 786440 | tf_op jit(solution)/shard_map/ppermute | solution.py:430
  439.3 10.3 %collective-permute-start.91 = (bf16[2,64,4096]{2,1,0:T(8,128)(2,1)S(1)}, bf16[2,64,4096]{2,1,0:T(8,128)(2,1)S(1)}, u32[]{:S(2)}, u32[]{:S(2)}) collective-permute-start(bf16[2,64,4096]{2,1,0:T(8,128)(2,1)S(1)} %get-tuple-element.933), channel_id=1, source_target_pairs={{0,1},{1,0},{2,3},{3,2},{4,5},{5,4},{6,7},{7,6},{8,9},{9,8},{10,11... | collective-permute-start | bytes 3145736 | tf_op jit(solution)/shard_map/ppermute | solution.py:425
  446.0 14.7 %collective-permute-start.94 = (bf16[64,4096]{1,0:T(8,128)(2,1)S(1)}, bf16[64,4096]{1,0:T(8,128)(2,1)S(1)}, u32[]{:S(2)}, u32[]{:S(2)}) collective-permute-start(bf16[64,4096]{1,0:T(8,128)(2,1)S(1)} %get-tuple-element.942), channel_id=1, source_target_pairs={{0,2},{1,3},{2,4},{3,5},{4,6},{5,7},{6,8},{7,9},{8,10},{9,11},{10,... | collective-permute-start | bytes 1572872 | tf_op jit(solution)/shard_map/ppermute | solution.py:436
  446.1 14.6 %collective-permute-start.98 = (bf16[64,4096]{1,0:T(8,128)(2,1)S(1)}, bf16[64,4096]{1,0:T(8,128)(2,1)S(1)}, u32[]{:S(2)}, u32[]{:S(2)}) collective-permute-start(bf16[64,4096]{1,0:T(8,128)(2,1)S(1)} %get-tuple-element.943), channel_id=1, source_target_pairs={{0,14},{1,15},{2,0},{3,1},{4,2},{5,3},{6,4},{7,5},{8,6},{9,7},{10,... | collective-permute-start | bytes 1572872 | tf_op jit(solution)/shard_map/ppermute | solution.py:437
  449.6 14.7 %collective-permute-start.92 = (bf16[3,64,4096]{2,1,0:T(8,128)(2,1)S(1)}, bf16[3,64,4096]{2,1,0:T(8,128)(2,1)S(1)}, u32[]{:S(2)}, u32[]{:S(2)}) collective-permute-start(bf16[3,64,4096]{2,1,0:T(8,128)(2,1)S(1)} %get-tuple-element.934), channel_id=1, source_target_pairs={{0,1},{1,0},{2,3},{3,2},{4,5},{5,4},{6,7},{7,6},{8,9},{9,8},{10,11... | collective-permute-start | bytes 4718600 | tf_op jit(solution)/shard_map/ppermute | solution.py:425
  460.9 13.8 %collective-permute-start.95 = (bf16[64,4096]{1,0:T(8,128)(2,1)S(1)}, bf16[64,4096]{1,0:T(8,128)(2,1)S(1)}, u32[]{:S(2)}, u32[]{:S(2)}) collective-permute-start(bf16[64,4096]{1,0:T(8,128)(2,1)S(1)} %get-tuple-element.940), channel_id=1, source_target_pairs={{0,2},{1,3},{2,4},{3,5},{4,6},{5,7},{6,8},{7,9},{8,10},{9,11},{10,... | collective-permute-start | bytes 1572872 | tf_op jit(solution)/shard_map/ppermute | solution.py:436
  461.0 13.7 %collective-permute-start.99 = (bf16[64,4096]{1,0:T(8,128)(2,1)S(1)}, bf16[64,4096]{1,0:T(8,128)(2,1)S(1)}, u32[]{:S(2)}, u32[]{:S(2)}) collective-permute-start(bf16[64,4096]{1,0:T(8,128)(2,1)S(1)} %get-tuple-element.941), channel_id=1, source_target_pairs={{0,14},{1,15},{2,0},{3,1},{4,2},{5,3},{6,4},{7,5},{8,6},{9,7},{10,... | collective-permute-start | bytes 1572872 | tf_op jit(solution)/shard_map/ppermute | solution.py:437
  474.9 12.8 %collective-permute-start.96 = (bf16[64,4096]{1,0:T(8,128)(2,1)S(1)}, bf16[64,4096]{1,0:T(8,128)(2,1)S(1)}, u32[]{:S(2)}, u32[]{:S(2)}) collective-permute-start(bf16[64,4096]{1,0:T(8,128)(2,1)S(1)} %get-tuple-element.938), channel_id=1, source_target_pairs={{0,2},{1,3},{2,4},{3,5},{4,6},{5,7},{6,8},{7,9},{8,10},{9,11},{10,... | collective-permute-start | bytes 1572872 | tf_op jit(solution)/shard_map/ppermute | solution.py:441
  475.0 12.8 %collective-permute-start.100 = (bf16[64,4096]{1,0:T(8,128)(2,1)S(1)}, bf16[64,4096]{1,0:T(8,128)(2,1)S(1)}, u32[]{:S(2)}, u32[]{:S(2)}) collective-permute-start(bf16[64,4096]{1,0:T(8,128)(2,1)S(1)} %get-tuple-element.939), channel_id=1, source_target_pairs={{0,14},{1,15},{2,0},{3,1},{4,2},{5,3},{6,4},{7,5},{8,6},{9,7},{10,... | collective-permute-start | bytes 1572872 | tf_op jit(solution)/shard_map/ppermute | solution.py:442
  (57 other events, 258.8 us)
